TPU v7x, 128 devices: a whole 4x4x4 slice. The times are simulated.
128 devices in a mesh: ctx: 32 (over z, y, core), tp: 4 (over x).
Axes of the slice: x: 4, y: 4, z: 4, core: 2. Of those that a mesh axis runs over, the one named last changes fastest.
Arguments:
- token_ids: int32 [8192], P('ctx'), may hold values from 0 to 511
- embed_table: bfloat16 [512, 3072], replicated, may hold values from -18 to 18
- gain_first: float32 [3072], replicated, may hold values from 0.5 to 1.5
- feat_weight: bfloat16 [3072, 3, 2048], P(None, None, 'tp'), may hold values from -0.109375 to 0.109375
- short_taps: float32 [3, 3, 2048], P(None, None, 'tp'), may hold values from -3 to 3
- long_filter: float32 [2048, 8192], P('tp', 'ctx'), may hold values from -1.8 to 1.8
- skip_gain: float32 [2048], P('tp'), may hold values from -4 to 4
- mix_weight: bfloat16 [2048, 3072], P('tp'), may hold values from -0.125 to 0.125
- gain_second: float32 [3072], replicated, may hold values from 0.5 to 1.5
- attn_weight: bfloat16 [3072, 3, 2048], P(None, None, 'tp'), may hold values from -1.5 to 1.5
Outputs:
- hidden: bfloat16 [8192, 3072], P('ctx', 'tp')
- context: bfloat16 [8192, 2048], P('ctx', 'tp')
All inputs are finite; a program needn't handle non-finite values.
Results may differ from a plain program's by a relative error of at most 0.029.
Values may be sent and summed in bfloat16 or wider, within the bound.
No kernel may reach another device: no remote copies, remote signals or barrier semaphores. Data moves between devices by JAX's collectives and lax.ppermute only.
A program may use at most 128 MiB of HBM per device.

v0:
```python
import functools
import math

import jax
import jax.numpy as jnp
import numpy as np
from jax import lax
from jax.experimental import pallas as pl
from jax.experimental.pallas import tpu as pltpu
from jax.sharding import PartitionSpec as P

D = 3072
WIDTH = 512
SHARE = 768
ROWS = 256
HALO = 16
HEAD_DIM = 128
SPAN = 8192
CTX = 32
PER = 16
VOCAB = 512
epsilon = 1e-05
rope_base = 10000.0
bf16 = jnp.bfloat16
f32 = jnp.float32
VMEM = pl.BlockSpec(memory_space=pltpu.VMEM)
SMEM = pl.BlockSpec(memory_space=pltpu.SMEM)
HBM = pl.BlockSpec(memory_space=pltpu.HBM)
MIB = 1 << 20


def params(mib):
    return pltpu.CompilerParams(vmem_limit_bytes=mib * MIB)


def cost(flops, moved):
    return pl.CostEstimate(flops=flops, bytes_accessed=moved, transcendentals=0)


def dot(a, b):
    return jnp.dot(a, b, preferred_element_type=f32)


def spot():
    r = lax.axis_index("ctx").astype(jnp.int32)
    p = lax.rem(r, 8)
    return lax.axis_index("tp").astype(jnp.int32), r, lax.div(r, 8), lax.div(p, 2), lax.rem(p, 2)


def feature_kernel(
    ids, ids_before, gain, taps, skip, filters, table, weight_hbm, mix_hbm,
    send, mixed0, share, cut1, cut2, cut3,
    weight, embedded, normed, acc, cut, kept,
    weight_sem, cut_sem, out_sem, share_sem,
):
    x, r, _, _, core = spot()
    parts = 4
    deep = D // parts

    def weight_copy(k, i):
        rows = pl.ds(k * deep, deep)
        return pltpu.make_async_copy(
            weight_hbm.at[i, rows, :], weight.at[i, rows, :], weight_sem.at[k, i]
        )

    def cut_copy(k):
        rows = pl.ds(pl.multiple_of(core * (WIDTH // 2), WIDTH // 2), WIDTH // 2)
        cols = pl.ds(pl.multiple_of(lax.rem(x + k, 4) * SHARE, SHARE), SHARE)
        return pltpu.make_async_copy(mix_hbm.at[rows, cols], cut.at[k - 1], cut_sem.at[k - 1])

    for k in range(parts):
        for i in range(3):
            weight_copy(k, i).start()
    direct = jnp.broadcast_to(skip[...], (128, WIDTH)).T
    lag = lax.broadcasted_iota(jnp.int32, (WIDTH, 128), 1)
    first = filters[:, :128] + jnp.where((lag == 0) & (r == 0), direct, 0.0)
    lags = jnp.concatenate([first, filters[:, 128:]], axis=1)
    send[:, PER:, :] = lags.astype(bf16).reshape(CTX, PER, ROWS)
    vocab = lax.broadcasted_iota(jnp.int32, (VOCAB, 128), 0)
    halo = jnp.where(ids_before[:, 128:] == vocab, 1.0, 0.0).T[128 - HALO :]
    own = [jnp.where(ids[:, c : c + 128] == vocab, 1.0, 0.0).T for c in (0, 128)]
    selector = jnp.concatenate([halo, *own], axis=0).astype(bf16)
    squares = jnp.zeros((ROWS + HALO, 1), f32)
    for k in range(parts):
        cols = pl.ds(k * deep, deep)
        rows = dot(selector, table[:, cols])
        squares = squares + jnp.sum(rows * rows, axis=1, keepdims=True)
        embedded[:, cols] = rows.astype(bf16)
        normed[:, cols] = (rows * gain[:, cols]).astype(bf16)
    scale = lax.rsqrt(squares * (1.0 / D) + epsilon)
    row_index = lax.broadcasted_iota(jnp.int32, (ROWS + HALO, 1), 0)
    scale = jnp.where((row_index >= HALO) | (r > 0), scale, 0.0)
    for k in (1, 2, 3):
        cut_copy(k).start()
    kept[...] = embedded[HALO:, pl.ds(pl.multiple_of(x * SHARE, SHARE), SHARE)]
    share_copy = pltpu.make_async_copy(kept, share, share_sem)
    share_copy.start()
    for k in range(parts):
        rows = pl.ds(k * deep, deep)
        for i in range(3):
            weight_copy(k, i).wait()
            part = dot(normed[:, rows], weight[i, rows, :])
            if k == 0:
                acc[i] = part
            else:
                acc[i] += part
    outs = [
        pltpu.make_async_copy(cut.at[n], out, out_sem.at[n])
        for n, out in enumerate((cut1, cut2, cut3))
    ]
    for n, copy in enumerate(outs):
        cut_copy(n + 1).wait()
        copy.start()
    mixed = []
    for i in range(3):
        f = (acc[i] * scale).astype(bf16).astype(f32)
        m = taps[0, i : i + 1, :] * f
        m = m + taps[1, i : i + 1, :] * pltpu.roll(f, 1, 0)
        m = m + taps[2, i : i + 1, :] * pltpu.roll(f, 2, 0)
        mixed.append(m[HALO:])
    mixed0[...] = mixed[0]
    send[:, :PER, :] = (mixed[1] * mixed[2]).T.astype(bf16).reshape(CTX, PER, ROWS)
    for copy in outs:
        copy.wait()
    share_copy.wait()


def features(ids, ids_before, gain, taps, skip, filters, table, weight, mix_weight):
    cut = jax.ShapeDtypeStruct((WIDTH // 2, SHARE), bf16)
    return pl.pallas_call(
        feature_kernel,
        out_shape=(
            jax.ShapeDtypeStruct((CTX, 2 * PER, ROWS), bf16),
            jax.ShapeDtypeStruct((ROWS, WIDTH), f32),
            jax.ShapeDtypeStruct((ROWS, SHARE), bf16),
            cut,
            cut,
            cut,
        ),
        in_specs=[VMEM] * 7 + [HBM] * 2,
        out_specs=(VMEM,) * 2 + (HBM,) * 4,
        scratch_shapes=[
            pltpu.VMEM((3, D, WIDTH), bf16),
            pltpu.VMEM((ROWS + HALO, D), bf16),
            pltpu.VMEM((ROWS + HALO, D), bf16),
            pltpu.VMEM((3, ROWS + HALO, WIDTH), f32),
            pltpu.VMEM((3, WIDTH // 2, SHARE), bf16),
            pltpu.VMEM((ROWS, SHARE), bf16),
            pltpu.SemaphoreType.DMA((4, 3)),
            pltpu.SemaphoreType.DMA((3,)),
            pltpu.SemaphoreType.DMA((3,)),
            pltpu.SemaphoreType.DMA,
        ],
        compiler_params=params(57),
        cost_estimate=cost(8_000_000_000, 14_000_000),
        name="features",
    )(ids, ids_before, gain, taps, skip, filters, table, weight, mix_weight)


def unit(turn):
    turn = turn % 1.0
    exact = {0.0: (1.0, 0.0), 0.25: (0.0, 1.0), 0.5: (-1.0, 0.0), 0.75: (0.0, -1.0)}
    if turn in exact:
        return exact[turn]
    return (math.cos(2 * math.pi * turn), math.sin(2 * math.pi * turn))


def scaled(value, factor):
    (a, b), (c, s) = value, factor
    if (c, s) == (1.0, 0.0):
        return (a, b)
    if (c, s) == (0.0, 1.0):
        return (-b, a)
    if (c, s) == (0.0, -1.0):
        return (b, -a)
    return (a * c - b * s, a * s + b * c)


def fourier(values, sign):
    n = len(values)
    if n == 1:
        return values
    even = fourier(values[0::2], sign)
    odd = fourier(values[1::2], sign)
    low, high = [], []
    for k in range(n // 2):
        a = even[k]
        b = scaled(odd[k], unit(sign * k / n))
        low.append((a[0] + b[0], a[1] + b[1]))
        high.append((a[0] - b[0], a[1] - b[1]))
    return low + high


def split(value):
    high = value.astype(bf16)
    return high, (value - high.astype(f32)).astype(bf16)


def conv_tables():
    k1 = np.arange(CTX)[:, None]
    i = np.arange(ROWS)[None, :]
    turn = 2 * np.pi * i * (k1 + 0.25) / SPAN
    twist = np.stack([np.cos(turn), np.sin(turn)]).astype(np.float32)
    grid = 2 * np.pi * (np.arange(ROWS)[:, None] * np.arange(ROWS)[None, :] % ROWS) / ROWS
    c, s = np.cos(grid), np.sin(grid)
    forward = np.block([c, s]).astype(np.float32)
    high = forward.astype(bf16)
    low = (forward - high.astype(np.float32)).astype(bf16)
    return twist, np.stack([high, low])


def conv_kernel(received, twist, table_hbm, out, short, table, high, low, mid, sem):
    table_copy = pltpu.make_async_copy(table_hbm, short, sem)
    table_copy.start()
    half = ROWS // 2
    blocks = 2 * PER // 16

    def load(step, _):
        g, side = step // 2, step % 2
        rows = pl.ds(pl.multiple_of(g * 16, 16), 16)
        lanes = pl.ds(pl.multiple_of(side * half, half), half)
        values = []
        for r in range(CTX):
            v = received[r, rows, lanes].astype(f32)
            c, s = unit(-r / (4 * CTX))
            values.append((v * c, v * s))
        spectrum = fourier(values, -1)
        for k in range(CTX):
            a, b = spectrum[k]
            c, s = twist[0, pl.ds(k, 1), lanes], twist[1, pl.ds(k, 1), lanes]
            re, im = a * c + b * s, b * c - a * s
            at = pl.ds(pl.multiple_of(g * (CTX * 16) + k * 16, 16), 16)
            for value, start in ((re, 0), (im, ROWS)):
                h, l = split(value)
                cols = pl.ds(pl.multiple_of(start + side * half, half), half)
                high[at, cols] = h
                low[at, cols] = l
        return 0

    lax.fori_loop(0, 2 * blocks, load, 0)

    table_copy.wait()
    for n in range(2):
        table[n, :ROWS, :ROWS] = short[n, :, :ROWS]
        table[n, :ROWS, ROWS:] = -short[n, :, ROWS:]
        table[n, ROWS:, :ROWS] = short[n, :, ROWS:]
        table[n, ROWS:, ROWS:] = short[n, :, :ROWS]

    def transform(rows):
        h, l = high[rows, :], low[rows, :]
        return dot(h, table[0]) + dot(l, table[0]) + dot(h, table[1])

    piece = 128
    for part in range(CTX * PER // piece):
        rows = slice(part * piece, (part + 1) * piece)
        filter_rows = slice(CTX * PER + part * piece, CTX * PER + (part + 1) * piece)
        a = transform(rows)
        b = transform(filter_rows)
        ar, ai, br, bi = a[:, :ROWS], a[:, ROWS:], b[:, :ROWS], b[:, ROWS:]
        h, l = split(ar * br - ai * bi)
        high[rows, :ROWS] = h
        low[rows, :ROWS] = l
        h, l = split(-(ar * bi + ai * br))
        high[rows, ROWS:] = h
        low[rows, ROWS:] = l
        mid[rows, :] = transform(rows)

    def store(side, _):
        lanes = pl.ds(pl.multiple_of(side * half, half), half)
        other = pl.ds(pl.multiple_of(ROWS + side * half, half), half)
        values = []
        for k in range(CTX):
            a, b = mid[k * PER : (k + 1) * PER, lanes], mid[k * PER : (k + 1) * PER, other]
            c, s = twist[0, pl.ds(k, 1), lanes], twist[1, pl.ds(k, 1), lanes]
            values.append((a * c + b * s, a * s - b * c))
        series = fourier(values, 1)
        for r in range(CTX):
            c, s = unit(r / (4 * CTX))
            a, b = series[r]
            out[r, :, lanes] = ((a * c - b * s) * (1.0 / SPAN)).astype(bf16)
        return 0

    lax.fori_loop(0, 2, store, 0)


def convolve(received):
    twist, table = conv_tables()
    return pl.pallas_call(
        conv_kernel,
        out_shape=jax.ShapeDtypeStruct((CTX, PER, ROWS), bf16),
        in_specs=[VMEM, VMEM, HBM],
        out_specs=VMEM,
        scratch_shapes=[
            pltpu.VMEM((2, ROWS, 2 * ROWS), bf16),
            pltpu.VMEM((2, 2 * ROWS, 2 * ROWS), bf16),
            pltpu.VMEM((2 * CTX * PER, 2 * ROWS), bf16),
            pltpu.VMEM((2 * CTX * PER, 2 * ROWS), bf16),
            pltpu.VMEM((CTX * PER, 2 * ROWS), f32),
            pltpu.SemaphoreType.DMA,
        ],
        compiler_params=params(24),
        cost_estimate=cost(1_000, 1_000),
        name="convolve",
    )(received, jnp.asarray(twist), jnp.asarray(table))


def gate_kernel(returned, mixed0, out):
    conv_out = returned[...].reshape(WIDTH, ROWS).astype(f32).T
    out[...] = (mixed0[...] * conv_out).astype(bf16)


def gate(returned, mixed0):
    return pl.pallas_call(
        gate_kernel,
        out_shape=jax.ShapeDtypeStruct((ROWS, WIDTH), bf16),
        in_specs=[VMEM] * 2,
        out_specs=VMEM,
        compiler_params=params(16),
        cost_estimate=cost(200_000_000, 1_500_000),
        name="gate",
    )(returned, mixed0)


def own_mix_kernel(gated, share, weight_hbm, out, weight, sem):
    start = pl.multiple_of(spot()[0] * SHARE, SHARE)
    copy = pltpu.make_async_copy(weight_hbm.at[:, pl.ds(start, SHARE)], weight, sem)
    copy.start()
    copy.wait()
    out[...] = share[...].astype(f32) + dot(gated[...], weight[...])


def mix_own(gated, share, weight):
    return pl.pallas_call(
        own_mix_kernel,
        out_shape=jax.ShapeDtypeStruct((ROWS, SHARE), f32),
        in_specs=[VMEM, VMEM, HBM],
        out_specs=VMEM,
        scratch_shapes=[pltpu.VMEM((WIDTH, SHARE), bf16), pltpu.SemaphoreType.DMA],
        compiler_params=params(16),
        cost_estimate=cost(1_500_000_000, 2_000_000),
        name="mix_own",
    )(gated, share, weight)


def add_mix_kernel(count, partial, *refs):
    gated, mine, theirs, out = refs[:count], refs[count : 2 * count], refs[2 * count : 3 * count], refs[-1]
    half = WIDTH // 2
    core = spot()[4]
    here = pl.ds(pl.multiple_of(core * half, half), half)
    there = pl.ds(pl.multiple_of((1 - core) * half, half), half)
    total = partial[...]
    for g, a, b in zip(gated, mine, theirs, strict=True):
        total = total + dot(g[:, here], a[...]) + dot(g[:, there], b[...])
    out[...] = total.astype(out.dtype)


def mix_add(partial, gated, mine, theirs, dtype):
    count = len(gated)
    return pl.pallas_call(
        functools.partial(add_mix_kernel, count),
        out_shape=jax.ShapeDtypeStruct((ROWS, SHARE), dtype),
        in_specs=[VMEM] * (1 + 3 * count),
        out_specs=VMEM,
        compiler_params=params(16),
        cost_estimate=cost(1_000_000_000 * count, 2_000_000),
        name="mix_add",
    )(partial, *gated, *mine, *theirs)


def project_kernel(which, last, *refs):
    count = len(which)
    pieces = 2 if last else count
    hidden, refs = refs[:pieces], refs[pieces:]
    gain, weight_hbm, refs = refs[0], refs[1], refs[2:]
    if which[0] > 0:
        before, squares_before, refs = refs[0], refs[1], refs[2:]
    if last:
        cosine, sine, *outs, weight, acc, weight_sem = refs
    else:
        acc, squares, weight, weight_sem = refs
    x, _, z, _, _ = spot()

    def start_of(k):
        return pl.multiple_of(lax.rem(x + (4 - k), 4) * SHARE, SHARE)

    def weight_copy(n, i):
        rows = pl.ds(start_of(which[n]), SHARE)
        return pltpu.make_async_copy(
            weight_hbm.at[i, rows, :], weight.at[n, i], weight_sem.at[n, i]
        )

    for n in range(count):
        for i in range(3):
            weight_copy(n, i).start()
    total = squares_before[...] if which[0] > 0 else jnp.zeros((ROWS, 1), f32)
    for n, k in enumerate(which):
        if last:
            v = jnp.concatenate([h[...] for h in hidden], axis=0).astype(f32)
        else:
            v = hidden[n][...].astype(f32)
        total = total + jnp.sum(v * v, axis=1, keepdims=True)
        scaled_rows = (v * gain[:, pl.ds(start_of(k), SHARE)]).astype(bf16)
        for i in range(3):
            weight_copy(n, i).wait()
            part = dot(scaled_rows, weight[n, i])
            if n == 0 and k == 0:
                acc[i] = part
            elif n == 0:
                acc[i] = before[i] + part
            else:
                acc[i] += part
    if not last:
        squares[...] = total
        return
    scale = lax.rsqrt(total * (1.0 / D) + epsilon)
    factor = math.log2(math.e) / math.sqrt(HEAD_DIM)
    c, s = cosine[...] * scale, sine[...] * scale
    half = HEAD_DIM
    for k, (out, query_out) in enumerate(zip(outs[:4], outs[4:], strict=True)):
        lanes = pl.ds(pl.multiple_of(lax.rem(z + k, 4) * HEAD_DIM, HEAD_DIM), HEAD_DIM)
        q, key, value = acc[0, :, lanes], acc[1, :, lanes], acc[2, :, lanes]
        q = (q * c + pltpu.roll(q, HEAD_DIM // 2, 1) * s) * factor
        key = key * c + pltpu.roll(key, HEAD_DIM // 2, 1) * s
        value = value * scale
        for n in range(2):
            rows = slice(n * half, (n + 1) * half)
            query_out[:, rows] = q[rows].T.astype(bf16)
            out[n] = key[rows].astype(bf16)
            out[2 + n] = value[rows].T.astype(bf16)


def project(which, hidden, gain, weight, before=(), turns=()):
    count = len(which)
    last = bool(turns)
    partial = jax.ShapeDtypeStruct((3, ROWS, WIDTH), f32)
    part = jax.ShapeDtypeStruct((4, 128, 128), bf16)
    query = jax.ShapeDtypeStruct((HEAD_DIM, ROWS), bf16)
    outs = (part,) * 4 + (query,) * 4 if last else (partial, jax.ShapeDtypeStruct((ROWS, 1), f32))
    return pl.pallas_call(
        functools.partial(project_kernel, which, last),
        out_shape=outs,
        in_specs=[VMEM] * (len(hidden) + 1) + [HBM] + [VMEM] * (len(before) + len(turns)),
        out_specs=(VMEM,) * len(outs),
        scratch_shapes=[pltpu.VMEM((count, 3, SHARE, WIDTH), bf16)]
        + ([pltpu.VMEM((3, ROWS, WIDTH), f32)] if last else [])
        + [pltpu.SemaphoreType.DMA((count, 3))],
        compiler_params=params(24),
        cost_estimate=cost(1_500_000_000 * count, 4_000_000 * count),
        name="project",
    )(*hidden, gain, weight, *before, *turns)


def sort_kernel(a0, a1, a2, a3, pairs):
    z = spot()[2]
    for k, a in enumerate((a0, a1, a2, a3)):
        at = lax.rem(z + (4 - k), 4)
        for n in range(2):
            pairs[0, 2 * at + n] = a[n]
            pairs[1, 2 * at + n] = a[2 + n]


def query_kernel(a0, a1, a2, a3, after, queries):
    z = spot()[2]
    for k, a in enumerate((a0, a1, a2, a3)):
        queries[lax.rem(z + (4 - k), 4)] = a[...]


def sort_blocks(kernel, shape, arrived, after=()):
    return pl.pallas_call(
        kernel,
        out_shape=jax.ShapeDtypeStruct(shape, bf16),
        in_specs=[VMEM] * (4 + len(after)),
        out_specs=VMEM,
        compiler_params=params(16),
        cost_estimate=cost(1_000, 1_000),
        name=kernel.__name__,
    )(*arrived, *after)


def fold(queries, pair, first, last, state, zq, lanes, mask=False):
    peak, total, summed = state
    keys = pair[0][2 * first : 2 * last].reshape((last - first) * ROWS, HEAD_DIM)
    values = jnp.concatenate([pair[1][j] for j in range(2 * first, 2 * last)], axis=1)
    scores = dot(keys, queries)
    if mask:
        key = lax.broadcasted_iota(jnp.int32, scores.shape, 0) - (last - 1 - first) * ROWS
        query = lax.broadcasted_iota(jnp.int32, scores.shape, 1)
        scores = jnp.where(key <= query, scores, -1e30)
    old = peak[zq, :, lanes]
    top = jnp.maximum(old, jnp.max(scores, axis=0, keepdims=True))
    carried = jnp.exp2(old - top)
    weights = jnp.exp2(scores - top)
    peak[zq, :, lanes] = top
    total[zq, :, lanes] = total[zq, :, lanes] * carried + jnp.sum(weights, axis=0, keepdims=True)
    summed[zq, :, lanes] = summed[zq, :, lanes] * carried + dot(values, weights.astype(bf16))


OWN, OTHER, BOTH = slice(0, ROWS), slice(ROWS, 2 * ROWS), slice(0, 2 * ROWS)


def fold_blocks(earlier, queries, pair, state, lanes):
    for zq in range(1, 4):
        fold(queries(zq), pair, 0, zq, state, zq, lanes)

    @pl.when(earlier)
    def _():
        for zq in range(4):
            fold(queries(zq), pair, zq, zq + 1, state, zq, lanes)


def own_kernel(own, other, pair, peak, total, summed):
    state = (peak, total, summed)
    halves = (pair.at[0], pair.at[1])
    peak[...] = jnp.full(peak.shape, -1e30, f32)
    total[...] = jnp.zeros(total.shape, f32)
    summed[...] = jnp.zeros(summed.shape, f32)
    for zq in range(4):
        fold(own[zq], halves, 0, zq + 1, state, zq, OWN, True)
    fold_blocks(spot()[4] == 0, lambda zq: other[zq], halves, state, OTHER)


def more_kernel(steps, last, own, other, *refs):
    count = len(steps)
    arrays = 2 if last else count
    y = spot()[3]
    pairs, old, refs = refs[:arrays], refs[arrays : arrays + 3], refs[arrays + 3 :]
    state = refs[-3:]
    for a, b in zip(old, state, strict=True):
        b[...] = a[...]
    for n, pair in enumerate(pairs[:count]):
        pair = (pair.at[0], pair.at[1]) if not last else pairs
        earlier = lax.rem(y + (4 - steps[n]), 4) < y
        both = lambda zq: jnp.concatenate([own[zq], other[zq]], axis=1)
        fold_blocks(earlier, both, pair, state, BOTH)
    if not last:
        return
    kept, level, sent = refs[:3]
    peak, total, summed = state
    for zq in range(4):
        count_of = jnp.maximum(total[zq], 1e-30)
        result = summed[zq] / count_of
        weight = peak[zq] + jnp.log2(count_of)
        kept[zq] = result[:, OWN]
        level[zq] = weight[:, OWN]
        sent[zq, 0:HEAD_DIM] = result[:, OTHER].astype(bf16)
        rest = weight[:, OTHER]
        rows = []
        for _ in range(3):
            piece = rest.astype(bf16).astype(f32)
            rows.append(piece)
            rest = rest - piece
        rows = jnp.concatenate(rows + [jnp.zeros((13, ROWS), f32)], axis=0)
        sent[zq, HEAD_DIM : HEAD_DIM + 16] = rows.astype(bf16)


STATE = (
    jax.ShapeDtypeStruct((4, 1, 2 * ROWS), f32),
    jax.ShapeDtypeStruct((4, 1, 2 * ROWS), f32),
    jax.ShapeDtypeStruct((4, HEAD_DIM, 2 * ROWS), f32),
)


def attend_own(own, other, pair):
    return pl.pallas_call(
        own_kernel,
        out_shape=STATE,
        in_specs=[VMEM] * 3,
        out_specs=(VMEM,) * 3,
        compiler_params=params(24),
        cost_estimate=cost(1_000, 1_000),
        name="attend_own",
    )(own, other, pair)


def attend_more(steps, own, other, pairs, state):
    count = len(pairs)
    return pl.pallas_call(
        functools.partial(more_kernel, steps, False),
        out_shape=STATE,
        in_specs=[VMEM] * (5 + count),
        out_specs=(VMEM,) * 3,
        compiler_params=params(24),
        cost_estimate=cost(4_000_000_000 * count, 3_000_000),
        name="attend_more",
    )(own, other, *pairs, *state)


def attend_last(steps, own, other, pair, state):
    return pl.pallas_call(
        functools.partial(more_kernel, steps, True),
        out_shape=(
            jax.ShapeDtypeStruct((4, HEAD_DIM, ROWS), f32),
            jax.ShapeDtypeStruct((4, 1, ROWS), f32),
            jax.ShapeDtypeStruct((4, HEAD_DIM + 16, ROWS), bf16),
        ),
        in_specs=[VMEM] * 7,
        out_specs=(VMEM,) * 3,
        scratch_shapes=[pltpu.VMEM(part.shape, f32) for part in STATE],
        compiler_params=params(24),
        cost_estimate=cost(4_000_000_000, 3_000_000),
        name="attend_last",
    )(own, other, *pair, *state)


def join_kernel(kept, level, got, *outs):
    z = spot()[2]
    for k, out in enumerate(outs):
        at = lax.rem(z + k, 4)
        rows = got[at, HEAD_DIM : HEAD_DIM + 16].astype(f32)
        their_level = rows[0:1] + rows[1:2] + rows[2:3]
        share = 1.0 / (1.0 + jnp.exp2(their_level - level[at]))
        theirs = got[at, 0:HEAD_DIM].astype(f32)
        out[...] = (kept[at] * share + theirs * (1.0 - share)).T.astype(bf16)


def join(kept, level, got):
    return pl.pallas_call(
        join_kernel,
        out_shape=(jax.ShapeDtypeStruct((ROWS, HEAD_DIM), bf16),) * 4,
        in_specs=[VMEM] * 3,
        out_specs=(VMEM,) * 4,
        compiler_params=params(16),
        cost_estimate=cost(1_000_000_000, 1_000_000),
        name="join",
    )(kept, level, got)


def assemble_kernel(a0, a1, a2, a3, out):
    z = spot()[2]
    for k, a in enumerate((a0, a1, a2, a3)):
        head = lax.rem(z + (4 - k), 4)
        out[:, pl.ds(pl.multiple_of(head * HEAD_DIM, HEAD_DIM), HEAD_DIM)] = a[...]


def assemble(arrived):
    return pl.pallas_call(
        assemble_kernel,
        out_shape=jax.ShapeDtypeStruct((ROWS, WIDTH), bf16),
        in_specs=[VMEM] * 4,
        out_specs=VMEM,
        compiler_params=params(16),
        cost_estimate=cost(1_000_000, 500_000),
        name="assemble",
    )(*arrived)


def along_x(value, by):
    return lax.ppermute(value, "tp", [(i, (i + by) % 4) for i in range(4)])


def along_z(value, by):
    return lax.ppermute(value, "ctx", [(i, (i + 8 * by) % CTX) for i in range(CTX)])


def along_y(value, by):
    return lax.ppermute(value, "ctx", [(i, i // 8 * 8 + (i + 2 * by) % 8) for i in range(CTX)])


def across(value):
    return lax.ppermute(value, "ctx", [(i, i ^ 1) for i in range(CTX)])


def body(
    token_ids, embed_table, gain_first, feat_weight, short_taps, long_filter,
    skip_gain, mix_weight, gain_second, attn_weight,
):
    ids_before = lax.ppermute(token_ids, "ctx", [(i, i + 1) for i in range(CTX - 1)])
    send, mixed0, share, *cuts = features(
        token_ids[None, :],
        ids_before[None, :],
        gain_first[None, :],
        short_taps,
        skip_gain[None, :],
        long_filter,
        embed_table,
        feat_weight.transpose(1, 0, 2),
        mix_weight,
    )
    mine = [along_x(cut, k) for k, cut in zip((1, 2, 3), cuts, strict=True)]
    theirs = [across(part) for part in mine]
    received = lax.all_to_all(send, "ctx", 0, 0, tiled=True)
    returned = lax.all_to_all(convolve(received), "ctx", 0, 0, tiled=True)

    gated = gate(returned, mixed0)
    g1, g3, g2 = [along_x(gated, k) for k in (1, 3, 2)]
    partial = mix_own(gated, share, mix_weight)
    partial = mix_add(partial, (g1, g3), mine[::2], theirs[::2], f32)
    hidden = mix_add(partial, (g2,), mine[1:2], theirs[1:2], bf16)

    h1, h3 = along_x(hidden, 1), along_x(hidden, 3)
    h2 = along_x(h1[: ROWS // 2], 1), along_x(h3[ROWS // 2 :], 3)
    positions = lax.axis_index("ctx") * ROWS + lax.broadcasted_iota(jnp.int32, (ROWS,), 0)
    frequency = rope_base ** (-(2.0 / HEAD_DIM) * jnp.arange(HEAD_DIM // 2, dtype=f32))
    angles = positions.astype(f32)[:, None] * frequency[None, :]
    cosine, sine = jnp.cos(angles), jnp.sin(angles)
    turns = (
        jnp.concatenate([cosine, cosine], axis=1),
        jnp.concatenate([-sine, sine], axis=1),
    )
    gain, weight = gain_second[None, :], attn_weight.transpose(1, 0, 2)
    partial = project((0,), (hidden,), gain, weight)
    partial = project((1, 3), (h1, h3), gain, weight, partial)
    blocks = project((2,), h2, gain, weight, partial, turns)

    blocks, asked = blocks[:4], blocks[4:]
    arrived = [blocks[0]] + [along_z(blocks[k], k) for k in (1, 2, 3)]
    pair = sort_blocks(sort_kernel, (2, 8, 128, 128), arrived)
    asked = [asked[0]] + [along_z(asked[k], k) for k in (1, 2, 3)]
    own = sort_blocks(query_kernel, (4, HEAD_DIM, ROWS), asked, (pair,))

    other = across(own)
    pair1, pair3 = along_y(pair, 1), along_y(pair, 3)
    far = along_y(pair1[0], 1), along_y(pair3[1], 3)
    state = attend_own(own, other, pair)
    state = attend_more((1, 3), own, other, (pair1, pair3), state)
    kept, level, sent = attend_last((2,), own, other, far, state)
    parts = join(kept, level, across(sent))
    back = [parts[0]] + [along_z(parts[k], k) for k in (1, 2, 3)]
    return (hidden, assemble(back))


def solution(mesh):
    return jax.shard_map(
        body,
        mesh=mesh,
        in_specs=(
            P("ctx"),
            P(),
            P(),
            P(None, None, "tp"),
            P(None, None, "tp"),
            P("tp", "ctx"),
            P("tp"),
            P("tp", None),
            P(),
            P(None, None, "tp"),
        ),
        out_specs=(P("ctx", "tp"), P("ctx", "tp")),
        check_vma=False,
    )
```

profile of v0, /device:TPU:30, one launch (start us, length us, event | category | flops | bytes accessed | tf_op | source)
XLA Modules:
  0.0 139.8 jit_solution(7265057237436213197)
XLA Ops:
  0.6 1.9 %collective-permute-start = (s32[256]{0:T(256)}, s32[256]{0:T(256)S(1)}, u32[]{:S(2)}, u32[]{:S(2)}) collective-permute-start(s32[256]{0:T(256)} %param.12), channel_id=1, source_target_pairs={{0,4},{4,8},{8,12},{12,16},{16,20},{20,24},{24,28},{28,32},{32,36}... | collective-permute-start | bytes 3080 | tf_op jit(solution)/shard_map/ppermute | solution.py:667
  2.6 3.2 %collective-permute-done = s32[256]{0:T(256)S(1)} collective-permute-done((s32[256]{0:T(256)}, s32[256]{0:T(256)S(1)}, u32[]{:S(2)}, u32[]{:S(2)}) %collective-permute-start) | collective-permute-done | bytes 1056 | tf_op jit(solution)/shard_map/ppermute | solution.py:667
  6.3 9.8 %features.1 = (bf16[32,32,256]{2,1,0:T(8,128)(2,1)}, f32[256,512]{1,0:T(8,128)}, bf16[256,768]{1,0:T(8,128)(2,1)}, bf16[256,768]{1,0:T(8,128)(2,1)}, bf16[256,768]{1,0:T(8,128)(2,1)}, /*index=5*/bf16[256,768]{1,0:T(8,128)(2,1)}) custom-call(s32[1,256]{1,0:T(1,128)} %bitcast.22, s32[1,256]{1,0:T(1,128)} %bitcast.23, f32[1,3072]{1,0:T(1,128)} %bitcast.20, ...), custom_call_target="tpu_custom_call" | custom-call | flops 8000000000 | bytes 14000000 | tf_op jit(solution)/shard_map/features/pallas_call | solution.py:130
  16.2 8.5 %all-to-all-start = ((bf16[32,32,256]{2,1,0:T(8,128)(2,1)}), bf16[32,32,256]{2,1,0:T(8,128)(2,1)S(1)}, u32[]{:S(2)}, u32[]{:S(2)}) async-start(bf16[32,32,256]{2,1,0:T(8,128)(2,1)} %get-tuple-element.33), calls=%async_computation | async-start | bytes 1048576 | tf_op jit(solution)/shard_map/all_to_all | solution.py:681
  28.1 5.9 %all-to-all-done.received = bf16[32,32,256]{2,1,0:T(8,128)(2,1)S(1)} async-done(((bf16[32,32,256]{2,1,0:T(8,128)(2,1)}), bf16[32,32,256]{2,1,0:T(8,128)(2,1)S(1)}, u32[]{:S(2)}, u32[]{:S(2)}) %all-to-all-start) | async-done | bytes 524320 | tf_op jit(solution)/shard_map/all_to_all | solution.py:681
  34.0 6.1 %convolve.1 = bf16[32,16,256]{2,1,0:T(8,128)(2,1)} custom-call(bf16[32,32,256]{2,1,0:T(8,128)(2,1)S(1)} %all-to-all-done.received, f32[2,32,256]{2,1,0:T(8,128)S(1)} %copy-done.4, bf16[2,256,512]{2,1,0:T(8,128)(2,1)S(1)} %copy-done.1), custom_call_target="tpu_custom_call" | custom-call | flops 1000 | bytes 1000 | tf_op jit(solution)/shard_map/convolve/pallas_call | solution.py:288
  40.1 6.2 %all-to-all-start.1 = ((bf16[32,16,256]{2,1,0:T(8,128)(2,1)}), bf16[32,16,256]{2,1,0:T(8,128)(2,1)S(1)}, u32[]{:S(2)}, u32[]{:S(2)}) async-start(bf16[32,16,256]{2,1,0:T(8,128)(2,1)} %convolve.1), calls=%async_computation.1 | async-start | bytes 524288 | tf_op jit(solution)/shard_map/all_to_all | solution.py:682
  46.9 6.5 %all-to-all-done.1.returned = bf16[32,16,256]{2,1,0:T(8,128)(2,1)S(1)} async-done(((bf16[32,16,256]{2,1,0:T(8,128)(2,1)}), bf16[32,16,256]{2,1,0:T(8,128)(2,1)S(1)}, u32[]{:S(2)}, u32[]{:S(2)}) %all-to-all-start.1) | async-done | bytes 262176 | tf_op jit(solution)/shard_map/all_to_all | solution.py:682
  57.3 1.9 %copy-done.5 = bf16[512,3072]{1,0:T(8,128)(2,1)S(1)} copy-done((bf16[512,3072]{1,0:T(8,128)(2,1)S(1)}, bf16[512,3072]{1,0:T(8,128)(2,1)}, u32[]{:S(2)}) %copy-start.5) | copy-done | bytes 3145752
  59.7 2.9 %collective-permute-done.1.refs_0_ = bf16[256,512]{1,0:T(8,128)(2,1)S(1)} collective-permute-done((bf16[256,512]{1,0:T(8,128)(2,1)S(1)}, bf16[256,512]{1,0:T(8,128)(2,1)S(1)}, u32[]{:S(2)}, u32[]{:S(2)}) %collective-permute-start.1) | collective-permute-done | bytes 262176 | tf_op jit(solution)/shard_map/ppermute | solution.py:648
  62.7 6.7 %collective-permute-done.2.refs_1_ = bf16[256,512]{1,0:T(8,128)(2,1)S(1)} collective-permute-done((bf16[256,512]{1,0:T(8,128)(2,1)S(1)}, bf16[256,512]{1,0:T(8,128)(2,1)S(1)}, u32[]{:S(2)}, u32[]{:S(2)}) %collective-permute-start.2) | collective-permute-done | bytes 262176 | tf_op jit(solution)/shard_map/ppermute | solution.py:648
  76.4 4.6 %collective-permute-done.10.refs_0_ = bf16[256,768]{1,0:T(8,128)(2,1)S(1)} collective-permute-done((bf16[256,768]{1,0:T(8,128)(2,1)}, bf16[256,768]{1,0:T(8,128)(2,1)S(1)}, u32[]{:S(2)}, u32[]{:S(2)}) %collective-permute-start.10) | collective-permute-done | bytes 393248 | tf_op jit(solution)/shard_map/ppermute | solution.py:648
  81.0 3.1 %collective-permute-start.11 = (bf16[128,768]{1,0:T(8,128)(2,1)S(1)}, bf16[128,768]{1,0:T(8,128)(2,1)S(1)}, u32[]{:S(2)}, u32[]{:S(2)}) collective-permute-start(bf16[128,768]{1,0:T(8,128)(2,1)S(1)} %slice.16), channel_id=1, source_target_pairs={{0,1},{1,2},{2,3},{3,0},{4,5},{5,6},{6,7},{7,4},{8,9},{9,10},{10,1... | collective-permute-start | bytes 589832 | tf_op jit(solution)/shard_map/ppermute | solution.py:648
  84.2 2.6 %project.4 = (f32[3,256,512]{2,1,0:T(8,128)S(1)}, f32[256,1]{1,0:T(8,128)S(1)}) custom-call(bf16[256,768]{1,0:T(8,128)(2,1)S(1)} %collective-permute-done.10.refs_0_, bf16[256,768]{1,0:T(8,128)(2,1)S(1)} %collective-permute-done.12.refs_1_, f32[1,3072]{1,0:T(1,128)S(1)} %bitcast.17, bf16[3,3072,512]{2,1,0:T(8,128)(2,1)S(1)} %bitcast.14, ...), custom_call_target="tpu_custom_call" | custom-call | flops 3000000000 | bytes 8000000 | tf_op jit(solution)/shard_map/project/pallas_call | solution.py:439
  87.4 3.7 %collective-permute-done.13.refs_1_ = bf16[128,768]{1,0:T(8,128)(2,1)S(1)} collective-permute-done((bf16[128,768]{1,0:T(8,128)(2,1)S(1)}, bf16[128,768]{1,0:T(8,128)(2,1)S(1)}, u32[]{:S(2)}, u32[]{:S(2)}) %collective-permute-start.13) | collective-permute-done | bytes 196640 | tf_op jit(solution)/shard_map/ppermute | solution.py:648
  91.1 1.9 %project.5 = (bf16[4,128,128]{2,1,0:T(8,128)(2,1)S(1)}, bf16[4,128,128]{2,1,0:T(8,128)(2,1)S(1)}, bf16[4,128,128]{2,1,0:T(8,128)(2,1)S(1)}, bf16[4,128,128]{2,1,...) custom-call(bf16[128,768]{1,0:T(8,128)(2,1)S(1)} %collective-permute, ...), custom_call_target="tpu_custom_call" | custom-call | flops 1500000000 | bytes 4000000 | tf_op jit(solution)/shard_map/project/pallas_call | solution.py:439
  93.7 1.9 %collective-permute-start.18 = (bf16[4,128,128]{2,1,0:T(8,128)(2,1)S(1)}, bf16[4,128,128]{2,1,0:T(8,128)(2,1)S(1)}, u32[]{:S(2)}, u32[]{:S(2)}) collective-permute-start(bf16[4,128,128]{2,1,0:T(8,128)(2,1)S(1)} %get-tuple-element.49), channel_id=1, source_target_pairs={{0,64},{4,68},{8,72},{12,76},{16,80},{20,84},{24,88},{28,92},{32,9... | collective-permute-start | bytes 393224 | tf_op jit(solution)/shard_map/ppermute | solution.py:652
  96.5 4.2 %collective-permute-done.17.a1 = bf16[4,128,128]{2,1,0:T(8,128)(2,1)S(1)} collective-permute-done((bf16[4,128,128]{2,1,0:T(8,128)(2,1)S(1)}, bf16[4,128,128]{2,1,0:T(8,128)(2,1)S(1)}, u32[]{:S(2)}, u32[]{:S(2)}) %collective-permute-start.17) | collective-permute-done | bytes 131104 | tf_op jit(solution)/shard_map/ppermute | solution.py:652
  104.3 3.0 %collective-permute-start.15 = (bf16[128,256]{1,0:T(8,128)(2,1)S(1)}, bf16[128,256]{1,0:T(8,128)(2,1)S(1)}, u32[]{:S(2)}, u32[]{:S(2)}) collective-permute-start(bf16[128,256]{1,0:T(8,128)(2,1)S(1)} %get-tuple-element.45), channel_id=1, source_target_pairs={{0,64},{4,68},{8,72},{12,76},{16,80},{20,84},{24,88},{28,92},{32,9... | collective-permute-start | bytes 196616 | tf_op jit(solution)/shard_map/ppermute | solution.py:652
  113.2 4.2 %attend_own.1 = (f32[4,1,512]{2,1,0:T(1,128)S(1)}, f32[4,1,512]{2,1,0:T(1,128)S(1)}, f32[4,128,512]{2,1,0:T(8,128)S(1)}) custom-call(bf16[4,128,256]{2,1,0:T(8,128)(2,1)S(1)} %query_kernel.1.own, bf16[4,128,256]{2,1,0:T(8,128)(2,1)S(1)} %collective-permute-done.20.other, bf16[2,8,128,128]{3,2,1,0:T(8,128)(2,1)S(1)} %sort_kernel.1.after.pair), custom_call_target="tpu_custom_call" | custom-call | flops 1000 | bytes 1000 | tf_op jit(solution)/shard_map/attend_own/pallas_call | solution.py:564
  119.7 6.1 %attend_more.1 = (f32[4,1,512]{2,1,0:T(1,128)S(1)}, f32[4,1,512]{2,1,0:T(1,128)S(1)}, f32[4,128,512]{2,1,0:T(8,128)S(1)}) custom-call(bf16[4,128,256]{2,1,0:T(8,128)(2,1)S(1)} %query_kernel.1.own, bf16[4,128,256]{2,1,0:T(8,128)(2,1)S(1)} %collective-permute-done.20.other, bf16[2,8,128,128]{3,2,1,0:T(8,128)(2,1)S(1)} %collective-permute-done.21.refs_0_, ...), custom_call_target="tpu_custom_call" | custom-call | flops 8000000000 | bytes 3000000 | tf_op jit(solution)/shard_map/attend_more/pallas_call | solution.py:577
  126.7 3.1 %attend_last.1 = (f32[4,128,256]{2,1,0:T(8,128)S(1)}, f32[4,1,256]{2,1,0:T(1,128)S(1)}, bf16[4,144,256]{2,1,0:T(8,128)(2,1)S(1)}) custom-call(bf16[4,128,256]{2,1,0:T(8,128)(2,1)S(1)} %query_kernel.1.own, bf16[4,128,256]{2,1,0:T(8,128)(2,1)S(1)} %collective-permute-done.20.other, bf16[8,128,128]{2,1,0:T(8,128)(2,1)S(1)} %collective-permute-done.22.refs_0_, ...), custom_call_target="tpu_custom_call" | custom-call | flops 4000000000 | bytes 3000000 | tf_op jit(solution)/shard_map/attend_last/pallas_call | solution.py:589
  132.4 2.1 %collective-permute-start.27 = (bf16[256,128]{1,0:T(8,128)(2,1)S(1)}, bf16[256,128]{1,0:T(8,128)(2,1)S(1)}, u32[]{:S(2)}, u32[]{:S(2)}) collective-permute-start(bf16[256,128]{1,0:T(8,128)(2,1)S(1)} %get-tuple-element.62), channel_id=1, source_target_pairs={{0,64},{4,68},{8,72},{12,76},{16,80},{20,84},{24,88},{28,92},{32,9... | collective-permute-start | bytes 196616 | tf_op jit(solution)/shard_map/ppermute | solution.py:652
  135.8 2.6 %collective-permute-done.26.a1 = bf16[256,128]{1,0:T(8,128)(2,1)S(1)} collective-permute-done((bf16[256,128]{1,0:T(8,128)(2,1)S(1)}, bf16[256,128]{1,0:T(8,128)(2,1)S(1)}, u32[]{:S(2)}, u32[]{:S(2)}) %collective-permute-start.26) | collective-permute-done | bytes 65568 | tf_op jit(solution)/shard_map/ppermute | solution.py:652
  (85 shorter events, 36.0 us)
Async XLA Ops:
  16.2 17.8 %all-to-all-start = ((bf16[32,32,256]{2,1,0:T(8,128)(2,1)}), bf16[32,32,256]{2,1,0:T(8,128)(2,1)S(1)}, u32[]{:S(2)}, u32[]{:S(2)}) async-start(bf16[32,32,256]{2,1,0:T(8,128)(2,1)} %get-tuple-element.33), calls=%async_computation | async-start | bytes 1048576 | tf_op jit(solution)/shard_map/all_to_all | solution.py:681
  24.6 21.7 %collective-permute-start.3 = (bf16[256,768]{1,0:T(8,128)(2,1)}, bf16[256,768]{1,0:T(8,128)(2,1)S(1)}, u32[]{:S(2)}, u32[]{:S(2)}) collective-permute-start(bf16[256,768]{1,0:T(8,128)(2,1)} %get-tuple-element.36), channel_id=1, source_target_pairs={{0,1},{1,2},{2,3},{3,0},{4,5},{5,6},{6,7},{7,4},{8,9},{9,10},{10,1... | collective-permute-start | bytes 1179656 | tf_op jit(solution)/shard_map/ppermute | solution.py:648
  25.2 21.4 %collective-permute-start.4 = (bf16[256,768]{1,0:T(8,128)(2,1)}, bf16[256,768]{1,0:T(8,128)(2,1)S(1)}, u32[]{:S(2)}, u32[]{:S(2)}) collective-permute-start(bf16[256,768]{1,0:T(8,128)(2,1)} %get-tuple-element.37), channel_id=1, source_target_pairs={{0,3},{1,0},{2,1},{3,2},{4,7},{5,4},{6,5},{7,6},{8,11},{9,8},{10,9... | collective-permute-start | bytes 1179656 | tf_op jit(solution)/shard_map/ppermute | solution.py:648
  26.7 28.9 %collective-permute-start.8 = (bf16[256,768]{1,0:T(8,128)(2,1)}, bf16[256,768]{1,0:T(8,128)(2,1)S(1)}, u32[]{:S(2)}, u32[]{:S(2)}) collective-permute-start(bf16[256,768]{1,0:T(8,128)(2,1)} %get-tuple-element.38), channel_id=1, source_target_pairs={{0,2},{1,3},{2,0},{3,1},{4,6},{5,7},{6,4},{7,5},{8,10},{9,11},{10,... | collective-permute-start | bytes 1179656 | tf_op jit(solution)/shard_map/ppermute | solution.py:648
  40.1 13.3 %all-to-all-start.1 = ((bf16[32,16,256]{2,1,0:T(8,128)(2,1)}), bf16[32,16,256]{2,1,0:T(8,128)(2,1)S(1)}, u32[]{:S(2)}, u32[]{:S(2)}) async-start(bf16[32,16,256]{2,1,0:T(8,128)(2,1)} %convolve.1), calls=%async_computation.1 | async-start | bytes 524288 | tf_op jit(solution)/shard_map/all_to_all | solution.py:682
  46.3 9.4 %collective-permute-start.5 = (bf16[256,768]{1,0:T(8,128)(2,1)S(1)}, bf16[256,768]{1,0:T(8,128)(2,1)S(1)}, u32[]{:S(2)}, u32[]{:S(2)}) collective-permute-start(bf16[256,768]{1,0:T(8,128)(2,1)S(1)} %collective-permute-done.3.refs_2_), channel_id=1, source_target_pairs={{0,4},{4,0},{8,12},{12,8},{16,20},{20,16},{24,28},{28,24},{32,36},... | collective-permute-start | bytes 1179656 | tf_op jit(solution)/shard_map/ppermute | solution.py:660
  46.5 13.2 %collective-permute-start.6 = (bf16[256,768]{1,0:T(8,128)(2,1)S(1)}, bf16[256,768]{1,0:T(8,128)(2,1)S(1)}, u32[]{:S(2)}, u32[]{:S(2)}) collective-permute-start(bf16[256,768]{1,0:T(8,128)(2,1)S(1)} %collective-permute-done.4.refs_3_), channel_id=1, source_target_pairs={{0,4},{4,0},{8,12},{12,8},{16,20},{20,16},{24,28},{28,24},{32,36},... | collective-permute-start | bytes 1179656 | tf_op jit(solution)/shard_map/ppermute | solution.py:660
  53.5 9.2 %collective-permute-start.1 = (bf16[256,512]{1,0:T(8,128)(2,1)S(1)}, bf16[256,512]{1,0:T(8,128)(2,1)S(1)}, u32[]{:S(2)}, u32[]{:S(2)}) collective-permute-start(bf16[256,512]{1,0:T(8,128)(2,1)S(1)} %gate.1.gated), channel_id=1, source_target_pairs={{0,1},{1,2},{2,3},{3,0},{4,5},{5,6},{6,7},{7,4},{8,9},{9,10},{10,1... | collective-permute-start | bytes 786440 | tf_op jit(solution)/shard_map/ppermute | solution.py:648
  54.1 15.3 %collective-permute-start.2 = (bf16[256,512]{1,0:T(8,128)(2,1)S(1)}, bf16[256,512]{1,0:T(8,128)(2,1)S(1)}, u32[]{:S(2)}, u32[]{:S(2)}) collective-permute-start(bf16[256,512]{1,0:T(8,128)(2,1)S(1)} %gate.1.gated), channel_id=1, source_target_pairs={{0,3},{1,0},{2,1},{3,2},{4,7},{5,4},{6,5},{7,6},{8,11},{9,8},{10,9... | collective-permute-start | bytes 786440 | tf_op jit(solution)/shard_map/ppermute | solution.py:648
  55.6 14.4 %collective-permute-start.9 = (bf16[256,768]{1,0:T(8,128)(2,1)S(1)}, bf16[256,768]{1,0:T(8,128)(2,1)S(1)}, u32[]{:S(2)}, u32[]{:S(2)}) collective-permute-start(bf16[256,768]{1,0:T(8,128)(2,1)S(1)} %collective-permute-done.8.refs_1_), channel_id=1, source_target_pairs={{0,4},{4,0},{8,12},{12,8},{16,20},{20,16},{24,28},{28,24},{32,36},... | collective-permute-start | bytes 1179656 | tf_op jit(solution)/shard_map/ppermute | solution.py:660
  55.7 14.4 %collective-permute-start.7 = (bf16[256,512]{1,0:T(8,128)(2,1)S(1)}, bf16[256,512]{1,0:T(8,128)(2,1)S(1)}, u32[]{:S(2)}, u32[]{:S(2)}) collective-permute-start(bf16[256,512]{1,0:T(8,128)(2,1)S(1)} %gate.1.gated), channel_id=1, source_target_pairs={{0,2},{1,3},{2,0},{3,1},{4,6},{5,7},{6,4},{7,5},{8,10},{9,11},{10,... | collective-permute-start | bytes 786440 | tf_op jit(solution)/shard_map/ppermute | solution.py:648
  71.2 9.9 %collective-permute-start.10 = (bf16[256,768]{1,0:T(8,128)(2,1)}, bf16[256,768]{1,0:T(8,128)(2,1)S(1)}, u32[]{:S(2)}, u32[]{:S(2)}) collective-permute-start(bf16[256,768]{1,0:T(8,128)(2,1)} %mix_add.3.refs_0_), channel_id=1, source_target_pairs={{0,1},{1,2},{2,3},{3,0},{4,5},{5,6},{6,7},{7,4},{8,9},{9,10},{10,1... | collective-permute-start | bytes 1179656 | tf_op jit(solution)/shard_map/ppermute | solution.py:648
  71.8 12.3 %collective-permute-start.12 = (bf16[256,768]{1,0:T(8,128)(2,1)}, bf16[256,768]{1,0:T(8,128)(2,1)S(1)}, u32[]{:S(2)}, u32[]{:S(2)}) collective-permute-start(bf16[256,768]{1,0:T(8,128)(2,1)} %mix_add.3.refs_0_), channel_id=1, source_target_pairs={{0,3},{1,0},{2,1},{3,2},{4,7},{5,4},{6,5},{7,6},{8,11},{9,8},{10,9... | collective-permute-start | bytes 1179656 | tf_op jit(solution)/shard_map/ppermute | solution.py:648
  81.0 6.4 %collective-permute-start.11 = (bf16[128,768]{1,0:T(8,128)(2,1)S(1)}, bf16[128,768]{1,0:T(8,128)(2,1)S(1)}, u32[]{:S(2)}, u32[]{:S(2)}) collective-permute-start(bf16[128,768]{1,0:T(8,128)(2,1)S(1)} %slice.16), channel_id=1, source_target_pairs={{0,1},{1,2},{2,3},{3,0},{4,5},{5,6},{6,7},{7,4},{8,9},{9,10},{10,1... | collective-permute-start | bytes 589832 | tf_op jit(solution)/shard_map/ppermute | solution.py:648
  84.2 6.9 %collective-permute-start.13 = (bf16[128,768]{1,0:T(8,128)(2,1)S(1)}, bf16[128,768]{1,0:T(8,128)(2,1)S(1)}, u32[]{:S(2)}, u32[]{:S(2)}) collective-permute-start(bf16[128,768]{1,0:T(8,128)(2,1)S(1)} %slice.17), channel_id=1, source_target_pairs={{0,3},{1,0},{2,1},{3,2},{4,7},{5,4},{6,5},{7,6},{8,11},{9,8},{10,9... | collective-permute-start | bytes 589832 | tf_op jit(solution)/shard_map/ppermute | solution.py:648
  93.1 7.7 %collective-permute-start.17 = (bf16[4,128,128]{2,1,0:T(8,128)(2,1)S(1)}, bf16[4,128,128]{2,1,0:T(8,128)(2,1)S(1)}, u32[]{:S(2)}, u32[]{:S(2)}) collective-permute-start(bf16[4,128,128]{2,1,0:T(8,128)(2,1)S(1)} %get-tuple-element.48), channel_id=1, source_target_pairs={{0,32},{4,36},{8,40},{12,44},{16,48},{20,52},{24,56},{28,60},{32,6... | collective-permute-start | bytes 393224 | tf_op jit(solution)/shard_map/ppermute | solution.py:652
  93.7 7.0 %collective-permute-start.18 = (bf16[4,128,128]{2,1,0:T(8,128)(2,1)S(1)}, bf16[4,128,128]{2,1,0:T(8,128)(2,1)S(1)}, u32[]{:S(2)}, u32[]{:S(2)}) collective-permute-start(bf16[4,128,128]{2,1,0:T(8,128)(2,1)S(1)} %get-tuple-element.49), channel_id=1, source_target_pairs={{0,64},{4,68},{8,72},{12,76},{16,80},{20,84},{24,88},{28,92},{32,9... | collective-permute-start | bytes 393224 | tf_op jit(solution)/shard_map/ppermute | solution.py:652
  95.6 6.0 %collective-permute-start.19 = (bf16[4,128,128]{2,1,0:T(8,128)(2,1)S(1)}, bf16[4,128,128]{2,1,0:T(8,128)(2,1)S(1)}, u32[]{:S(2)}, u32[]{:S(2)}) collective-permute-start(bf16[4,128,128]{2,1,0:T(8,128)(2,1)S(1)} %get-tuple-element.50), channel_id=1, source_target_pairs={{0,96},{4,100},{8,104},{12,108},{16,112},{20,116},{24,120},{28,124... | collective-permute-start | bytes 393224 | tf_op jit(solution)/shard_map/ppermute | solution.py:652
  101.7 15.8 %collective-permute-start.21 = (bf16[2,8,128,128]{3,2,1,0:T(8,128)(2,1)S(1)}, bf16[2,8,128,128]{3,2,1,0:T(8,128)(2,1)S(1)}, u32[]{:S(2)}, u32[]{:S(2)}) collective-permute-start(bf16[2,8,128,128]{3,2,1,0:T(8,128)(2,1)S(1)} %sort_kernel.1.after.pair), channel_id=1, source_target_pairs={{0,8},{4,12},{8,16},{12,20},{16,24},{20,28},{24,0},{28,4},{32,40},... | collective-permute-start | bytes 1572872 | tf_op jit(solution)/shard_map/ppermute | solution.py:656
  107.5 11.0 %collective-permute-start.23 = (bf16[2,8,128,128]{3,2,1,0:T(8,128)(2,1)S(1)}, bf16[2,8,128,128]{3,2,1,0:T(8,128)(2,1)S(1)}, u32[]{:S(2)}, u32[]{:S(2)}) collective-permute-start(bf16[2,8,128,128]{3,2,1,0:T(8,128)(2,1)S(1)} %sort_kernel.1.after.pair), channel_id=1, source_target_pairs={{0,24},{4,28},{8,0},{12,4},{16,8},{20,12},{24,16},{28,20},{32,56},... | collective-permute-start | bytes 1572872 | tf_op jit(solution)/shard_map/ppermute | solution.py:656
  117.5 8.3 %collective-permute-start.22 = (bf16[8,128,128]{2,1,0:T(8,128)(2,1)S(1)}, bf16[8,128,128]{2,1,0:T(8,128)(2,1)S(1)}, u32[]{:S(2)}, u32[]{:S(2)}) collective-permute-start(bf16[8,128,128]{2,1,0:T(8,128)(2,1)S(1)} %slice_bitcast_fusion.1), channel_id=1, source_target_pairs={{0,8},{4,12},{8,16},{12,20},{16,24},{20,28},{24,0},{28,4},{32,40},... | collective-permute-start | bytes 786440 | tf_op jit(solution)/shard_map/ppermute | solution.py:656
  118.5 8.1 %collective-permute-start.24 = (bf16[8,128,128]{2,1,0:T(8,128)(2,1)S(1)}, bf16[8,128,128]{2,1,0:T(8,128)(2,1)S(1)}, u32[]{:S(2)}, u32[]{:S(2)}) collective-permute-start(bf16[8,128,128]{2,1,0:T(8,128)(2,1)S(1)} %slice_bitcast_fusion), channel_id=1, source_target_pairs={{0,24},{4,28},{8,0},{12,4},{16,8},{20,12},{24,16},{28,20},{32,56},... | collective-permute-start | bytes 786440 | tf_op jit(solution)/shard_map/ppermute | solution.py:656
  131.6 6.9 %collective-permute-start.26 = (bf16[256,128]{1,0:T(8,128)(2,1)S(1)}, bf16[256,128]{1,0:T(8,128)(2,1)S(1)}, u32[]{:S(2)}, u32[]{:S(2)}) collective-permute-start(bf16[256,128]{1,0:T(8,128)(2,1)S(1)} %get-tuple-element.61), channel_id=1, source_target_pairs={{0,32},{4,36},{8,40},{12,44},{16,48},{20,52},{24,56},{28,60},{32,6... | collective-permute-start | bytes 196616 | tf_op jit(solution)/shard_map/ppermute | solution.py:652
  132.4 6.1 %collective-permute-start.27 = (bf16[256,128]{1,0:T(8,128)(2,1)S(1)}, bf16[256,128]{1,0:T(8,128)(2,1)S(1)}, u32[]{:S(2)}, u32[]{:S(2)}) collective-permute-start(bf16[256,128]{1,0:T(8,128)(2,1)S(1)} %get-tuple-element.62), channel_id=1, source_target_pairs={{0,64},{4,68},{8,72},{12,76},{16,80},{20,84},{24,88},{28,92},{32,9... | collective-permute-start | bytes 196616 | tf_op jit(solution)/shard_map/ppermute | solution.py:652
  (18 other events, 219.1 us)
where the time goes:
time: 140 us
  waiting for transfers between devices  50.3 us (36%)
  starting transfers between devices  45.6 us (33%)
  Pallas kernels  38.7 us (28%)
  local copies, waits for them, and re-layouts  3.55 us (3%)
    ppermute x10, waiting for transfers between devices, along_x(): return lax.ppermute(value, 'tp', [(i, (i + by) % 4) for i in range(4)])  18.6 us
    ppermute x10, starting transfers between devices, along_x(): return lax.ppermute(value, 'tp', [(i, (i + by) % 4) for i in range(4)])  12.5 us
    ppermute x9, waiting for transfers between devices, along_z(): lax.ppermute(value, 'ctx', [(i, (i + 8 * by) % CTX) for i in range(CTX)])  12.2 us
    ppermute x9, starting transfers between devices, along_z(): lax.ppermute(value, 'ctx', [(i, (i + 8 * by) % CTX) for i in range(CTX)])  12 us
    pallas_call x1, Pallas kernels, features(): pl.pallas_call(feature_kernel, out_shape=(jax.ShapeDtypeStruct((CTX, 2 *...  9.83 us
    all_to_all x1, starting transfers between devices, body(): received = lax.all_to_all(send, 'ctx', 0, 0, tiled=True)  8.47 us
    all_to_all x1, waiting for transfers between devices, body(): returned = lax.all_to_all(convolve(received), 'ctx', 0, 0, tiled=True)  6.49 us
    all_to_all x1, starting transfers between devices, body(): returned = lax.all_to_all(convolve(received), 'ctx', 0, 0, tiled=True)  6.2 us
  transfers between devices with their start and end apart: 31, of which 18 were waited for; matrix products, arithmetic and copies ran while one was open for 1% of the time, Pallas kernels for 15%

commit v1 on v0

--- a/solution.py
+++ b/solution.py
@@ -47,63 +47,71 @@
     return lax.axis_index("tp").astype(jnp.int32), r, lax.div(r, 8), lax.div(p, 2), lax.rem(p, 2)
 
 
+def selected(ids, table, cols):
+    vocab = lax.broadcasted_iota(jnp.int32, (VOCAB, 128), 0)
+    pieces = [jnp.where(ids[:, c : c + 128] == vocab, 1.0, 0.0).T for c in range(0, ids.shape[1], 128)]
+    selector = jnp.concatenate(pieces, axis=0).astype(bf16)
+    return [dot(selector, table[:, c]) for c in cols]
+
+
+PARTS = [slice(k * SHARE, (k + 1) * SHARE) for k in range(4)]
+
+
+def embed_kernel(ids, table, gain, scaled_rows, squares, share, edge, embedded):
+    total = jnp.zeros((ROWS, 1), f32)
+    for cols, rows in zip(PARTS, selected(ids, table, PARTS), strict=True):
+        total = total + jnp.sum(rows * rows, axis=1, keepdims=True)
+        embedded[:, cols] = rows.astype(bf16)
+        scaled_rows[:, cols] = (rows * gain[:, cols]).astype(bf16)
+    squares[...] = total
+    scale = lax.rsqrt(total[ROWS - HALO :] * (1.0 / D) + epsilon)
+    edge[...] = (embedded[ROWS - HALO :, :].astype(f32) * scale * gain[...]).astype(bf16)
+    share[...] = embedded[:, pl.ds(pl.multiple_of(spot()[0] * SHARE, SHARE), SHARE)]
+
+
+def embed(ids, table, gain):
+    return pl.pallas_call(
+        embed_kernel,
+        out_shape=(
+            jax.ShapeDtypeStruct((ROWS, D), bf16),
+            jax.ShapeDtypeStruct((ROWS, 1), f32),
+            jax.ShapeDtypeStruct((ROWS, SHARE), bf16),
+            jax.ShapeDtypeStruct((HALO, D), bf16),
+        ),
+        in_specs=[VMEM] * 3,
+        out_specs=(VMEM,) * 4,
+        scratch_shapes=[pltpu.VMEM((ROWS, D), bf16)],
+        compiler_params=params(24),
+        cost_estimate=cost(20_000_000_000, 6_000_000),
+        name="embed",
+    )(ids, table, gain)
+
+
 def feature_kernel(
-    ids, ids_before, gain, taps, skip, filters, table, weight_hbm, mix_hbm,
-    send, mixed0, share, cut1, cut2, cut3,
-    weight, embedded, normed, acc, cut, kept,
-    weight_sem, cut_sem, out_sem, share_sem,
+    edge_before, scaled_rows, squares, taps, skip, filters, weight, mix_hbm,
+    send, mixed0, cut1, cut2, cut3,
+    rows_all, acc, cut, cut_sem, out_sem,
 ):
     x, r, _, _, core = spot()
-    parts = 4
-    deep = D // parts
-
-    def weight_copy(k, i):
-        rows = pl.ds(k * deep, deep)
-        return pltpu.make_async_copy(
-            weight_hbm.at[i, rows, :], weight.at[i, rows, :], weight_sem.at[k, i]
-        )
 
     def cut_copy(k):
         rows = pl.ds(pl.multiple_of(core * (WIDTH // 2), WIDTH // 2), WIDTH // 2)
         cols = pl.ds(pl.multiple_of(lax.rem(x + k, 4) * SHARE, SHARE), SHARE)
         return pltpu.make_async_copy(mix_hbm.at[rows, cols], cut.at[k - 1], cut_sem.at[k - 1])
 
-    for k in range(parts):
-        for i in range(3):
-            weight_copy(k, i).start()
+    for k in (1, 2, 3):
+        cut_copy(k).start()
     direct = jnp.broadcast_to(skip[...], (128, WIDTH)).T
     lag = lax.broadcasted_iota(jnp.int32, (WIDTH, 128), 1)
     first = filters[:, :128] + jnp.where((lag == 0) & (r == 0), direct, 0.0)
     lags = jnp.concatenate([first, filters[:, 128:]], axis=1)
     send[:, PER:, :] = lags.astype(bf16).reshape(CTX, PER, ROWS)
-    vocab = lax.broadcasted_iota(jnp.int32, (VOCAB, 128), 0)
-    halo = jnp.where(ids_before[:, 128:] == vocab, 1.0, 0.0).T[128 - HALO :]
-    own = [jnp.where(ids[:, c : c + 128] == vocab, 1.0, 0.0).T for c in (0, 128)]
-    selector = jnp.concatenate([halo, *own], axis=0).astype(bf16)
-    squares = jnp.zeros((ROWS + HALO, 1), f32)
-    for k in range(parts):
-        cols = pl.ds(k * deep, deep)
-        rows = dot(selector, table[:, cols])
-        squares = squares + jnp.sum(rows * rows, axis=1, keepdims=True)
-        embedded[:, cols] = rows.astype(bf16)
-        normed[:, cols] = (rows * gain[:, cols]).astype(bf16)
-    scale = lax.rsqrt(squares * (1.0 / D) + epsilon)
-    row_index = lax.broadcasted_iota(jnp.int32, (ROWS + HALO, 1), 0)
-    scale = jnp.where((row_index >= HALO) | (r > 0), scale, 0.0)
-    for k in (1, 2, 3):
-        cut_copy(k).start()
-    kept[...] = embedded[HALO:, pl.ds(pl.multiple_of(x * SHARE, SHARE), SHARE)]
-    share_copy = pltpu.make_async_copy(kept, share, share_sem)
-    share_copy.start()
-    for k in range(parts):
-        rows = pl.ds(k * deep, deep)
-        for i in range(3):
-            weight_copy(k, i).wait()
-            part = dot(normed[:, rows], weight[i, rows, :])
-            if k == 0:
-                acc[i] = part
-            else:
-                acc[i] += part
+    rows_all[HALO:, :] = scaled_rows[...]
+    rows_all[:HALO, :] = edge_before[...]
+    scale = lax.rsqrt(squares[...] * (1.0 / D) + epsilon)
+    scale = jnp.concatenate([jnp.ones((HALO, 1), f32), scale], axis=0)
+    for i in range(3):
+        acc[i] = dot(rows_all[...], weight[i])
     outs = [
         pltpu.make_async_copy(cut.at[n], out, out_sem.at[n])
         for n, out in enumerate((cut1, cut2, cut3))
@@ -122,39 +130,32 @@
     send[:, :PER, :] = (mixed[1] * mixed[2]).T.astype(bf16).reshape(CTX, PER, ROWS)
     for copy in outs:
         copy.wait()
-    share_copy.wait()
-
-
-def features(ids, ids_before, gain, taps, skip, filters, table, weight, mix_weight):
+
+
+def features(edge_before, scaled_rows, squares, taps, skip, filters, weight, mix_weight):
     cut = jax.ShapeDtypeStruct((WIDTH // 2, SHARE), bf16)
     return pl.pallas_call(
         feature_kernel,
         out_shape=(
             jax.ShapeDtypeStruct((CTX, 2 * PER, ROWS), bf16),
             jax.ShapeDtypeStruct((ROWS, WIDTH), f32),
-            jax.ShapeDtypeStruct((ROWS, SHARE), bf16),
             cut,
             cut,
             cut,
         ),
-        in_specs=[VMEM] * 7 + [HBM] * 2,
-        out_specs=(VMEM,) * 2 + (HBM,) * 4,
+        in_specs=[VMEM] * 7 + [HBM],
+        out_specs=(VMEM,) * 2 + (HBM,) * 3,
         scratch_shapes=[
-            pltpu.VMEM((3, D, WIDTH), bf16),
-            pltpu.VMEM((ROWS + HALO, D), bf16),
             pltpu.VMEM((ROWS + HALO, D), bf16),
             pltpu.VMEM((3, ROWS + HALO, WIDTH), f32),
             pltpu.VMEM((3, WIDTH // 2, SHARE), bf16),
-            pltpu.VMEM((ROWS, SHARE), bf16),
-            pltpu.SemaphoreType.DMA((4, 3)),
             pltpu.SemaphoreType.DMA((3,)),
             pltpu.SemaphoreType.DMA((3,)),
-            pltpu.SemaphoreType.DMA,
         ],
-        compiler_params=params(57),
+        compiler_params=params(34),
         cost_estimate=cost(8_000_000_000, 14_000_000),
         name="features",
-    )(ids, ids_before, gain, taps, skip, filters, table, weight, mix_weight)
+    )(edge_before, scaled_rows, squares, taps, skip, filters, weight, mix_weight)
 
 
 def unit(turn):
@@ -203,10 +204,7 @@
     twist = np.stack([np.cos(turn), np.sin(turn)]).astype(np.float32)
     grid = 2 * np.pi * (np.arange(ROWS)[:, None] * np.arange(ROWS)[None, :] % ROWS) / ROWS
     c, s = np.cos(grid), np.sin(grid)
-    forward = np.block([c, s]).astype(np.float32)
-    high = forward.astype(bf16)
-    low = (forward - high.astype(np.float32)).astype(bf16)
-    return twist, np.stack([high, low])
+    return twist, np.block([c, s]).astype(bf16)
 
 
 def conv_kernel(received, twist, table_hbm, out, short, table, high, low, mid, sem):
@@ -240,15 +238,14 @@
     lax.fori_loop(0, 2 * blocks, load, 0)
 
     table_copy.wait()
-    for n in range(2):
-        table[n, :ROWS, :ROWS] = short[n, :, :ROWS]
-        table[n, :ROWS, ROWS:] = -short[n, :, ROWS:]
-        table[n, ROWS:, :ROWS] = short[n, :, ROWS:]
-        table[n, ROWS:, ROWS:] = short[n, :, :ROWS]
+    table[:ROWS, :ROWS] = short[:, :ROWS]
+    table[:ROWS, ROWS:] = -short[:, ROWS:]
+    table[ROWS:, :ROWS] = short[:, ROWS:]
+    table[ROWS:, ROWS:] = short[:, :ROWS]
 
     def transform(rows):
         h, l = high[rows, :], low[rows, :]
-        return dot(h, table[0]) + dot(l, table[0]) + dot(h, table[1])
+        return dot(h, table[...]) + dot(l, table[...])
 
     piece = 128
     for part in range(CTX * PER // piece):
@@ -291,8 +288,8 @@
         in_specs=[VMEM, VMEM, HBM],
         out_specs=VMEM,
         scratch_shapes=[
-            pltpu.VMEM((2, ROWS, 2 * ROWS), bf16),
-            pltpu.VMEM((2, 2 * ROWS, 2 * ROWS), bf16),
+            pltpu.VMEM((ROWS, 2 * ROWS), bf16),
+            pltpu.VMEM((2 * ROWS, 2 * ROWS), bf16),
             pltpu.VMEM((2 * CTX * PER, 2 * ROWS), bf16),
             pltpu.VMEM((2 * CTX * PER, 2 * ROWS), bf16),
             pltpu.VMEM((CTX * PER, 2 * ROWS), f32),
@@ -343,23 +340,28 @@
 
 
 def add_mix_kernel(count, partial, *refs):
-    gated, mine, theirs, out = refs[:count], refs[count : 2 * count], refs[2 * count : 3 * count], refs[-1]
+    gated, mine, theirs, out = refs[:2], refs[2 : 2 + count], refs[2 + count : 2 + 2 * count], refs[-1]
     half = WIDTH // 2
     core = spot()[4]
     here = pl.ds(pl.multiple_of(core * half, half), half)
     there = pl.ds(pl.multiple_of((1 - core) * half, half), half)
     total = partial[...]
-    for g, a, b in zip(gated, mine, theirs, strict=True):
-        total = total + dot(g[:, here], a[...]) + dot(g[:, there], b[...])
+    if count == 1:
+        near = [jnp.concatenate([g[:, here] for g in gated], axis=0)]
+        far = [jnp.concatenate([g[:, there] for g in gated], axis=0)]
+    else:
+        near, far = [g[:, here] for g in gated], [g[:, there] for g in gated]
+    for g, h, a, b in zip(near, far, mine, theirs, strict=True):
+        total = total + dot(g, a[...]) + dot(h, b[...])
     out[...] = total.astype(out.dtype)
 
 
 def mix_add(partial, gated, mine, theirs, dtype):
-    count = len(gated)
+    count = len(mine)
     return pl.pallas_call(
         functools.partial(add_mix_kernel, count),
         out_shape=jax.ShapeDtypeStruct((ROWS, SHARE), dtype),
-        in_specs=[VMEM] * (1 + 3 * count),
+        in_specs=[VMEM] * (3 + 2 * count),
         out_specs=VMEM,
         compiler_params=params(16),
         cost_estimate=cost(1_000_000_000 * count, 2_000_000),
@@ -416,7 +418,7 @@
     factor = math.log2(math.e) / math.sqrt(HEAD_DIM)
     c, s = cosine[...] * scale, sine[...] * scale
     half = HEAD_DIM
-    for k, (out, query_out) in enumerate(zip(outs[:4], outs[4:], strict=True)):
+    for k, out in enumerate(outs):
         lanes = pl.ds(pl.multiple_of(lax.rem(z + k, 4) * HEAD_DIM, HEAD_DIM), HEAD_DIM)
         q, key, value = acc[0, :, lanes], acc[1, :, lanes], acc[2, :, lanes]
         q = (q * c + pltpu.roll(q, HEAD_DIM // 2, 1) * s) * factor
@@ -424,7 +426,7 @@
         value = value * scale
         for n in range(2):
             rows = slice(n * half, (n + 1) * half)
-            query_out[:, rows] = q[rows].T.astype(bf16)
+            out[4 + n] = q[rows].T.astype(bf16)
             out[n] = key[rows].astype(bf16)
             out[2 + n] = value[rows].T.astype(bf16)
 
@@ -433,9 +435,8 @@
     count = len(which)
     last = bool(turns)
     partial = jax.ShapeDtypeStruct((3, ROWS, WIDTH), f32)
-    part = jax.ShapeDtypeStruct((4, 128, 128), bf16)
-    query = jax.ShapeDtypeStruct((HEAD_DIM, ROWS), bf16)
-    outs = (part,) * 4 + (query,) * 4 if last else (partial, jax.ShapeDtypeStruct((ROWS, 1), f32))
+    part = jax.ShapeDtypeStruct((6, 128, 128), bf16)
+    outs = (part,) * 4 if last else (partial, jax.ShapeDtypeStruct((ROWS, 1), f32))
     return pl.pallas_call(
         functools.partial(project_kernel, which, last),
         out_shape=outs,
@@ -450,31 +451,29 @@
     )(*hidden, gain, weight, *before, *turns)
 
 
-def sort_kernel(a0, a1, a2, a3, pairs):
+def sort_kernel(a0, a1, a2, a3, queries, pairs):
     z = spot()[2]
     for k, a in enumerate((a0, a1, a2, a3)):
         at = lax.rem(z + (4 - k), 4)
         for n in range(2):
             pairs[0, 2 * at + n] = a[n]
             pairs[1, 2 * at + n] = a[2 + n]
-
-
-def query_kernel(a0, a1, a2, a3, after, queries):
-    z = spot()[2]
-    for k, a in enumerate((a0, a1, a2, a3)):
-        queries[lax.rem(z + (4 - k), 4)] = a[...]
-
-
-def sort_blocks(kernel, shape, arrived, after=()):
-    return pl.pallas_call(
-        kernel,
-        out_shape=jax.ShapeDtypeStruct(shape, bf16),
-        in_specs=[VMEM] * (4 + len(after)),
-        out_specs=VMEM,
+        queries[at] = jnp.concatenate([a[4], a[5]], axis=1)
+
+
+def sort_blocks(arrived):
+    return pl.pallas_call(
+        sort_kernel,
+        out_shape=(
+            jax.ShapeDtypeStruct((4, HEAD_DIM, ROWS), bf16),
+            jax.ShapeDtypeStruct((2, 8, 128, 128), bf16),
+        ),
+        in_specs=[VMEM] * 4,
+        out_specs=(VMEM, VMEM),
         compiler_params=params(16),
         cost_estimate=cost(1_000, 1_000),
-        name=kernel.__name__,
-    )(*arrived, *after)
+        name="sort",
+    )(*arrived)
 
 
 def fold(queries, pair, first, last, state, zq, lanes, mask=False):
@@ -664,15 +663,15 @@
     token_ids, embed_table, gain_first, feat_weight, short_taps, long_filter,
     skip_gain, mix_weight, gain_second, attn_weight,
 ):
-    ids_before = lax.ppermute(token_ids, "ctx", [(i, i + 1) for i in range(CTX - 1)])
-    send, mixed0, share, *cuts = features(
-        token_ids[None, :],
-        ids_before[None, :],
-        gain_first[None, :],
+    scaled_rows, squares, share, edge = embed(token_ids[None, :], embed_table, gain_first[None, :])
+    edge_before = lax.ppermute(edge, "ctx", [(i, i + 1) for i in range(CTX - 1)])
+    send, mixed0, *cuts = features(
+        edge_before,
+        scaled_rows,
+        squares,
         short_taps,
         skip_gain[None, :],
         long_filter,
-        embed_table,
         feat_weight.transpose(1, 0, 2),
         mix_weight,
     )
@@ -682,10 +681,11 @@
     returned = lax.all_to_all(convolve(received), "ctx", 0, 0, tiled=True)
 
     gated = gate(returned, mixed0)
-    g1, g3, g2 = [along_x(gated, k) for k in (1, 3, 2)]
+    g1, g3 = along_x(gated, 1), along_x(gated, 3)
+    g2 = along_x(g1[: ROWS // 2], 1), along_x(g3[ROWS // 2 :], 3)
     partial = mix_own(gated, share, mix_weight)
     partial = mix_add(partial, (g1, g3), mine[::2], theirs[::2], f32)
-    hidden = mix_add(partial, (g2,), mine[1:2], theirs[1:2], bf16)
+    hidden = mix_add(partial, g2, mine[1:2], theirs[1:2], bf16)
 
     h1, h3 = along_x(hidden, 1), along_x(hidden, 3)
     h2 = along_x(h1[: ROWS // 2], 1), along_x(h3[ROWS // 2 :], 3)
@@ -702,11 +702,8 @@
     partial = project((1, 3), (h1, h3), gain, weight, partial)
     blocks = project((2,), h2, gain, weight, partial, turns)
 
-    blocks, asked = blocks[:4], blocks[4:]
     arrived = [blocks[0]] + [along_z(blocks[k], k) for k in (1, 2, 3)]
-    pair = sort_blocks(sort_kernel, (2, 8, 128, 128), arrived)
-    asked = [asked[0]] + [along_z(asked[k], k) for k in (1, 2, 3)]
-    own = sort_blocks(query_kernel, (4, HEAD_DIM, ROWS), asked, (pair,))
+    own, pair = sort_blocks(arrived)
 
     other = across(own)
     pair1, pair3 = along_y(pair, 1), along_y(pair, 3)

time: 140 us -> 137 us (0.979)
  local copies, waits for them, and re-layouts: 3.55 us -> 8.02 us
  starting transfers between devices: 45.6 us -> 42.8 us
  Pallas kernels: 38.7 us -> 36 us
  waiting for transfers between devices: 50.3 us -> 48.2 us
    unnamed x22 -> x36, local copies, waits for them, and re-layouts: 3.48 us -> 7.93 us
    pallas_call x1, Pallas kernels: 9.83 us -> 5.45 us  [features(): pl.pallas_call(feature_kernel, out_shape=(jax.ShapeDtypeStruct((CTX, 2 *...]
    ppermute x9 -> x6, starting transfers between devices: 12 us -> 8.24 us  [along_z(): lax.ppermute(value, 'ctx', [(i, (i + 8 * by) % CTX) for i in range(CTX)])]
    ppermute x10 -> x11, waiting for transfers between devices: 18.6 us -> 15.6 us  [along_x(): return lax.ppermute(value, 'tp', [(i, (i + by) % 4) for i in range(4)])]
    ppermute x4, waiting for transfers between devices: 0.93 us -> 3.15 us  [along_y(): lax.ppermute(value, 'ctx', [(i, i // 8 * 8 + (i + 2 * by) % 8) for i in r...]
    ppermute x9 -> x6, waiting for transfers between devices: 12.2 us -> 10.2 us  [along_z(): lax.ppermute(value, 'ctx', [(i, (i + 8 * by) % CTX) for i in range(CTX)])]
    pallas_call x2, Pallas kernels: 1.71 us -> 3.13 us  [mix_add(): pl.pallas_call(functools.partial(add_mix_kernel, count), out_shape=jax.Sh...]
    ppermute x10 -> x11, starting transfers between devices: 12.5 us -> 12.1 us  [along_x(): return lax.ppermute(value, 'tp', [(i, (i + by) % 4) for i in range(4)])]
  transfers between devices with their start and end apart: 31 -> 29, of which waited for: 18 -> 19; matrix products, arithmetic and copies ran while one was open for 1% -> 1% of each run, Pallas kernels for 15% -> 16%
where the time goes in v1:
time: 137 us
  waiting for transfers between devices  48.2 us (35%)
  starting transfers between devices  42.8 us (31%)
  Pallas kernels  36 us (26%)
  local copies, waits for them, and re-layouts  8.02 us (6%)
    ppermute x11, waiting for transfers between devices, along_x(): return lax.ppermute(value, 'tp', [(i, (i + by) % 4) for i in range(4)])  15.6 us
    ppermute x11, starting transfers between devices, along_x(): return lax.ppermute(value, 'tp', [(i, (i + by) % 4) for i in range(4)])  12.1 us
    ppermute x6, waiting for transfers between devices, along_z(): lax.ppermute(value, 'ctx', [(i, (i + 8 * by) % CTX) for i in range(CTX)])  10.2 us
    all_to_all x1, starting transfers between devices, body(): received = lax.all_to_all(send, 'ctx', 0, 0, tiled=True)  8.34 us
    ppermute x6, starting transfers between devices, along_z(): lax.ppermute(value, 'ctx', [(i, (i + 8 * by) % CTX) for i in range(CTX)])  8.24 us
    unnamed x36, local copies, waits for them, and re-layouts  7.93 us
    all_to_all x1, waiting for transfers between devices, body(): returned = lax.all_to_all(convolve(received), 'ctx', 0, 0, tiled=True)  6.49 us
    all_to_all x1, starting transfers between devices, body(): returned = lax.all_to_all(convolve(received), 'ctx', 0, 0, tiled=True)  6.34 us
  transfers between devices with their start and end apart: 29, of which 19 were waited for; matrix products, arithmetic and copies ran while one was open for 1% of the time, Pallas kernels for 16%

profile of v1, /device:TPU:30, one launch (start us, length us, event | category | flops | bytes accessed | tf_op | source)
XLA Modules:
  0.0 136.7 jit_solution(16684969529745513630)
XLA Ops:
  6.0 2.3 %collective-permute-start = (bf16[16,3072]{1,0:T(8,128)(2,1)S(1)}, bf16[16,3072]{1,0:T(8,128)(2,1)S(1)}, u32[]{:S(2)}, u32[]{:S(2)}) collective-permute-start(bf16[16,3072]{1,0:T(8,128)(2,1)S(1)} %get-tuple-element.34), channel_id=1, source_target_pairs={{0,4},{4,8},{8,12},{12,16},{16,20},{20,24},{24,28},{28,32},{32,36}... | collective-permute-start | bytes 294920 | tf_op jit(solution)/shard_map/ppermute | solution.py:667
  8.3 3.9 %collective-permute-done.edge_before = bf16[16,3072]{1,0:T(8,128)(2,1)S(1)} collective-permute-done((bf16[16,3072]{1,0:T(8,128)(2,1)S(1)}, bf16[16,3072]{1,0:T(8,128)(2,1)S(1)}, u32[]{:S(2)}, u32[]{:S(2)}) %collective-permute-start) | collective-permute-done | bytes 98336 | tf_op jit(solution)/shard_map/ppermute | solution.py:667
  12.2 5.5 %features.1 = (bf16[32,32,256]{2,1,0:T(8,128)(2,1)}, f32[256,512]{1,0:T(8,128)S(1)}, bf16[256,768]{1,0:T(8,128)(2,1)}, bf16[256,768]{1,0:T(8,128)(2,1)S(1)}, bf16[256,768]{1,0:T(8,128)(2,1)}) custom-call(bf16[16,3072]{1,0:T(8,128)(2,1)S(1)} %collective-permute-done.edge_before, bf16[256,3072]{1,0:T(8,128)(2,1)S(1)} %get-tuple-element.35.scaled_rows, ...), custom_call_target="tpu_custom_call" | custom-call | flops 8000000000 | bytes 14000000 | tf_op jit(solution)/shard_map/features/pallas_call | solution.py:137
  17.7 8.3 %all-to-all-start = ((bf16[32,32,256]{2,1,0:T(8,128)(2,1)}), bf16[32,32,256]{2,1,0:T(8,128)(2,1)S(1)}, u32[]{:S(2)}, u32[]{:S(2)}) async-start(bf16[32,32,256]{2,1,0:T(8,128)(2,1)} %get-tuple-element.37), calls=%async_computation | async-start | bytes 1048576 | tf_op jit(solution)/shard_map/all_to_all | solution.py:680
  29.5 5.9 %all-to-all-done.received = bf16[32,32,256]{2,1,0:T(8,128)(2,1)S(1)} async-done(((bf16[32,32,256]{2,1,0:T(8,128)(2,1)}), bf16[32,32,256]{2,1,0:T(8,128)(2,1)S(1)}, u32[]{:S(2)}, u32[]{:S(2)}) %all-to-all-start) | async-done | bytes 524320 | tf_op jit(solution)/shard_map/all_to_all | solution.py:680
  35.4 5.2 %convolve.1 = bf16[32,16,256]{2,1,0:T(8,128)(2,1)} custom-call(bf16[32,32,256]{2,1,0:T(8,128)(2,1)S(1)} %all-to-all-done.received, f32[2,32,256]{2,1,0:T(8,128)S(1)} %copy-done.3, bf16[256,512]{1,0:T(8,128)(2,1)S(1)} %copy-done.1), custom_call_target="tpu_custom_call" | custom-call | flops 1000 | bytes 1000 | tf_op jit(solution)/shard_map/convolve/pallas_call | solution.py:285
  40.7 6.3 %all-to-all-start.1 = ((bf16[32,16,256]{2,1,0:T(8,128)(2,1)}), bf16[32,16,256]{2,1,0:T(8,128)(2,1)S(1)}, u32[]{:S(2)}, u32[]{:S(2)}) async-start(bf16[32,16,256]{2,1,0:T(8,128)(2,1)} %convolve.1), calls=%async_computation.1 | async-start | bytes 524288 | tf_op jit(solution)/shard_map/all_to_all | solution.py:681
  47.6 6.5 %all-to-all-done.1.returned = bf16[32,16,256]{2,1,0:T(8,128)(2,1)S(1)} async-done(((bf16[32,16,256]{2,1,0:T(8,128)(2,1)}), bf16[32,16,256]{2,1,0:T(8,128)(2,1)S(1)}, u32[]{:S(2)}, u32[]{:S(2)}) %all-to-all-start.1) | async-done | bytes 262176 | tf_op jit(solution)/shard_map/all_to_all | solution.py:681
  59.8 3.3 %collective-permute-done.1.refs_0_ = bf16[256,512]{1,0:T(8,128)(2,1)S(1)} collective-permute-done((bf16[256,512]{1,0:T(8,128)(2,1)S(1)}, bf16[256,512]{1,0:T(8,128)(2,1)S(1)}, u32[]{:S(2)}, u32[]{:S(2)}) %collective-permute-start.1) | collective-permute-done | bytes 262176 | tf_op jit(solution)/shard_map/ppermute | solution.py:647
  65.5 2.0 %mix_add.2.partial = f32[256,768]{1,0:T(8,128)S(1)} custom-call(f32[256,768]{1,0:T(8,128)S(1)} %mix_own.1.partial, bf16[256,512]{1,0:T(8,128)(2,1)S(1)} %collective-permute-done.1.refs_0_, bf16[256,512]{1,0:T(8,128)(2,1)S(1)} %collective-permute-done.2.refs_1_, bf16[256,768]{1,0:T(8,128)(2,1)S(1)} %collective-permute-done.3.refs_2_, ...), custom_call_target="tpu_custom_call" | custom-call | flops 2000000000 | bytes 2000000 | tf_op jit(solution)/shard_map/mix_add/pallas_call | solution.py:361
  68.4 2.9 %collective-permute-done.8.refs_1_ = bf16[128,512]{1,0:T(8,128)(2,1)S(1)} collective-permute-done((bf16[128,512]{1,0:T(8,128)(2,1)S(1)}, bf16[128,512]{1,0:T(8,128)(2,1)S(1)}, u32[]{:S(2)}, u32[]{:S(2)}) %collective-permute-start.8) | collective-permute-done | bytes 131104 | tf_op jit(solution)/shard_map/ppermute | solution.py:647
  72.5 2.0 %collective-permute-start.13 = (bf16[256,768]{1,0:T(8,128)(2,1)}, bf16[256,768]{1,0:T(8,128)(2,1)S(1)}, u32[]{:S(2)}, u32[]{:S(2)}) collective-permute-start(bf16[256,768]{1,0:T(8,128)(2,1)} %mix_add.3.refs_0_), channel_id=1, source_target_pairs={{0,3},{1,0},{2,1},{3,2},{4,7},{5,4},{6,5},{7,6},{8,11},{9,8},{10,9... | collective-permute-start | bytes 1179656 | tf_op jit(solution)/shard_map/ppermute | solution.py:647
  77.7 4.4 %collective-permute-done.11.refs_0_ = bf16[256,768]{1,0:T(8,128)(2,1)S(1)} collective-permute-done((bf16[256,768]{1,0:T(8,128)(2,1)}, bf16[256,768]{1,0:T(8,128)(2,1)S(1)}, u32[]{:S(2)}, u32[]{:S(2)}) %collective-permute-start.11) | collective-permute-done | bytes 393248 | tf_op jit(solution)/shard_map/ppermute | solution.py:647
  84.3 2.6 %project.4 = (f32[3,256,512]{2,1,0:T(8,128)S(1)}, f32[256,1]{1,0:T(8,128)S(1)}) custom-call(bf16[256,768]{1,0:T(8,128)(2,1)S(1)} %collective-permute-done.11.refs_0_, bf16[256,768]{1,0:T(8,128)(2,1)S(1)} %collective-permute-done.13.refs_1_, f32[1,3072]{1,0:T(1,128)S(1)} %bitcast.16, bf16[3,3072,512]{2,1,0:T(8,128)(2,1)S(1)} %bitcast.13, ...), custom_call_target="tpu_custom_call" | custom-call | flops 3000000000 | bytes 8000000 | tf_op jit(solution)/shard_map/project/pallas_call | solution.py:440
  87.8 3.0 %collective-permute-done.14.refs_1_ = bf16[128,768]{1,0:T(8,128)(2,1)S(1)} collective-permute-done((bf16[128,768]{1,0:T(8,128)(2,1)S(1)}, bf16[128,768]{1,0:T(8,128)(2,1)S(1)}, u32[]{:S(2)}, u32[]{:S(2)}) %collective-permute-start.14) | collective-permute-done | bytes 196640 | tf_op jit(solution)/shard_map/ppermute | solution.py:647
  90.9 1.9 %project.5 = (bf16[6,128,128]{2,1,0:T(8,128)(2,1)S(1)}, bf16[6,128,128]{2,1,0:T(8,128)(2,1)S(1)}, bf16[6,128,128]{2,1,0:T(8,128)(2,1)S(1)}, bf16[6,128,128]{2,1,0:T(8,128)(2,1)S(1)}) custom-call(bf16[128,768]{1,0:T(8,128)(2,1)S(1)} %collective-permute-done.12.refs_0_, bf16[128,768]{1,0:T(8,128)(2,1)S(1)} %collective-permute-done.14.refs_1_, ...), custom_call_target="tpu_custom_call" | custom-call | flops 1500000000 | bytes 4000000 | tf_op jit(solution)/shard_map/project/pallas_call | solution.py:440
  93.4 1.9 %collective-permute-start.16 = (bf16[6,128,128]{2,1,0:T(8,128)(2,1)S(1)}, bf16[6,128,128]{2,1,0:T(8,128)(2,1)S(1)}, u32[]{:S(2)}, u32[]{:S(2)}) collective-permute-start(bf16[6,128,128]{2,1,0:T(8,128)(2,1)S(1)} %get-tuple-element.49), channel_id=1, source_target_pairs={{0,64},{4,68},{8,72},{12,76},{16,80},{20,84},{24,88},{28,92},{32,9... | collective-permute-start | bytes 589832 | tf_op jit(solution)/shard_map/ppermute | solution.py:651
  96.1 5.7 %collective-permute-done.15.a1 = bf16[6,128,128]{2,1,0:T(8,128)(2,1)S(1)} collective-permute-done((bf16[6,128,128]{2,1,0:T(8,128)(2,1)S(1)}, bf16[6,128,128]{2,1,0:T(8,128)(2,1)S(1)}, u32[]{:S(2)}, u32[]{:S(2)}) %collective-permute-start.15) | collective-permute-done | bytes 196640 | tf_op jit(solution)/shard_map/ppermute | solution.py:651
  106.4 4.0 %attend_own.1 = (f32[4,1,512]{2,1,0:T(1,128)S(1)}, f32[4,1,512]{2,1,0:T(1,128)S(1)}, f32[4,128,512]{2,1,0:T(8,128)S(1)}) custom-call(bf16[4,128,256]{2,1,0:T(8,128)(2,1)S(1)} %get-tuple-element.51.own, bf16[4,128,256]{2,1,0:T(8,128)(2,1)S(1)} %collective-permute-done.18.other, bf16[2,8,128,128]{3,2,1,0:T(8,128)(2,1)S(1)} %get-tuple-element.52.pair), custom_call_target="tpu_custom_call" | custom-call | flops 1000 | bytes 1000 | tf_op jit(solution)/shard_map/attend_own/pallas_call | solution.py:563
  112.1 2.4 %collective-permute-start.20 = (bf16[8,128,128]{2,1,0:T(8,128)(2,1)S(1)}, bf16[8,128,128]{2,1,0:T(8,128)(2,1)S(1)}, u32[]{:S(2)}, u32[]{:S(2)}) collective-permute-start(bf16[8,128,128]{2,1,0:T(8,128)(2,1)S(1)} %slice_bitcast_fusion.1), channel_id=1, source_target_pairs={{0,8},{4,12},{8,16},{12,20},{16,24},{20,28},{24,0},{28,4},{32,40},... | collective-permute-start | bytes 786440 | tf_op jit(solution)/shard_map/ppermute | solution.py:655
  114.9 6.1 %attend_more.1 = (f32[4,1,512]{2,1,0:T(1,128)S(1)}, f32[4,1,512]{2,1,0:T(1,128)S(1)}, f32[4,128,512]{2,1,0:T(8,128)S(1)}) custom-call(bf16[4,128,256]{2,1,0:T(8,128)(2,1)S(1)} %get-tuple-element.51.own, bf16[4,128,256]{2,1,0:T(8,128)(2,1)S(1)} %collective-permute-done.18.other, bf16[2,8,128,128]{3,2,1,0:T(8,128)(2,1)S(1)} %collective-permute-done.19.refs_0_, ...), custom_call_target="tpu_custom_call" | custom-call | flops 8000000000 | bytes 3000000 | tf_op jit(solution)/shard_map/attend_more/pallas_call | solution.py:576
  122.5 3.1 %attend_last.1 = (f32[4,128,256]{2,1,0:T(8,128)S(1)}, f32[4,1,256]{2,1,0:T(1,128)S(1)}, bf16[4,144,256]{2,1,0:T(8,128)(2,1)S(1)}) custom-call(bf16[4,128,256]{2,1,0:T(8,128)(2,1)S(1)} %get-tuple-element.51.own, bf16[4,128,256]{2,1,0:T(8,128)(2,1)S(1)} %collective-permute-done.18.other, bf16[8,128,128]{2,1,0:T(8,128)(2,1)S(1)} %collective-permute-done.20.refs_0_, ...), custom_call_target="tpu_custom_call" | custom-call | flops 4000000000 | bytes 3000000 | tf_op jit(solution)/shard_map/attend_last/pallas_call | solution.py:588
  128.9 2.7 %collective-permute-start.25 = (bf16[256,128]{1,0:T(8,128)(2,1)S(1)}, bf16[256,128]{1,0:T(8,128)(2,1)S(1)}, u32[]{:S(2)}, u32[]{:S(2)}) collective-permute-start(bf16[256,128]{1,0:T(8,128)(2,1)S(1)} %get-tuple-element.64), channel_id=1, source_target_pairs={{0,64},{4,68},{8,72},{12,76},{16,80},{20,84},{24,88},{28,92},{32,9... | collective-permute-start | bytes 196616 | tf_op jit(solution)/shard_map/ppermute | solution.py:651
  133.0 2.2 %collective-permute-done.25.a2 = bf16[256,128]{1,0:T(8,128)(2,1)S(1)} collective-permute-done((bf16[256,128]{1,0:T(8,128)(2,1)S(1)}, bf16[256,128]{1,0:T(8,128)(2,1)S(1)}, u32[]{:S(2)}, u32[]{:S(2)}) %collective-permute-start.25) | collective-permute-done | bytes 65568 | tf_op jit(solution)/shard_map/ppermute | solution.py:651
  (97 shorter events, 41.5 us)
Async XLA Ops:
  6.0 6.2 %collective-permute-start = (bf16[16,3072]{1,0:T(8,128)(2,1)S(1)}, bf16[16,3072]{1,0:T(8,128)(2,1)S(1)}, u32[]{:S(2)}, u32[]{:S(2)}) collective-permute-start(bf16[16,3072]{1,0:T(8,128)(2,1)S(1)} %get-tuple-element.34), channel_id=1, source_target_pairs={{0,4},{4,8},{8,12},{12,16},{16,20},{20,24},{24,28},{28,32},{32,36}... | collective-permute-start | bytes 294920 | tf_op jit(solution)/shard_map/ppermute | solution.py:667
  17.7 17.7 %all-to-all-start = ((bf16[32,32,256]{2,1,0:T(8,128)(2,1)}), bf16[32,32,256]{2,1,0:T(8,128)(2,1)S(1)}, u32[]{:S(2)}, u32[]{:S(2)}) async-start(bf16[32,32,256]{2,1,0:T(8,128)(2,1)} %get-tuple-element.37), calls=%async_computation | async-start | bytes 1048576 | tf_op jit(solution)/shard_map/all_to_all | solution.py:680
  26.0 21.0 %collective-permute-start.3 = (bf16[256,768]{1,0:T(8,128)(2,1)}, bf16[256,768]{1,0:T(8,128)(2,1)S(1)}, u32[]{:S(2)}, u32[]{:S(2)}) collective-permute-start(bf16[256,768]{1,0:T(8,128)(2,1)} %get-tuple-element.40), channel_id=1, source_target_pairs={{0,1},{1,2},{2,3},{3,0},{4,5},{5,6},{6,7},{7,4},{8,9},{9,10},{10,1... | collective-permute-start | bytes 1179656 | tf_op jit(solution)/shard_map/ppermute | solution.py:647
  26.6 20.7 %collective-permute-start.4 = (bf16[256,768]{1,0:T(8,128)(2,1)}, bf16[256,768]{1,0:T(8,128)(2,1)S(1)}, u32[]{:S(2)}, u32[]{:S(2)}) collective-permute-start(bf16[256,768]{1,0:T(8,128)(2,1)} %get-tuple-element.41), channel_id=1, source_target_pairs={{0,3},{1,0},{2,1},{3,2},{4,7},{5,4},{6,5},{7,6},{8,11},{9,8},{10,9... | collective-permute-start | bytes 1179656 | tf_op jit(solution)/shard_map/ppermute | solution.py:647
  28.1 28.2 %collective-permute-start.9 = (bf16[256,768]{1,0:T(8,128)(2,1)S(1)}, bf16[256,768]{1,0:T(8,128)(2,1)S(1)}, u32[]{:S(2)}, u32[]{:S(2)}) collective-permute-start(bf16[256,768]{1,0:T(8,128)(2,1)S(1)} %get-tuple-element.42), channel_id=1, source_target_pairs={{0,2},{1,3},{2,0},{3,1},{4,6},{5,7},{6,4},{7,5},{8,10},{9,11},{10,... | collective-permute-start | bytes 1179656 | tf_op jit(solution)/shard_map/ppermute | solution.py:647
  40.7 13.4 %all-to-all-start.1 = ((bf16[32,16,256]{2,1,0:T(8,128)(2,1)}), bf16[32,16,256]{2,1,0:T(8,128)(2,1)S(1)}, u32[]{:S(2)}, u32[]{:S(2)}) async-start(bf16[32,16,256]{2,1,0:T(8,128)(2,1)} %convolve.1), calls=%async_computation.1 | async-start | bytes 524288 | tf_op jit(solution)/shard_map/all_to_all | solution.py:681
  47.0 18.5 %collective-permute-start.5 = (bf16[256,768]{1,0:T(8,128)(2,1)S(1)}, bf16[256,768]{1,0:T(8,128)(2,1)}, u32[]{:S(2)}, u32[]{:S(2)}) collective-permute-start(bf16[256,768]{1,0:T(8,128)(2,1)S(1)} %collective-permute-done.3.refs_2_), channel_id=1, source_target_pairs={{0,4},{4,0},{8,12},{12,8},{16,20},{20,16},{24,28},{28,24},{32,36},... | collective-permute-start | bytes 1179656 | tf_op jit(solution)/shard_map/ppermute | solution.py:659
  47.3 18.2 %collective-permute-start.6 = (bf16[256,768]{1,0:T(8,128)(2,1)S(1)}, bf16[256,768]{1,0:T(8,128)(2,1)}, u32[]{:S(2)}, u32[]{:S(2)}) collective-permute-start(bf16[256,768]{1,0:T(8,128)(2,1)S(1)} %collective-permute-done.4.refs_3_), channel_id=1, source_target_pairs={{0,4},{4,0},{8,12},{12,8},{16,20},{20,16},{24,28},{28,24},{32,36},... | collective-permute-start | bytes 1179656 | tf_op jit(solution)/shard_map/ppermute | solution.py:659
  54.3 8.9 %collective-permute-start.1 = (bf16[256,512]{1,0:T(8,128)(2,1)S(1)}, bf16[256,512]{1,0:T(8,128)(2,1)S(1)}, u32[]{:S(2)}, u32[]{:S(2)}) collective-permute-start(bf16[256,512]{1,0:T(8,128)(2,1)S(1)} %gate.1.gated), channel_id=1, source_target_pairs={{0,1},{1,2},{2,3},{3,0},{4,5},{5,6},{6,7},{7,4},{8,9},{9,10},{10,1... | collective-permute-start | bytes 786440 | tf_op jit(solution)/shard_map/ppermute | solution.py:647
  54.8 10.1 %collective-permute-start.2 = (bf16[256,512]{1,0:T(8,128)(2,1)S(1)}, bf16[256,512]{1,0:T(8,128)(2,1)S(1)}, u32[]{:S(2)}, u32[]{:S(2)}) collective-permute-start(bf16[256,512]{1,0:T(8,128)(2,1)S(1)} %gate.1.gated), channel_id=1, source_target_pairs={{0,3},{1,0},{2,1},{3,2},{4,7},{5,4},{6,5},{7,6},{8,11},{9,8},{10,9... | collective-permute-start | bytes 786440 | tf_op jit(solution)/shard_map/ppermute | solution.py:647
  56.4 11.2 %collective-permute-start.10 = (bf16[256,768]{1,0:T(8,128)(2,1)S(1)}, bf16[256,768]{1,0:T(8,128)(2,1)S(1)}, u32[]{:S(2)}, u32[]{:S(2)}) collective-permute-start(bf16[256,768]{1,0:T(8,128)(2,1)S(1)} %collective-permute-done.9.refs_2_), channel_id=1, source_target_pairs={{0,4},{4,0},{8,12},{12,8},{16,20},{20,16},{24,28},{28,24},{32,36},... | collective-permute-start | bytes 1179656 | tf_op jit(solution)/shard_map/ppermute | solution.py:659
  64.9 6.4 %collective-permute-start.8 = (bf16[128,512]{1,0:T(8,128)(2,1)S(1)}, bf16[128,512]{1,0:T(8,128)(2,1)S(1)}, u32[]{:S(2)}, u32[]{:S(2)}) collective-permute-start(bf16[128,512]{1,0:T(8,128)(2,1)S(1)} %slice.25), channel_id=1, source_target_pairs={{0,3},{1,0},{2,1},{3,2},{4,7},{5,4},{6,5},{7,6},{8,11},{9,8},{10,9... | collective-permute-start | bytes 393224 | tf_op jit(solution)/shard_map/ppermute | solution.py:647
  72.5 9.6 %collective-permute-start.11 = (bf16[256,768]{1,0:T(8,128)(2,1)}, bf16[256,768]{1,0:T(8,128)(2,1)S(1)}, u32[]{:S(2)}, u32[]{:S(2)}) collective-permute-start(bf16[256,768]{1,0:T(8,128)(2,1)} %mix_add.3.refs_0_), channel_id=1, source_target_pairs={{0,1},{1,2},{2,3},{3,0},{4,5},{5,6},{6,7},{7,4},{8,9},{9,10},{10,1... | collective-permute-start | bytes 1179656 | tf_op jit(solution)/shard_map/ppermute | solution.py:647
  72.5 11.4 %collective-permute-start.13 = (bf16[256,768]{1,0:T(8,128)(2,1)}, bf16[256,768]{1,0:T(8,128)(2,1)S(1)}, u32[]{:S(2)}, u32[]{:S(2)}) collective-permute-start(bf16[256,768]{1,0:T(8,128)(2,1)} %mix_add.3.refs_0_), channel_id=1, source_target_pairs={{0,3},{1,0},{2,1},{3,2},{4,7},{5,4},{6,5},{7,6},{8,11},{9,8},{10,9... | collective-permute-start | bytes 1179656 | tf_op jit(solution)/shard_map/ppermute | solution.py:647
  82.1 5.7 %collective-permute-start.12 = (bf16[128,768]{1,0:T(8,128)(2,1)S(1)}, bf16[128,768]{1,0:T(8,128)(2,1)S(1)}, u32[]{:S(2)}, u32[]{:S(2)}) collective-permute-start(bf16[128,768]{1,0:T(8,128)(2,1)S(1)} %slice.26), channel_id=1, source_target_pairs={{0,1},{1,2},{2,3},{3,0},{4,5},{5,6},{6,7},{7,4},{8,9},{9,10},{10,1... | collective-permute-start | bytes 589832 | tf_op jit(solution)/shard_map/ppermute | solution.py:647
  83.9 6.9 %collective-permute-start.14 = (bf16[128,768]{1,0:T(8,128)(2,1)S(1)}, bf16[128,768]{1,0:T(8,128)(2,1)S(1)}, u32[]{:S(2)}, u32[]{:S(2)}) collective-permute-start(bf16[128,768]{1,0:T(8,128)(2,1)S(1)} %slice.27), channel_id=1, source_target_pairs={{0,3},{1,0},{2,1},{3,2},{4,7},{5,4},{6,5},{7,6},{8,11},{9,8},{10,9... | collective-permute-start | bytes 589832 | tf_op jit(solution)/shard_map/ppermute | solution.py:647
  92.8 9.1 %collective-permute-start.15 = (bf16[6,128,128]{2,1,0:T(8,128)(2,1)S(1)}, bf16[6,128,128]{2,1,0:T(8,128)(2,1)S(1)}, u32[]{:S(2)}, u32[]{:S(2)}) collective-permute-start(bf16[6,128,128]{2,1,0:T(8,128)(2,1)S(1)} %get-tuple-element.48), channel_id=1, source_target_pairs={{0,32},{4,36},{8,40},{12,44},{16,48},{20,52},{24,56},{28,60},{32,6... | collective-permute-start | bytes 589832 | tf_op jit(solution)/shard_map/ppermute | solution.py:651
  93.4 8.5 %collective-permute-start.16 = (bf16[6,128,128]{2,1,0:T(8,128)(2,1)S(1)}, bf16[6,128,128]{2,1,0:T(8,128)(2,1)S(1)}, u32[]{:S(2)}, u32[]{:S(2)}) collective-permute-start(bf16[6,128,128]{2,1,0:T(8,128)(2,1)S(1)} %get-tuple-element.49), channel_id=1, source_target_pairs={{0,64},{4,68},{8,72},{12,76},{16,80},{20,84},{24,88},{28,92},{32,9... | collective-permute-start | bytes 589832 | tf_op jit(solution)/shard_map/ppermute | solution.py:651
  95.3 7.4 %collective-permute-start.17 = (bf16[6,128,128]{2,1,0:T(8,128)(2,1)S(1)}, bf16[6,128,128]{2,1,0:T(8,128)(2,1)S(1)}, u32[]{:S(2)}, u32[]{:S(2)}) collective-permute-start(bf16[6,128,128]{2,1,0:T(8,128)(2,1)S(1)} %get-tuple-element.50), channel_id=1, source_target_pairs={{0,96},{4,100},{8,104},{12,108},{16,112},{20,116},{24,120},{28,124... | collective-permute-start | bytes 589832 | tf_op jit(solution)/shard_map/ppermute | solution.py:651
  102.8 9.3 %collective-permute-start.19 = (bf16[2,8,128,128]{3,2,1,0:T(8,128)(2,1)S(1)}, bf16[2,8,128,128]{3,2,1,0:T(8,128)(2,1)S(1)}, u32[]{:S(2)}, u32[]{:S(2)}) collective-permute-start(bf16[2,8,128,128]{3,2,1,0:T(8,128)(2,1)S(1)} %get-tuple-element.52.pair), channel_id=1, source_target_pairs={{0,8},{4,12},{8,16},{12,20},{16,24},{20,28},{24,0},{28,4},{32,40},... | collective-permute-start | bytes 1572872 | tf_op jit(solution)/shard_map/ppermute | solution.py:655
  104.1 10.5 %collective-permute-start.21 = (bf16[2,8,128,128]{3,2,1,0:T(8,128)(2,1)S(1)}, bf16[2,8,128,128]{3,2,1,0:T(8,128)(2,1)S(1)}, u32[]{:S(2)}, u32[]{:S(2)}) collective-permute-start(bf16[2,8,128,128]{3,2,1,0:T(8,128)(2,1)S(1)} %get-tuple-element.52.pair), channel_id=1, source_target_pairs={{0,24},{4,28},{8,0},{12,4},{16,8},{20,12},{24,16},{28,20},{32,56},... | collective-permute-start | bytes 1572872 | tf_op jit(solution)/shard_map/ppermute | solution.py:655
  112.1 8.8 %collective-permute-start.20 = (bf16[8,128,128]{2,1,0:T(8,128)(2,1)S(1)}, bf16[8,128,128]{2,1,0:T(8,128)(2,1)S(1)}, u32[]{:S(2)}, u32[]{:S(2)}) collective-permute-start(bf16[8,128,128]{2,1,0:T(8,128)(2,1)S(1)} %slice_bitcast_fusion.1), channel_id=1, source_target_pairs={{0,8},{4,12},{8,16},{12,20},{16,24},{20,28},{24,0},{28,4},{32,40},... | collective-permute-start | bytes 786440 | tf_op jit(solution)/shard_map/ppermute | solution.py:655
  114.6 7.9 %collective-permute-start.22 = (bf16[8,128,128]{2,1,0:T(8,128)(2,1)S(1)}, bf16[8,128,128]{2,1,0:T(8,128)(2,1)S(1)}, u32[]{:S(2)}, u32[]{:S(2)}) collective-permute-start(bf16[8,128,128]{2,1,0:T(8,128)(2,1)S(1)} %slice_bitcast_fusion), channel_id=1, source_target_pairs={{0,24},{4,28},{8,0},{12,4},{16,8},{20,12},{24,16},{28,20},{32,56},... | collective-permute-start | bytes 786440 | tf_op jit(solution)/shard_map/ppermute | solution.py:655
  128.9 6.2 %collective-permute-start.25 = (bf16[256,128]{1,0:T(8,128)(2,1)S(1)}, bf16[256,128]{1,0:T(8,128)(2,1)S(1)}, u32[]{:S(2)}, u32[]{:S(2)}) collective-permute-start(bf16[256,128]{1,0:T(8,128)(2,1)S(1)} %get-tuple-element.64), channel_id=1, source_target_pairs={{0,64},{4,68},{8,72},{12,76},{16,80},{20,84},{24,88},{28,92},{32,9... | collective-permute-start | bytes 196616 | tf_op jit(solution)/shard_map/ppermute | solution.py:651
  (23 other events, 182.4 us)

commit v2 on v1

--- a/solution.py
+++ b/solution.py
@@ -87,10 +87,28 @@
     )(ids, table, gain)
 
 
+def product_kernel(scaled_rows, squares, weight, out):
+    scale = lax.rsqrt(squares[...] * (1.0 / D) + epsilon)
+    for i in range(3):
+        out[i] = (dot(scaled_rows[...], weight[i]) * scale).astype(bf16)
+
+
+def own_features(scaled_rows, squares, weight):
+    return pl.pallas_call(
+        product_kernel,
+        out_shape=jax.ShapeDtypeStruct((3, ROWS, WIDTH), bf16),
+        in_specs=[VMEM] * 3,
+        out_specs=VMEM,
+        compiler_params=params(34),
+        cost_estimate=cost(8_000_000_000, 12_000_000),
+        name="own_features",
+    )(scaled_rows, squares, weight)
+
+
 def feature_kernel(
-    edge_before, scaled_rows, squares, taps, skip, filters, weight, mix_hbm,
+    edge_before, own, taps, skip, filters, weight, mix_hbm,
     send, mixed0, cut1, cut2, cut3,
-    rows_all, acc, cut, cut_sem, out_sem,
+    cut, cut_sem, out_sem,
 ):
     x, r, _, _, core = spot()
 
@@ -106,12 +124,7 @@
     first = filters[:, :128] + jnp.where((lag == 0) & (r == 0), direct, 0.0)
     lags = jnp.concatenate([first, filters[:, 128:]], axis=1)
     send[:, PER:, :] = lags.astype(bf16).reshape(CTX, PER, ROWS)
-    rows_all[HALO:, :] = scaled_rows[...]
-    rows_all[:HALO, :] = edge_before[...]
-    scale = lax.rsqrt(squares[...] * (1.0 / D) + epsilon)
-    scale = jnp.concatenate([jnp.ones((HALO, 1), f32), scale], axis=0)
-    for i in range(3):
-        acc[i] = dot(rows_all[...], weight[i])
+    edge = [dot(edge_before[...], weight[i]).astype(bf16) for i in range(3)]
     outs = [
         pltpu.make_async_copy(cut.at[n], out, out_sem.at[n])
         for n, out in enumerate((cut1, cut2, cut3))
@@ -121,7 +134,7 @@
         copy.start()
     mixed = []
     for i in range(3):
-        f = (acc[i] * scale).astype(bf16).astype(f32)
+        f = jnp.concatenate([edge[i], own[i]], axis=0).astype(f32)
         m = taps[0, i : i + 1, :] * f
         m = m + taps[1, i : i + 1, :] * pltpu.roll(f, 1, 0)
         m = m + taps[2, i : i + 1, :] * pltpu.roll(f, 2, 0)
@@ -132,7 +145,7 @@
         copy.wait()
 
 
-def features(edge_before, scaled_rows, squares, taps, skip, filters, weight, mix_weight):
+def features(edge_before, own, taps, skip, filters, weight, mix_weight):
     cut = jax.ShapeDtypeStruct((WIDTH // 2, SHARE), bf16)
     return pl.pallas_call(
         feature_kernel,
@@ -143,11 +156,9 @@
             cut,
             cut,
         ),
-        in_specs=[VMEM] * 7 + [HBM],
+        in_specs=[VMEM] * 6 + [HBM],
         out_specs=(VMEM,) * 2 + (HBM,) * 3,
         scratch_shapes=[
-            pltpu.VMEM((ROWS + HALO, D), bf16),
-            pltpu.VMEM((3, ROWS + HALO, WIDTH), f32),
             pltpu.VMEM((3, WIDTH // 2, SHARE), bf16),
             pltpu.SemaphoreType.DMA((3,)),
             pltpu.SemaphoreType.DMA((3,)),
@@ -155,7 +166,7 @@
         compiler_params=params(34),
         cost_estimate=cost(8_000_000_000, 14_000_000),
         name="features",
-    )(edge_before, scaled_rows, squares, taps, skip, filters, weight, mix_weight)
+    )(edge_before, own, taps, skip, filters, weight, mix_weight)
 
 
 def unit(turn):
@@ -507,7 +518,7 @@
             fold(queries(zq), pair, zq, zq + 1, state, zq, lanes)
 
 
-def own_kernel(own, other, pair, peak, total, summed):
+def own_kernel(own, pair, peak, total, summed):
     state = (peak, total, summed)
     halves = (pair.at[0], pair.at[1])
     peak[...] = jnp.full(peak.shape, -1e30, f32)
@@ -515,19 +526,21 @@
     summed[...] = jnp.zeros(summed.shape, f32)
     for zq in range(4):
         fold(own[zq], halves, 0, zq + 1, state, zq, OWN, True)
-    fold_blocks(spot()[4] == 0, lambda zq: other[zq], halves, state, OTHER)
 
 
 def more_kernel(steps, last, own, other, *refs):
     count = len(steps)
     arrays = 2 if last else count
-    y = spot()[3]
+    y, core = spot()[3:]
     pairs, old, refs = refs[:arrays], refs[arrays : arrays + 3], refs[arrays + 3 :]
     state = refs[-3:]
     for a, b in zip(old, state, strict=True):
         b[...] = a[...]
     for n, pair in enumerate(pairs[:count]):
         pair = (pair.at[0], pair.at[1]) if not last else pairs
+        if steps[n] == 0:
+            fold_blocks(core == 0, lambda zq: other[zq], pair, state, OTHER)
+            continue
         earlier = lax.rem(y + (4 - steps[n]), 4) < y
         both = lambda zq: jnp.concatenate([own[zq], other[zq]], axis=1)
         fold_blocks(earlier, both, pair, state, BOTH)
@@ -559,16 +572,16 @@
 )
 
 
-def attend_own(own, other, pair):
+def attend_own(own, pair):
     return pl.pallas_call(
         own_kernel,
         out_shape=STATE,
-        in_specs=[VMEM] * 3,
+        in_specs=[VMEM] * 2,
         out_specs=(VMEM,) * 3,
         compiler_params=params(24),
         cost_estimate=cost(1_000, 1_000),
         name="attend_own",
-    )(own, other, pair)
+    )(own, pair)
 
 
 def attend_more(steps, own, other, pairs, state):
@@ -579,7 +592,7 @@
         in_specs=[VMEM] * (5 + count),
         out_specs=(VMEM,) * 3,
         compiler_params=params(24),
-        cost_estimate=cost(4_000_000_000 * count, 3_000_000),
+        cost_estimate=cost(4_000_000_000 * count if steps[0] else 1_000, 1_000),
         name="attend_more",
     )(own, other, *pairs, *state)
 
@@ -665,14 +678,15 @@
 ):
     scaled_rows, squares, share, edge = embed(token_ids[None, :], embed_table, gain_first[None, :])
     edge_before = lax.ppermute(edge, "ctx", [(i, i + 1) for i in range(CTX - 1)])
+    feat_parts = feat_weight.transpose(1, 0, 2)
+    own_parts = own_features(scaled_rows, squares, feat_parts)
     send, mixed0, *cuts = features(
         edge_before,
-        scaled_rows,
-        squares,
+        own_parts,
         short_taps,
         skip_gain[None, :],
         long_filter,
-        feat_weight.transpose(1, 0, 2),
+        feat_parts,
         mix_weight,
     )
     mine = [along_x(cut, k) for k, cut in zip((1, 2, 3), cuts, strict=True)]
@@ -705,10 +719,12 @@
     arrived = [blocks[0]] + [along_z(blocks[k], k) for k in (1, 2, 3)]
     own, pair = sort_blocks(arrived)
 
-    other = across(own)
     pair1, pair3 = along_y(pair, 1), along_y(pair, 3)
     far = along_y(pair1[0], 1), along_y(pair3[1], 3)
-    state = attend_own(own, other, pair)
+    state = attend_own(own, pair)
+    own_after, *state = lax.optimization_barrier((own, *state))
+    other = across(own_after)
+    state = attend_more((0,), own, other, (pair,), state)
     state = attend_more((1, 3), own, other, (pair1, pair3), state)
     kept, level, sent = attend_last((2,), own, other, far, state)
     parts = join(kept, level, across(sent))

time: 137 us -> 136 us (level)
  waiting for transfers between devices: 48.2 us -> 45.4 us
  Pallas kernels: 36 us -> 37.4 us
    ppermute x1, waiting for transfers between devices: 3.88 us -> 1.26 us  [body(): lax.ppermute(edge, 'ctx', [(i, i + 1) for i in range(CTX - 1)])]
    pallas_call x1 -> x2, Pallas kernels: 6.06 us -> 8.58 us  [attend_more(): pl.pallas_call(functools.partial(more_kernel, steps, False), out_shape=ST...]
    pallas_call x1, Pallas kernels: 5.45 us -> 4.02 us  [features(): pl.pallas_call(feature_kernel, out_shape=(jax.ShapeDtypeStruct((CTX, 2 *...]
    pallas_call x1 -> x2, Pallas kernels: 4.01 us -> 4.39 us  [the longest x1 2.68 us: own_features(): pl.pallas_call(product_kernel, out_shape=jax.ShapeDtypeStruct((3, ROWS, W...]
  transfers between devices with their start and end apart: 29 -> 29, of which waited for: 19 -> 19; matrix products, arithmetic and copies ran while one was open for 1% -> 1% of each run, Pallas kernels for 16% -> 18%
where the time goes in v2:
time: 136 us; the launch traced here: 135 us
  waiting for transfers between devices  45.4 us (33%)
  starting transfers between devices  42.6 us (31%)
  Pallas kernels  37.4 us (28%)
  local copies, waits for them, and re-layouts  8.03 us (6%)
    ppermute x11, waiting for transfers between devices, along_x(): return lax.ppermute(value, 'tp', [(i, (i + by) % 4) for i in range(4)])  15.6 us
    ppermute x11, starting transfers between devices, along_x(): return lax.ppermute(value, 'tp', [(i, (i + by) % 4) for i in range(4)])  12.1 us
    ppermute x6, waiting for transfers between devices, along_z(): lax.ppermute(value, 'ctx', [(i, (i + 8 * by) % CTX) for i in range(CTX)])  10.2 us
    pallas_call x2, Pallas kernels, attend_more(): pl.pallas_call(functools.partial(more_kernel, steps, False), out_shape=ST...  8.58 us
    all_to_all x1, starting transfers between devices, body(): received = lax.all_to_all(send, 'ctx', 0, 0, tiled=True)  8.33 us
    ppermute x6, starting transfers between devices, along_z(): lax.ppermute(value, 'ctx', [(i, (i + 8 * by) % CTX) for i in range(CTX)])  8.23 us
    unnamed x36, local copies, waits for them, and re-layouts  7.94 us
    all_to_all x1, waiting for transfers between devices, body(): returned = lax.all_to_all(convolve(received), 'ctx', 0, 0, tiled=True)  6.49 us
  transfers between devices with their start and end apart: 29, of which 19 were waited for; matrix products, arithmetic and copies ran while one was open for 1% of the time, Pallas kernels for 18%

profile of v2, /device:TPU:30, one launch (start us, length us, event | category | flops | bytes accessed | tf_op | source)
XLA Modules:
  0.0 135.1 jit_solution(11927672125307814594)
XLA Ops:
  6.0 2.0 %collective-permute-start = (bf16[16,3072]{1,0:T(8,128)(2,1)S(1)}, bf16[16,3072]{1,0:T(8,128)(2,1)S(1)}, u32[]{:S(2)}, u32[]{:S(2)}) collective-permute-start(bf16[16,3072]{1,0:T(8,128)(2,1)S(1)} %get-tuple-element.41), channel_id=1, source_target_pairs={{0,4},{4,8},{8,12},{12,16},{16,20},{20,24},{24,28},{28,32},{32,36}... | collective-permute-start | bytes 294920 | tf_op jit(solution)/shard_map/ppermute | solution.py:680
  8.1 2.7 %own_features.1.own = bf16[3,256,512]{2,1,0:T(8,128)(2,1)S(1)} custom-call(bf16[256,3072]{1,0:T(8,128)(2,1)S(1)} %get-tuple-element.42.scaled_rows, f32[256,1]{1,0:T(8,128)S(1)} %get-tuple-element.43.squares, bf16[3,3072,512]{2,1,0:T(8,128)(2,1)S(1)} %bitcast.18), custom_call_target="tpu_custom_call" | custom-call | flops 8000000000 | bytes 12000000 | tf_op jit(solution)/shard_map/own_features/pallas_call | solution.py:97
  12.1 4.0 %features.1 = (bf16[32,32,256]{2,1,0:T(8,128)(2,1)}, f32[256,512]{1,0:T(8,128)S(1)}, bf16[256,768]{1,0:T(8,128)(2,1)}, bf16[256,768]{1,0:T(8,128)(2,1)S(1)}, bf16[256,768]{1,0:T(8,128)(2,1)}) custom-call(bf16[16,3072]{1,0:T(8,128)(2,1)S(1)} %collective-permute-done.edge_before, bf16[3,256,512]{2,1,0:T(8,128)(2,1)S(1)} %own_features.1.own, ...), custom_call_target="tpu_custom_call" | custom-call | flops 8000000000 | bytes 14000000 | tf_op jit(solution)/shard_map/features/pallas_call | solution.py:150
  16.1 8.3 %all-to-all-start = ((bf16[32,32,256]{2,1,0:T(8,128)(2,1)}), bf16[32,32,256]{2,1,0:T(8,128)(2,1)S(1)}, u32[]{:S(2)}, u32[]{:S(2)}) async-start(bf16[32,32,256]{2,1,0:T(8,128)(2,1)} %get-tuple-element.44), calls=%async_computation | async-start | bytes 1048576 | tf_op jit(solution)/shard_map/all_to_all | solution.py:694
  27.9 5.9 %all-to-all-done.received = bf16[32,32,256]{2,1,0:T(8,128)(2,1)S(1)} async-done(((bf16[32,32,256]{2,1,0:T(8,128)(2,1)}), bf16[32,32,256]{2,1,0:T(8,128)(2,1)S(1)}, u32[]{:S(2)}, u32[]{:S(2)}) %all-to-all-start) | async-done | bytes 524320 | tf_op jit(solution)/shard_map/all_to_all | solution.py:694
  33.8 5.2 %convolve.1 = bf16[32,16,256]{2,1,0:T(8,128)(2,1)} custom-call(bf16[32,32,256]{2,1,0:T(8,128)(2,1)S(1)} %all-to-all-done.received, f32[2,32,256]{2,1,0:T(8,128)S(1)} %copy-done.3, bf16[256,512]{1,0:T(8,128)(2,1)S(1)} %copy-done.1), custom_call_target="tpu_custom_call" | custom-call | flops 1000 | bytes 1000 | tf_op jit(solution)/shard_map/convolve/pallas_call | solution.py:296
  39.1 6.3 %all-to-all-start.1 = ((bf16[32,16,256]{2,1,0:T(8,128)(2,1)}), bf16[32,16,256]{2,1,0:T(8,128)(2,1)S(1)}, u32[]{:S(2)}, u32[]{:S(2)}) async-start(bf16[32,16,256]{2,1,0:T(8,128)(2,1)} %convolve.1), calls=%async_computation.1 | async-start | bytes 524288 | tf_op jit(solution)/shard_map/all_to_all | solution.py:695
  46.0 6.5 %all-to-all-done.1.returned = bf16[32,16,256]{2,1,0:T(8,128)(2,1)S(1)} async-done(((bf16[32,16,256]{2,1,0:T(8,128)(2,1)}), bf16[32,16,256]{2,1,0:T(8,128)(2,1)S(1)}, u32[]{:S(2)}, u32[]{:S(2)}) %all-to-all-start.1) | async-done | bytes 262176 | tf_op jit(solution)/shard_map/all_to_all | solution.py:695
  58.2 3.3 %collective-permute-done.1.refs_0_ = bf16[256,512]{1,0:T(8,128)(2,1)S(1)} collective-permute-done((bf16[256,512]{1,0:T(8,128)(2,1)S(1)}, bf16[256,512]{1,0:T(8,128)(2,1)S(1)}, u32[]{:S(2)}, u32[]{:S(2)}) %collective-permute-start.1) | collective-permute-done | bytes 262176 | tf_op jit(solution)/shard_map/ppermute | solution.py:660
  63.9 2.0 %mix_add.2.partial = f32[256,768]{1,0:T(8,128)S(1)} custom-call(f32[256,768]{1,0:T(8,128)S(1)} %mix_own.1.partial, bf16[256,512]{1,0:T(8,128)(2,1)S(1)} %collective-permute-done.1.refs_0_, bf16[256,512]{1,0:T(8,128)(2,1)S(1)} %collective-permute-done.2.refs_1_, bf16[256,768]{1,0:T(8,128)(2,1)S(1)} %collective-permute-done.3.refs_2_, ...), custom_call_target="tpu_custom_call" | custom-call | flops 2000000000 | bytes 2000000 | tf_op jit(solution)/shard_map/mix_add/pallas_call | solution.py:372
  66.8 2.9 %collective-permute-done.8.refs_1_ = bf16[128,512]{1,0:T(8,128)(2,1)S(1)} collective-permute-done((bf16[128,512]{1,0:T(8,128)(2,1)S(1)}, bf16[128,512]{1,0:T(8,128)(2,1)S(1)}, u32[]{:S(2)}, u32[]{:S(2)}) %collective-permute-start.8) | collective-permute-done | bytes 131104 | tf_op jit(solution)/shard_map/ppermute | solution.py:660
  70.9 2.0 %collective-permute-start.13 = (bf16[256,768]{1,0:T(8,128)(2,1)}, bf16[256,768]{1,0:T(8,128)(2,1)S(1)}, u32[]{:S(2)}, u32[]{:S(2)}) collective-permute-start(bf16[256,768]{1,0:T(8,128)(2,1)} %mix_add.3.refs_0_), channel_id=1, source_target_pairs={{0,3},{1,0},{2,1},{3,2},{4,7},{5,4},{6,5},{7,6},{8,11},{9,8},{10,9... | collective-permute-start | bytes 1179656 | tf_op jit(solution)/shard_map/ppermute | solution.py:660
  76.1 4.4 %collective-permute-done.11.refs_0_ = bf16[256,768]{1,0:T(8,128)(2,1)S(1)} collective-permute-done((bf16[256,768]{1,0:T(8,128)(2,1)}, bf16[256,768]{1,0:T(8,128)(2,1)S(1)}, u32[]{:S(2)}, u32[]{:S(2)}) %collective-permute-start.11) | collective-permute-done | bytes 393248 | tf_op jit(solution)/shard_map/ppermute | solution.py:660
  82.7 2.6 %project.4 = (f32[3,256,512]{2,1,0:T(8,128)S(1)}, f32[256,1]{1,0:T(8,128)S(1)}) custom-call(bf16[256,768]{1,0:T(8,128)(2,1)S(1)} %collective-permute-done.11.refs_0_, bf16[256,768]{1,0:T(8,128)(2,1)S(1)} %collective-permute-done.13.refs_1_, f32[1,3072]{1,0:T(1,128)S(1)} %bitcast.16, bf16[3,3072,512]{2,1,0:T(8,128)(2,1)S(1)} %bitcast.13, ...), custom_call_target="tpu_custom_call" | custom-call | flops 3000000000 | bytes 8000000 | tf_op jit(solution)/shard_map/project/pallas_call | solution.py:451
  86.2 3.0 %collective-permute-done.14.refs_1_ = bf16[128,768]{1,0:T(8,128)(2,1)S(1)} collective-permute-done((bf16[128,768]{1,0:T(8,128)(2,1)S(1)}, bf16[128,768]{1,0:T(8,128)(2,1)S(1)}, u32[]{:S(2)}, u32[]{:S(2)}) %collective-permute-start.14) | collective-permute-done | bytes 196640 | tf_op jit(solution)/shard_map/ppermute | solution.py:660
  89.3 1.9 %project.5 = (bf16[6,128,128]{2,1,0:T(8,128)(2,1)S(1)}, bf16[6,128,128]{2,1,0:T(8,128)(2,1)S(1)}, bf16[6,128,128]{2,1,0:T(8,128)(2,1)S(1)}, bf16[6,128,128]{2,1,0:T(8,128)(2,1)S(1)}) custom-call(bf16[128,768]{1,0:T(8,128)(2,1)S(1)} %collective-permute-done.12.refs_0_, bf16[128,768]{1,0:T(8,128)(2,1)S(1)} %collective-permute-done.14.refs_1_, ...), custom_call_target="tpu_custom_call" | custom-call | flops 1500000000 | bytes 4000000 | tf_op jit(solution)/shard_map/project/pallas_call | solution.py:451
  91.8 1.9 %collective-permute-start.16 = (bf16[6,128,128]{2,1,0:T(8,128)(2,1)S(1)}, bf16[6,128,128]{2,1,0:T(8,128)(2,1)S(1)}, u32[]{:S(2)}, u32[]{:S(2)}) collective-permute-start(bf16[6,128,128]{2,1,0:T(8,128)(2,1)S(1)} %get-tuple-element.56), channel_id=1, source_target_pairs={{0,64},{4,68},{8,72},{12,76},{16,80},{20,84},{24,88},{28,92},{32,9... | collective-permute-start | bytes 589832 | tf_op jit(solution)/shard_map/ppermute | solution.py:664
  94.6 5.7 %collective-permute-done.15.a1 = bf16[6,128,128]{2,1,0:T(8,128)(2,1)S(1)} collective-permute-done((bf16[6,128,128]{2,1,0:T(8,128)(2,1)S(1)}, bf16[6,128,128]{2,1,0:T(8,128)(2,1)S(1)}, u32[]{:S(2)}, u32[]{:S(2)}) %collective-permute-start.15) | collective-permute-done | bytes 196640 | tf_op jit(solution)/shard_map/ppermute | solution.py:664
  106.7 2.5 %attend_more.2 = (f32[4,1,512]{2,1,0:T(1,128)S(1)}, f32[4,1,512]{2,1,0:T(1,128)S(1)}, f32[4,128,512]{2,1,0:T(8,128)S(1)}) custom-call(bf16[4,128,256]{2,1,0:T(8,128)(2,1)S(1)} %get-tuple-element.63.own, bf16[4,128,256]{2,1,0:T(8,128)(2,1)S(1)} %collective-permute-done.18.other, bf16[2,8,128,128]{3,2,1,0:T(8,128)(2,1)S(1)} %get-tuple-element.59.pair.refs_0_, ...), custom_call_target="tpu_custom_call" | custom-call | flops 1000 | bytes 1000 | tf_op jit(solution)/shard_map/attend_more/pallas_call | solution.py:589
  110.6 2.4 %collective-permute-start.20 = (bf16[8,128,128]{2,1,0:T(8,128)(2,1)S(1)}, bf16[8,128,128]{2,1,0:T(8,128)(2,1)S(1)}, u32[]{:S(2)}, u32[]{:S(2)}) collective-permute-start(bf16[8,128,128]{2,1,0:T(8,128)(2,1)S(1)} %slice_bitcast_fusion.1), channel_id=1, source_target_pairs={{0,8},{4,12},{8,16},{12,20},{16,24},{20,28},{24,0},{28,4},{32,40},... | collective-permute-start | bytes 786440 | tf_op jit(solution)/shard_map/ppermute | solution.py:668
  113.3 6.1 %attend_more.3 = (f32[4,1,512]{2,1,0:T(1,128)S(1)}, f32[4,1,512]{2,1,0:T(1,128)S(1)}, f32[4,128,512]{2,1,0:T(8,128)S(1)}) custom-call(bf16[4,128,256]{2,1,0:T(8,128)(2,1)S(1)} %get-tuple-element.63.own, bf16[4,128,256]{2,1,0:T(8,128)(2,1)S(1)} %collective-permute-done.18.other, bf16[2,8,128,128]{3,2,1,0:T(8,128)(2,1)S(1)} %collective-permute-done.19.refs_0_, ...), custom_call_target="tpu_custom_call" | custom-call | flops 8000000000 | bytes 1000 | tf_op jit(solution)/shard_map/attend_more/pallas_call | solution.py:589
  120.9 3.1 %attend_last.1 = (f32[4,128,256]{2,1,0:T(8,128)S(1)}, f32[4,1,256]{2,1,0:T(1,128)S(1)}, bf16[4,144,256]{2,1,0:T(8,128)(2,1)S(1)}) custom-call(bf16[4,128,256]{2,1,0:T(8,128)(2,1)S(1)} %get-tuple-element.63.own, bf16[4,128,256]{2,1,0:T(8,128)(2,1)S(1)} %collective-permute-done.18.other, bf16[8,128,128]{2,1,0:T(8,128)(2,1)S(1)} %collective-permute-done.20.refs_0_, ...), custom_call_target="tpu_custom_call" | custom-call | flops 4000000000 | bytes 3000000 | tf_op jit(solution)/shard_map/attend_last/pallas_call | solution.py:601
  127.3 2.7 %collective-permute-start.25 = (bf16[256,128]{1,0:T(8,128)(2,1)S(1)}, bf16[256,128]{1,0:T(8,128)(2,1)S(1)}, u32[]{:S(2)}, u32[]{:S(2)}) collective-permute-start(bf16[256,128]{1,0:T(8,128)(2,1)S(1)} %get-tuple-element.78), channel_id=1, source_target_pairs={{0,64},{4,68},{8,72},{12,76},{16,80},{20,84},{24,88},{28,92},{32,9... | collective-permute-start | bytes 196616 | tf_op jit(solution)/shard_map/ppermute | solution.py:664
  131.4 2.2 %collective-permute-done.25.a2 = bf16[256,128]{1,0:T(8,128)(2,1)S(1)} collective-permute-done((bf16[256,128]{1,0:T(8,128)(2,1)S(1)}, bf16[256,128]{1,0:T(8,128)(2,1)S(1)}, u32[]{:S(2)}, u32[]{:S(2)}) %collective-permute-start.25) | collective-permute-done | bytes 65568 | tf_op jit(solution)/shard_map/ppermute | solution.py:664
  (99 shorter events, 44.3 us)
Async XLA Ops:
  6.0 6.1 %collective-permute-start = (bf16[16,3072]{1,0:T(8,128)(2,1)S(1)}, bf16[16,3072]{1,0:T(8,128)(2,1)S(1)}, u32[]{:S(2)}, u32[]{:S(2)}) collective-permute-start(bf16[16,3072]{1,0:T(8,128)(2,1)S(1)} %get-tuple-element.41), channel_id=1, source_target_pairs={{0,4},{4,8},{8,12},{12,16},{16,20},{20,24},{24,28},{28,32},{32,36}... | collective-permute-start | bytes 294920 | tf_op jit(solution)/shard_map/ppermute | solution.py:680
  16.1 17.7 %all-to-all-start = ((bf16[32,32,256]{2,1,0:T(8,128)(2,1)}), bf16[32,32,256]{2,1,0:T(8,128)(2,1)S(1)}, u32[]{:S(2)}, u32[]{:S(2)}) async-start(bf16[32,32,256]{2,1,0:T(8,128)(2,1)} %get-tuple-element.44), calls=%async_computation | async-start | bytes 1048576 | tf_op jit(solution)/shard_map/all_to_all | solution.py:694
  24.5 21.0 %collective-permute-start.3 = (bf16[256,768]{1,0:T(8,128)(2,1)}, bf16[256,768]{1,0:T(8,128)(2,1)S(1)}, u32[]{:S(2)}, u32[]{:S(2)}) collective-permute-start(bf16[256,768]{1,0:T(8,128)(2,1)} %get-tuple-element.47), channel_id=1, source_target_pairs={{0,1},{1,2},{2,3},{3,0},{4,5},{5,6},{6,7},{7,4},{8,9},{9,10},{10,1... | collective-permute-start | bytes 1179656 | tf_op jit(solution)/shard_map/ppermute | solution.py:660
  25.0 20.7 %collective-permute-start.4 = (bf16[256,768]{1,0:T(8,128)(2,1)}, bf16[256,768]{1,0:T(8,128)(2,1)S(1)}, u32[]{:S(2)}, u32[]{:S(2)}) collective-permute-start(bf16[256,768]{1,0:T(8,128)(2,1)} %get-tuple-element.48), channel_id=1, source_target_pairs={{0,3},{1,0},{2,1},{3,2},{4,7},{5,4},{6,5},{7,6},{8,11},{9,8},{10,9... | collective-permute-start | bytes 1179656 | tf_op jit(solution)/shard_map/ppermute | solution.py:660
  26.5 28.2 %collective-permute-start.9 = (bf16[256,768]{1,0:T(8,128)(2,1)S(1)}, bf16[256,768]{1,0:T(8,128)(2,1)S(1)}, u32[]{:S(2)}, u32[]{:S(2)}) collective-permute-start(bf16[256,768]{1,0:T(8,128)(2,1)S(1)} %get-tuple-element.49), channel_id=1, source_target_pairs={{0,2},{1,3},{2,0},{3,1},{4,6},{5,7},{6,4},{7,5},{8,10},{9,11},{10,... | collective-permute-start | bytes 1179656 | tf_op jit(solution)/shard_map/ppermute | solution.py:660
  39.1 13.4 %all-to-all-start.1 = ((bf16[32,16,256]{2,1,0:T(8,128)(2,1)}), bf16[32,16,256]{2,1,0:T(8,128)(2,1)S(1)}, u32[]{:S(2)}, u32[]{:S(2)}) async-start(bf16[32,16,256]{2,1,0:T(8,128)(2,1)} %convolve.1), calls=%async_computation.1 | async-start | bytes 524288 | tf_op jit(solution)/shard_map/all_to_all | solution.py:695
  45.4 18.5 %collective-permute-start.5 = (bf16[256,768]{1,0:T(8,128)(2,1)S(1)}, bf16[256,768]{1,0:T(8,128)(2,1)}, u32[]{:S(2)}, u32[]{:S(2)}) collective-permute-start(bf16[256,768]{1,0:T(8,128)(2,1)S(1)} %collective-permute-done.3.refs_2_), channel_id=1, source_target_pairs={{0,4},{4,0},{8,12},{12,8},{16,20},{20,16},{24,28},{28,24},{32,36},... | collective-permute-start | bytes 1179656 | tf_op jit(solution)/shard_map/ppermute | solution.py:672
  45.7 18.2 %collective-permute-start.6 = (bf16[256,768]{1,0:T(8,128)(2,1)S(1)}, bf16[256,768]{1,0:T(8,128)(2,1)}, u32[]{:S(2)}, u32[]{:S(2)}) collective-permute-start(bf16[256,768]{1,0:T(8,128)(2,1)S(1)} %collective-permute-done.4.refs_3_), channel_id=1, source_target_pairs={{0,4},{4,0},{8,12},{12,8},{16,20},{20,16},{24,28},{28,24},{32,36},... | collective-permute-start | bytes 1179656 | tf_op jit(solution)/shard_map/ppermute | solution.py:672
  52.7 8.9 %collective-permute-start.1 = (bf16[256,512]{1,0:T(8,128)(2,1)S(1)}, bf16[256,512]{1,0:T(8,128)(2,1)S(1)}, u32[]{:S(2)}, u32[]{:S(2)}) collective-permute-start(bf16[256,512]{1,0:T(8,128)(2,1)S(1)} %gate.1.gated), channel_id=1, source_target_pairs={{0,1},{1,2},{2,3},{3,0},{4,5},{5,6},{6,7},{7,4},{8,9},{9,10},{10,1... | collective-permute-start | bytes 786440 | tf_op jit(solution)/shard_map/ppermute | solution.py:660
  53.2 10.1 %collective-permute-start.2 = (bf16[256,512]{1,0:T(8,128)(2,1)S(1)}, bf16[256,512]{1,0:T(8,128)(2,1)S(1)}, u32[]{:S(2)}, u32[]{:S(2)}) collective-permute-start(bf16[256,512]{1,0:T(8,128)(2,1)S(1)} %gate.1.gated), channel_id=1, source_target_pairs={{0,3},{1,0},{2,1},{3,2},{4,7},{5,4},{6,5},{7,6},{8,11},{9,8},{10,9... | collective-permute-start | bytes 786440 | tf_op jit(solution)/shard_map/ppermute | solution.py:660
  54.8 11.2 %collective-permute-start.10 = (bf16[256,768]{1,0:T(8,128)(2,1)S(1)}, bf16[256,768]{1,0:T(8,128)(2,1)S(1)}, u32[]{:S(2)}, u32[]{:S(2)}) collective-permute-start(bf16[256,768]{1,0:T(8,128)(2,1)S(1)} %collective-permute-done.9.refs_2_), channel_id=1, source_target_pairs={{0,4},{4,0},{8,12},{12,8},{16,20},{20,16},{24,28},{28,24},{32,36},... | collective-permute-start | bytes 1179656 | tf_op jit(solution)/shard_map/ppermute | solution.py:672
  63.3 6.4 %collective-permute-start.8 = (bf16[128,512]{1,0:T(8,128)(2,1)S(1)}, bf16[128,512]{1,0:T(8,128)(2,1)S(1)}, u32[]{:S(2)}, u32[]{:S(2)}) collective-permute-start(bf16[128,512]{1,0:T(8,128)(2,1)S(1)} %slice.25), channel_id=1, source_target_pairs={{0,3},{1,0},{2,1},{3,2},{4,7},{5,4},{6,5},{7,6},{8,11},{9,8},{10,9... | collective-permute-start | bytes 393224 | tf_op jit(solution)/shard_map/ppermute | solution.py:660
  70.9 9.6 %collective-permute-start.11 = (bf16[256,768]{1,0:T(8,128)(2,1)}, bf16[256,768]{1,0:T(8,128)(2,1)S(1)}, u32[]{:S(2)}, u32[]{:S(2)}) collective-permute-start(bf16[256,768]{1,0:T(8,128)(2,1)} %mix_add.3.refs_0_), channel_id=1, source_target_pairs={{0,1},{1,2},{2,3},{3,0},{4,5},{5,6},{6,7},{7,4},{8,9},{9,10},{10,1... | collective-permute-start | bytes 1179656 | tf_op jit(solution)/shard_map/ppermute | solution.py:660
  70.9 11.4 %collective-permute-start.13 = (bf16[256,768]{1,0:T(8,128)(2,1)}, bf16[256,768]{1,0:T(8,128)(2,1)S(1)}, u32[]{:S(2)}, u32[]{:S(2)}) collective-permute-start(bf16[256,768]{1,0:T(8,128)(2,1)} %mix_add.3.refs_0_), channel_id=1, source_target_pairs={{0,3},{1,0},{2,1},{3,2},{4,7},{5,4},{6,5},{7,6},{8,11},{9,8},{10,9... | collective-permute-start | bytes 1179656 | tf_op jit(solution)/shard_map/ppermute | solution.py:660
  80.5 5.7 %collective-permute-start.12 = (bf16[128,768]{1,0:T(8,128)(2,1)S(1)}, bf16[128,768]{1,0:T(8,128)(2,1)S(1)}, u32[]{:S(2)}, u32[]{:S(2)}) collective-permute-start(bf16[128,768]{1,0:T(8,128)(2,1)S(1)} %slice.26), channel_id=1, source_target_pairs={{0,1},{1,2},{2,3},{3,0},{4,5},{5,6},{6,7},{7,4},{8,9},{9,10},{10,1... | collective-permute-start | bytes 589832 | tf_op jit(solution)/shard_map/ppermute | solution.py:660
  82.3 6.9 %collective-permute-start.14 = (bf16[128,768]{1,0:T(8,128)(2,1)S(1)}, bf16[128,768]{1,0:T(8,128)(2,1)S(1)}, u32[]{:S(2)}, u32[]{:S(2)}) collective-permute-start(bf16[128,768]{1,0:T(8,128)(2,1)S(1)} %slice.27), channel_id=1, source_target_pairs={{0,3},{1,0},{2,1},{3,2},{4,7},{5,4},{6,5},{7,6},{8,11},{9,8},{10,9... | collective-permute-start | bytes 589832 | tf_op jit(solution)/shard_map/ppermute | solution.py:660
  91.2 9.1 %collective-permute-start.15 = (bf16[6,128,128]{2,1,0:T(8,128)(2,1)S(1)}, bf16[6,128,128]{2,1,0:T(8,128)(2,1)S(1)}, u32[]{:S(2)}, u32[]{:S(2)}) collective-permute-start(bf16[6,128,128]{2,1,0:T(8,128)(2,1)S(1)} %get-tuple-element.55), channel_id=1, source_target_pairs={{0,32},{4,36},{8,40},{12,44},{16,48},{20,52},{24,56},{28,60},{32,6... | collective-permute-start | bytes 589832 | tf_op jit(solution)/shard_map/ppermute | solution.py:664
  91.8 8.5 %collective-permute-start.16 = (bf16[6,128,128]{2,1,0:T(8,128)(2,1)S(1)}, bf16[6,128,128]{2,1,0:T(8,128)(2,1)S(1)}, u32[]{:S(2)}, u32[]{:S(2)}) collective-permute-start(bf16[6,128,128]{2,1,0:T(8,128)(2,1)S(1)} %get-tuple-element.56), channel_id=1, source_target_pairs={{0,64},{4,68},{8,72},{12,76},{16,80},{20,84},{24,88},{28,92},{32,9... | collective-permute-start | bytes 589832 | tf_op jit(solution)/shard_map/ppermute | solution.py:664
  93.7 7.4 %collective-permute-start.17 = (bf16[6,128,128]{2,1,0:T(8,128)(2,1)S(1)}, bf16[6,128,128]{2,1,0:T(8,128)(2,1)S(1)}, u32[]{:S(2)}, u32[]{:S(2)}) collective-permute-start(bf16[6,128,128]{2,1,0:T(8,128)(2,1)S(1)} %get-tuple-element.57), channel_id=1, source_target_pairs={{0,96},{4,100},{8,104},{12,108},{16,112},{20,116},{24,120},{28,124... | collective-permute-start | bytes 589832 | tf_op jit(solution)/shard_map/ppermute | solution.py:664
  101.2 9.3 %collective-permute-start.19 = (bf16[2,8,128,128]{3,2,1,0:T(8,128)(2,1)S(1)}, bf16[2,8,128,128]{3,2,1,0:T(8,128)(2,1)S(1)}, u32[]{:S(2)}, u32[]{:S(2)}) collective-permute-start(bf16[2,8,128,128]{3,2,1,0:T(8,128)(2,1)S(1)} %get-tuple-element.59.pair.refs_0_), channel_id=1, source_target_pairs={{0,8},{4,12},{8,16},{12,20},{16,24},{20,28},{24,0},{28,4},{32,40},... | collective-permute-start | bytes 1572872 | tf_op jit(solution)/shard_map/ppermute | solution.py:668
  102.5 10.5 %collective-permute-start.21 = (bf16[2,8,128,128]{3,2,1,0:T(8,128)(2,1)S(1)}, bf16[2,8,128,128]{3,2,1,0:T(8,128)(2,1)S(1)}, u32[]{:S(2)}, u32[]{:S(2)}) collective-permute-start(bf16[2,8,128,128]{3,2,1,0:T(8,128)(2,1)S(1)} %get-tuple-element.59.pair.refs_0_), channel_id=1, source_target_pairs={{0,24},{4,28},{8,0},{12,4},{16,8},{20,12},{24,16},{28,20},{32,56},... | collective-permute-start | bytes 1572872 | tf_op jit(solution)/shard_map/ppermute | solution.py:668
  110.6 8.8 %collective-permute-start.20 = (bf16[8,128,128]{2,1,0:T(8,128)(2,1)S(1)}, bf16[8,128,128]{2,1,0:T(8,128)(2,1)S(1)}, u32[]{:S(2)}, u32[]{:S(2)}) collective-permute-start(bf16[8,128,128]{2,1,0:T(8,128)(2,1)S(1)} %slice_bitcast_fusion.1), channel_id=1, source_target_pairs={{0,8},{4,12},{8,16},{12,20},{16,24},{20,28},{24,0},{28,4},{32,40},... | collective-permute-start | bytes 786440 | tf_op jit(solution)/shard_map/ppermute | solution.py:668
  113.0 7.9 %collective-permute-start.22 = (bf16[8,128,128]{2,1,0:T(8,128)(2,1)S(1)}, bf16[8,128,128]{2,1,0:T(8,128)(2,1)S(1)}, u32[]{:S(2)}, u32[]{:S(2)}) collective-permute-start(bf16[8,128,128]{2,1,0:T(8,128)(2,1)S(1)} %slice_bitcast_fusion), channel_id=1, source_target_pairs={{0,24},{4,28},{8,0},{12,4},{16,8},{20,12},{24,16},{28,20},{32,56},... | collective-permute-start | bytes 786440 | tf_op jit(solution)/shard_map/ppermute | solution.py:668
  127.3 6.2 %collective-permute-start.25 = (bf16[256,128]{1,0:T(8,128)(2,1)S(1)}, bf16[256,128]{1,0:T(8,128)(2,1)S(1)}, u32[]{:S(2)}, u32[]{:S(2)}) collective-permute-start(bf16[256,128]{1,0:T(8,128)(2,1)S(1)} %get-tuple-element.78), channel_id=1, source_target_pairs={{0,64},{4,68},{8,72},{12,76},{16,80},{20,84},{24,88},{28,92},{32,9... | collective-permute-start | bytes 196616 | tf_op jit(solution)/shard_map/ppermute | solution.py:664
  (23 other events, 158.3 us)

commit v3 on v2

--- a/solution.py
+++ b/solution.py
@@ -226,8 +226,8 @@
 
     def load(step, _):
         g, side = step // 2, step % 2
-        rows = pl.ds(pl.multiple_of(g * 16, 16), 16)
-        lanes = pl.ds(pl.multiple_of(side * half, half), half)
+        rows = slice(g * 16, g * 16 + 16)
+        lanes = slice(side * half, side * half + half)
         values = []
         for r in range(CTX):
             v = received[r, rows, lanes].astype(f32)
@@ -238,15 +238,16 @@
             a, b = spectrum[k]
             c, s = twist[0, pl.ds(k, 1), lanes], twist[1, pl.ds(k, 1), lanes]
             re, im = a * c + b * s, b * c - a * s
-            at = pl.ds(pl.multiple_of(g * (CTX * 16) + k * 16, 16), 16)
+            at = slice(g * (CTX * 16) + k * 16, g * (CTX * 16) + k * 16 + 16)
             for value, start in ((re, 0), (im, ROWS)):
                 h, l = split(value)
-                cols = pl.ds(pl.multiple_of(start + side * half, half), half)
+                cols = slice(start + side * half, start + side * half + half)
                 high[at, cols] = h
                 low[at, cols] = l
         return 0
 
-    lax.fori_loop(0, 2 * blocks, load, 0)
+    for step in range(2 * blocks):
+        load(step, 0)
 
     table_copy.wait()
     table[:ROWS, :ROWS] = short[:, :ROWS]
@@ -258,7 +259,7 @@
         h, l = high[rows, :], low[rows, :]
         return dot(h, table[...]) + dot(l, table[...])
 
-    piece = 128
+    piece = 512
     for part in range(CTX * PER // piece):
         rows = slice(part * piece, (part + 1) * piece)
         filter_rows = slice(CTX * PER + part * piece, CTX * PER + (part + 1) * piece)
@@ -274,8 +275,8 @@
         mid[rows, :] = transform(rows)
 
     def store(side, _):
-        lanes = pl.ds(pl.multiple_of(side * half, half), half)
-        other = pl.ds(pl.multiple_of(ROWS + side * half, half), half)
+        lanes = slice(side * half, side * half + half)
+        other = slice(ROWS + side * half, ROWS + side * half + half)
         values = []
         for k in range(CTX):
             a, b = mid[k * PER : (k + 1) * PER, lanes], mid[k * PER : (k + 1) * PER, other]
@@ -288,7 +289,8 @@
             out[r, :, lanes] = ((a * c - b * s) * (1.0 / SPAN)).astype(bf16)
         return 0
 
-    lax.fori_loop(0, 2, store, 0)
+    for side in range(2):
+        store(side, 0)
 
 
 def convolve(received):
@@ -716,7 +718,8 @@
     partial = project((1, 3), (h1, h3), gain, weight, partial)
     blocks = project((2,), h2, gain, weight, partial, turns)
 
-    arrived = [blocks[0]] + [along_z(blocks[k], k) for k in (1, 2, 3)]
+    far_z, near_z, last_z = [along_z(blocks[k], k) for k in (2, 1, 3)]
+    arrived = [blocks[0], near_z, far_z, last_z]
     own, pair = sort_blocks(arrived)
 
     pair1, pair3 = along_y(pair, 1), along_y(pair, 3)

time: 136 us -> 134 us (0.985)
  no operation moved by 1% of the time
where the time goes in v3:
time: 134 us
  waiting for transfers between devices  45.5 us (34%)
  starting transfers between devices  41.9 us (31%)
  Pallas kernels  36.6 us (27%)
  local copies, waits for them, and re-layouts  8.03 us (6%)
    ppermute x11, waiting for transfers between devices, along_x(): return lax.ppermute(value, 'tp', [(i, (i + by) % 4) for i in range(4)])  16.7 us
    ppermute x11, starting transfers between devices, along_x(): return lax.ppermute(value, 'tp', [(i, (i + by) % 4) for i in range(4)])  11.9 us
    ppermute x6, waiting for transfers between devices, along_z(): lax.ppermute(value, 'ctx', [(i, (i + 8 * by) % CTX) for i in range(CTX)])  9.99 us
    pallas_call x2, Pallas kernels, attend_more(): pl.pallas_call(functools.partial(more_kernel, steps, False), out_shape=ST...  8.78 us
    ppermute x6, starting transfers between devices, along_z(): lax.ppermute(value, 'ctx', [(i, (i + 8 * by) % CTX) for i in range(CTX)])  8.44 us
    all_to_all x1, starting transfers between devices, body(): received = lax.all_to_all(send, 'ctx', 0, 0, tiled=True)  8.33 us
    unnamed x36, local copies, waits for them, and re-layouts  7.94 us
    all_to_all x1, starting transfers between devices, body(): returned = lax.all_to_all(convolve(received), 'ctx', 0, 0, tiled=True)  6.33 us
  transfers between devices with their start and end apart: 29, of which 19 were waited for; matrix products, arithmetic and copies ran while one was open for 1% of the time, Pallas kernels for 18%

profile of v3, /device:TPU:30, one launch (start us, length us, event | category | flops | bytes accessed | tf_op | source)
XLA Modules:
  0.0 133.8 jit_solution(11078854742959938542)
XLA Ops:
  6.0 2.0 %collective-permute-start = (bf16[16,3072]{1,0:T(8,128)(2,1)S(1)}, bf16[16,3072]{1,0:T(8,128)(2,1)S(1)}, u32[]{:S(2)}, u32[]{:S(2)}) collective-permute-start(bf16[16,3072]{1,0:T(8,128)(2,1)S(1)} %get-tuple-element.41), channel_id=1, source_target_pairs={{0,4},{4,8},{8,12},{12,16},{16,20},{20,24},{24,28},{28,32},{32,36}... | collective-permute-start | bytes 294920 | tf_op jit(solution)/shard_map/ppermute | solution.py:682
  8.1 2.7 %own_features.1.own = bf16[3,256,512]{2,1,0:T(8,128)(2,1)S(1)} custom-call(bf16[256,3072]{1,0:T(8,128)(2,1)S(1)} %get-tuple-element.42.scaled_rows, f32[256,1]{1,0:T(8,128)S(1)} %get-tuple-element.43.squares, bf16[3,3072,512]{2,1,0:T(8,128)(2,1)S(1)} %bitcast.18), custom_call_target="tpu_custom_call" | custom-call | flops 8000000000 | bytes 12000000 | tf_op jit(solution)/shard_map/own_features/pallas_call | solution.py:97
  12.1 4.0 %features.1 = (bf16[32,32,256]{2,1,0:T(8,128)(2,1)}, f32[256,512]{1,0:T(8,128)S(1)}, bf16[256,768]{1,0:T(8,128)(2,1)}, bf16[256,768]{1,0:T(8,128)(2,1)S(1)}, bf16[256,768]{1,0:T(8,128)(2,1)}) custom-call(bf16[16,3072]{1,0:T(8,128)(2,1)S(1)} %collective-permute-done.edge_before, bf16[3,256,512]{2,1,0:T(8,128)(2,1)S(1)} %own_features.1.own, ...), custom_call_target="tpu_custom_call" | custom-call | flops 8000000000 | bytes 14000000 | tf_op jit(solution)/shard_map/features/pallas_call | solution.py:150
  16.1 8.3 %all-to-all-start = ((bf16[32,32,256]{2,1,0:T(8,128)(2,1)}), bf16[32,32,256]{2,1,0:T(8,128)(2,1)S(1)}, u32[]{:S(2)}, u32[]{:S(2)}) async-start(bf16[32,32,256]{2,1,0:T(8,128)(2,1)} %get-tuple-element.44), calls=%async_computation | async-start | bytes 1048576 | tf_op jit(solution)/shard_map/all_to_all | solution.py:696
  27.9 5.9 %all-to-all-done.received = bf16[32,32,256]{2,1,0:T(8,128)(2,1)S(1)} async-done(((bf16[32,32,256]{2,1,0:T(8,128)(2,1)}), bf16[32,32,256]{2,1,0:T(8,128)(2,1)S(1)}, u32[]{:S(2)}, u32[]{:S(2)}) %all-to-all-start) | async-done | bytes 524320 | tf_op jit(solution)/shard_map/all_to_all | solution.py:696
  33.8 4.3 %convolve.1 = bf16[32,16,256]{2,1,0:T(8,128)(2,1)} custom-call(bf16[32,32,256]{2,1,0:T(8,128)(2,1)S(1)} %all-to-all-done.received, f32[2,32,256]{2,1,0:T(8,128)S(1)} %copy-done.3, bf16[256,512]{1,0:T(8,128)(2,1)S(1)} %copy-done.1), custom_call_target="tpu_custom_call" | custom-call | flops 1000 | bytes 1000 | tf_op jit(solution)/shard_map/convolve/pallas_call | solution.py:298
  38.2 6.3 %all-to-all-start.1 = ((bf16[32,16,256]{2,1,0:T(8,128)(2,1)}), bf16[32,16,256]{2,1,0:T(8,128)(2,1)S(1)}, u32[]{:S(2)}, u32[]{:S(2)}) async-start(bf16[32,16,256]{2,1,0:T(8,128)(2,1)} %convolve.1), calls=%async_computation.1 | async-start | bytes 524288 | tf_op jit(solution)/shard_map/all_to_all | solution.py:697
  45.7 5.9 %all-to-all-done.1.returned = bf16[32,16,256]{2,1,0:T(8,128)(2,1)S(1)} async-done(((bf16[32,16,256]{2,1,0:T(8,128)(2,1)}), bf16[32,16,256]{2,1,0:T(8,128)(2,1)S(1)}, u32[]{:S(2)}, u32[]{:S(2)}) %all-to-all-start.1) | async-done | bytes 262176 | tf_op jit(solution)/shard_map/all_to_all | solution.py:697
  57.3 3.3 %collective-permute-done.1.refs_0_ = bf16[256,512]{1,0:T(8,128)(2,1)S(1)} collective-permute-done((bf16[256,512]{1,0:T(8,128)(2,1)S(1)}, bf16[256,512]{1,0:T(8,128)(2,1)S(1)}, u32[]{:S(2)}, u32[]{:S(2)}) %collective-permute-start.1) | collective-permute-done | bytes 262176 | tf_op jit(solution)/shard_map/ppermute | solution.py:662
  62.8 1.9 %mix_add.2.partial = f32[256,768]{1,0:T(8,128)S(1)} custom-call(f32[256,768]{1,0:T(8,128)S(1)} %mix_own.1.partial, bf16[256,512]{1,0:T(8,128)(2,1)S(1)} %collective-permute-done.1.refs_0_, bf16[256,512]{1,0:T(8,128)(2,1)S(1)} %collective-permute-done.2.refs_1_, bf16[256,768]{1,0:T(8,128)(2,1)S(1)} %collective-permute-done.3.refs_2_, ...), custom_call_target="tpu_custom_call" | custom-call | flops 2000000000 | bytes 2000000 | tf_op jit(solution)/shard_map/mix_add/pallas_call | solution.py:374
  65.9 2.8 %collective-permute-done.8.refs_1_ = bf16[128,512]{1,0:T(8,128)(2,1)S(1)} collective-permute-done((bf16[128,512]{1,0:T(8,128)(2,1)S(1)}, bf16[128,512]{1,0:T(8,128)(2,1)S(1)}, u32[]{:S(2)}, u32[]{:S(2)}) %collective-permute-start.8) | collective-permute-done | bytes 131104 | tf_op jit(solution)/shard_map/ppermute | solution.py:662
  75.0 4.4 %collective-permute-done.11.refs_0_ = bf16[256,768]{1,0:T(8,128)(2,1)S(1)} collective-permute-done((bf16[256,768]{1,0:T(8,128)(2,1)}, bf16[256,768]{1,0:T(8,128)(2,1)S(1)}, u32[]{:S(2)}, u32[]{:S(2)}) %collective-permute-start.11) | collective-permute-done | bytes 393248 | tf_op jit(solution)/shard_map/ppermute | solution.py:662
  79.4 2.0 %collective-permute-start.12 = (bf16[128,768]{1,0:T(8,128)(2,1)S(1)}, bf16[128,768]{1,0:T(8,128)(2,1)S(1)}, u32[]{:S(2)}, u32[]{:S(2)}) collective-permute-start(bf16[128,768]{1,0:T(8,128)(2,1)S(1)} %slice.26), channel_id=1, source_target_pairs={{0,1},{1,2},{2,3},{3,0},{4,5},{5,6},{6,7},{7,4},{8,9},{9,10},{10,1... | collective-permute-start | bytes 589832 | tf_op jit(solution)/shard_map/ppermute | solution.py:662
  81.6 2.6 %project.4 = (f32[3,256,512]{2,1,0:T(8,128)S(1)}, f32[256,1]{1,0:T(8,128)S(1)}) custom-call(bf16[256,768]{1,0:T(8,128)(2,1)S(1)} %collective-permute-done.11.refs_0_, bf16[256,768]{1,0:T(8,128)(2,1)S(1)} %collective-permute-done.13.refs_1_, f32[1,3072]{1,0:T(1,128)S(1)} %bitcast.16, bf16[3,3072,512]{2,1,0:T(8,128)(2,1)S(1)} %bitcast.13, ...), custom_call_target="tpu_custom_call" | custom-call | flops 3000000000 | bytes 8000000 | tf_op jit(solution)/shard_map/project/pallas_call | solution.py:453
  85.2 3.2 %collective-permute-done.14.refs_1_ = bf16[128,768]{1,0:T(8,128)(2,1)S(1)} collective-permute-done((bf16[128,768]{1,0:T(8,128)(2,1)S(1)}, bf16[128,768]{1,0:T(8,128)(2,1)S(1)}, u32[]{:S(2)}, u32[]{:S(2)}) %collective-permute-start.14) | collective-permute-done | bytes 196640 | tf_op jit(solution)/shard_map/ppermute | solution.py:662
  88.4 1.9 %project.5 = (bf16[6,128,128]{2,1,0:T(8,128)(2,1)S(1)}, bf16[6,128,128]{2,1,0:T(8,128)(2,1)S(1)}, bf16[6,128,128]{2,1,0:T(8,128)(2,1)S(1)}, bf16[6,128,128]{2,1,0:T(8,128)(2,1)S(1)}) custom-call(bf16[128,768]{1,0:T(8,128)(2,1)S(1)} %collective-permute-done.12.refs_0_, bf16[128,768]{1,0:T(8,128)(2,1)S(1)} %collective-permute-done.14.refs_1_, ...), custom_call_target="tpu_custom_call" | custom-call | flops 1500000000 | bytes 4000000 | tf_op jit(solution)/shard_map/project/pallas_call | solution.py:453
  90.9 1.9 %collective-permute-start.16 = (bf16[6,128,128]{2,1,0:T(8,128)(2,1)S(1)}, bf16[6,128,128]{2,1,0:T(8,128)(2,1)S(1)}, u32[]{:S(2)}, u32[]{:S(2)}) collective-permute-start(bf16[6,128,128]{2,1,0:T(8,128)(2,1)S(1)} %get-tuple-element.56), channel_id=1, source_target_pairs={{0,64},{4,68},{8,72},{12,76},{16,80},{20,84},{24,88},{28,92},{32,9... | collective-permute-start | bytes 589832 | tf_op jit(solution)/shard_map/ppermute | solution.py:666
  93.7 5.7 %collective-permute-done.15.a1 = bf16[6,128,128]{2,1,0:T(8,128)(2,1)S(1)} collective-permute-done((bf16[6,128,128]{2,1,0:T(8,128)(2,1)S(1)}, bf16[6,128,128]{2,1,0:T(8,128)(2,1)S(1)}, u32[]{:S(2)}, u32[]{:S(2)}) %collective-permute-start.15) | collective-permute-done | bytes 196640 | tf_op jit(solution)/shard_map/ppermute | solution.py:666
  105.8 2.7 %attend_more.2 = (f32[4,1,512]{2,1,0:T(1,128)S(1)}, f32[4,1,512]{2,1,0:T(1,128)S(1)}, f32[4,128,512]{2,1,0:T(8,128)S(1)}) custom-call(bf16[4,128,256]{2,1,0:T(8,128)(2,1)S(1)} %get-tuple-element.63.own, bf16[4,128,256]{2,1,0:T(8,128)(2,1)S(1)} %collective-permute-done.18.other, bf16[2,8,128,128]{3,2,1,0:T(8,128)(2,1)S(1)} %get-tuple-element.59.pair.refs_0_, ...), custom_call_target="tpu_custom_call" | custom-call | flops 1000 | bytes 1000 | tf_op jit(solution)/shard_map/attend_more/pallas_call | solution.py:591
  109.7 2.2 %collective-permute-start.20 = (bf16[8,128,128]{2,1,0:T(8,128)(2,1)S(1)}, bf16[8,128,128]{2,1,0:T(8,128)(2,1)S(1)}, u32[]{:S(2)}, u32[]{:S(2)}) collective-permute-start(bf16[8,128,128]{2,1,0:T(8,128)(2,1)S(1)} %slice_bitcast_fusion.1), channel_id=1, source_target_pairs={{0,8},{4,12},{8,16},{12,20},{16,24},{20,28},{24,0},{28,4},{32,40},... | collective-permute-start | bytes 786440 | tf_op jit(solution)/shard_map/ppermute | solution.py:670
  112.0 6.1 %attend_more.3 = (f32[4,1,512]{2,1,0:T(1,128)S(1)}, f32[4,1,512]{2,1,0:T(1,128)S(1)}, f32[4,128,512]{2,1,0:T(8,128)S(1)}) custom-call(bf16[4,128,256]{2,1,0:T(8,128)(2,1)S(1)} %get-tuple-element.63.own, bf16[4,128,256]{2,1,0:T(8,128)(2,1)S(1)} %collective-permute-done.18.other, bf16[2,8,128,128]{3,2,1,0:T(8,128)(2,1)S(1)} %collective-permute-done.19.refs_0_, ...), custom_call_target="tpu_custom_call" | custom-call | flops 8000000000 | bytes 1000 | tf_op jit(solution)/shard_map/attend_more/pallas_call | solution.py:591
  119.6 3.1 %attend_last.1 = (f32[4,128,256]{2,1,0:T(8,128)S(1)}, f32[4,1,256]{2,1,0:T(1,128)S(1)}, bf16[4,144,256]{2,1,0:T(8,128)(2,1)S(1)}) custom-call(bf16[4,128,256]{2,1,0:T(8,128)(2,1)S(1)} %get-tuple-element.63.own, bf16[4,128,256]{2,1,0:T(8,128)(2,1)S(1)} %collective-permute-done.18.other, bf16[8,128,128]{2,1,0:T(8,128)(2,1)S(1)} %collective-permute-done.20.refs_0_, ...), custom_call_target="tpu_custom_call" | custom-call | flops 4000000000 | bytes 3000000 | tf_op jit(solution)/shard_map/attend_last/pallas_call | solution.py:603
  126.2 2.5 %collective-permute-start.25 = (bf16[256,128]{1,0:T(8,128)(2,1)S(1)}, bf16[256,128]{1,0:T(8,128)(2,1)S(1)}, u32[]{:S(2)}, u32[]{:S(2)}) collective-permute-start(bf16[256,128]{1,0:T(8,128)(2,1)S(1)} %get-tuple-element.78), channel_id=1, source_target_pairs={{0,64},{4,68},{8,72},{12,76},{16,80},{20,84},{24,88},{28,92},{32,9... | collective-permute-start | bytes 196616 | tf_op jit(solution)/shard_map/ppermute | solution.py:666
  130.1 2.2 %collective-permute-done.25.a2 = bf16[256,128]{1,0:T(8,128)(2,1)S(1)} collective-permute-done((bf16[256,128]{1,0:T(8,128)(2,1)S(1)}, bf16[256,128]{1,0:T(8,128)(2,1)S(1)}, u32[]{:S(2)}, u32[]{:S(2)}) %collective-permute-start.25) | collective-permute-done | bytes 65568 | tf_op jit(solution)/shard_map/ppermute | solution.py:666
  (99 shorter events, 44.8 us)
Async XLA Ops:
  6.0 6.1 %collective-permute-start = (bf16[16,3072]{1,0:T(8,128)(2,1)S(1)}, bf16[16,3072]{1,0:T(8,128)(2,1)S(1)}, u32[]{:S(2)}, u32[]{:S(2)}) collective-permute-start(bf16[16,3072]{1,0:T(8,128)(2,1)S(1)} %get-tuple-element.41), channel_id=1, source_target_pairs={{0,4},{4,8},{8,12},{12,16},{16,20},{20,24},{24,28},{28,32},{32,36}... | collective-permute-start | bytes 294920 | tf_op jit(solution)/shard_map/ppermute | solution.py:682
  16.1 17.7 %all-to-all-start = ((bf16[32,32,256]{2,1,0:T(8,128)(2,1)}), bf16[32,32,256]{2,1,0:T(8,128)(2,1)S(1)}, u32[]{:S(2)}, u32[]{:S(2)}) async-start(bf16[32,32,256]{2,1,0:T(8,128)(2,1)} %get-tuple-element.44), calls=%async_computation | async-start | bytes 1048576 | tf_op jit(solution)/shard_map/all_to_all | solution.py:696
  24.5 20.1 %collective-permute-start.3 = (bf16[256,768]{1,0:T(8,128)(2,1)}, bf16[256,768]{1,0:T(8,128)(2,1)S(1)}, u32[]{:S(2)}, u32[]{:S(2)}) collective-permute-start(bf16[256,768]{1,0:T(8,128)(2,1)} %get-tuple-element.47), channel_id=1, source_target_pairs={{0,1},{1,2},{2,3},{3,0},{4,5},{5,6},{6,7},{7,4},{8,9},{9,10},{10,1... | collective-permute-start | bytes 1179656 | tf_op jit(solution)/shard_map/ppermute | solution.py:662
  25.0 20.7 %collective-permute-start.4 = (bf16[256,768]{1,0:T(8,128)(2,1)}, bf16[256,768]{1,0:T(8,128)(2,1)S(1)}, u32[]{:S(2)}, u32[]{:S(2)}) collective-permute-start(bf16[256,768]{1,0:T(8,128)(2,1)} %get-tuple-element.48), channel_id=1, source_target_pairs={{0,3},{1,0},{2,1},{3,2},{4,7},{5,4},{6,5},{7,6},{8,11},{9,8},{10,9... | collective-permute-start | bytes 1179656 | tf_op jit(solution)/shard_map/ppermute | solution.py:662
  26.5 27.3 %collective-permute-start.9 = (bf16[256,768]{1,0:T(8,128)(2,1)S(1)}, bf16[256,768]{1,0:T(8,128)(2,1)S(1)}, u32[]{:S(2)}, u32[]{:S(2)}) collective-permute-start(bf16[256,768]{1,0:T(8,128)(2,1)S(1)} %get-tuple-element.49), channel_id=1, source_target_pairs={{0,2},{1,3},{2,0},{3,1},{4,6},{5,7},{6,4},{7,5},{8,10},{9,11},{10,... | collective-permute-start | bytes 1179656 | tf_op jit(solution)/shard_map/ppermute | solution.py:662
  38.2 13.4 %all-to-all-start.1 = ((bf16[32,16,256]{2,1,0:T(8,128)(2,1)}), bf16[32,16,256]{2,1,0:T(8,128)(2,1)S(1)}, u32[]{:S(2)}, u32[]{:S(2)}) async-start(bf16[32,16,256]{2,1,0:T(8,128)(2,1)} %convolve.1), calls=%async_computation.1 | async-start | bytes 524288 | tf_op jit(solution)/shard_map/all_to_all | solution.py:697
  44.5 18.3 %collective-permute-start.5 = (bf16[256,768]{1,0:T(8,128)(2,1)S(1)}, bf16[256,768]{1,0:T(8,128)(2,1)}, u32[]{:S(2)}, u32[]{:S(2)}) collective-permute-start(bf16[256,768]{1,0:T(8,128)(2,1)S(1)} %collective-permute-done.3.refs_2_), channel_id=1, source_target_pairs={{0,4},{4,0},{8,12},{12,8},{16,20},{20,16},{24,28},{28,24},{32,36},... | collective-permute-start | bytes 1179656 | tf_op jit(solution)/shard_map/ppermute | solution.py:674
  45.7 17.1 %collective-permute-start.6 = (bf16[256,768]{1,0:T(8,128)(2,1)S(1)}, bf16[256,768]{1,0:T(8,128)(2,1)}, u32[]{:S(2)}, u32[]{:S(2)}) collective-permute-start(bf16[256,768]{1,0:T(8,128)(2,1)S(1)} %collective-permute-done.4.refs_3_), channel_id=1, source_target_pairs={{0,4},{4,0},{8,12},{12,8},{16,20},{20,16},{24,28},{28,24},{32,36},... | collective-permute-start | bytes 1179656 | tf_op jit(solution)/shard_map/ppermute | solution.py:674
  51.8 8.9 %collective-permute-start.1 = (bf16[256,512]{1,0:T(8,128)(2,1)S(1)}, bf16[256,512]{1,0:T(8,128)(2,1)S(1)}, u32[]{:S(2)}, u32[]{:S(2)}) collective-permute-start(bf16[256,512]{1,0:T(8,128)(2,1)S(1)} %gate.1.gated), channel_id=1, source_target_pairs={{0,1},{1,2},{2,3},{3,0},{4,5},{5,6},{6,7},{7,4},{8,9},{9,10},{10,1... | collective-permute-start | bytes 786440 | tf_op jit(solution)/shard_map/ppermute | solution.py:662
  52.3 10.1 %collective-permute-start.2 = (bf16[256,512]{1,0:T(8,128)(2,1)S(1)}, bf16[256,512]{1,0:T(8,128)(2,1)S(1)}, u32[]{:S(2)}, u32[]{:S(2)}) collective-permute-start(bf16[256,512]{1,0:T(8,128)(2,1)S(1)} %gate.1.gated), channel_id=1, source_target_pairs={{0,3},{1,0},{2,1},{3,2},{4,7},{5,4},{6,5},{7,6},{8,11},{9,8},{10,9... | collective-permute-start | bytes 786440 | tf_op jit(solution)/shard_map/ppermute | solution.py:662
  53.9 10.9 %collective-permute-start.10 = (bf16[256,768]{1,0:T(8,128)(2,1)S(1)}, bf16[256,768]{1,0:T(8,128)(2,1)S(1)}, u32[]{:S(2)}, u32[]{:S(2)}) collective-permute-start(bf16[256,768]{1,0:T(8,128)(2,1)S(1)} %collective-permute-done.9.refs_2_), channel_id=1, source_target_pairs={{0,4},{4,0},{8,12},{12,8},{16,20},{20,16},{24,28},{28,24},{32,36},... | collective-permute-start | bytes 1179656 | tf_op jit(solution)/shard_map/ppermute | solution.py:674
  62.4 6.2 %collective-permute-start.8 = (bf16[128,512]{1,0:T(8,128)(2,1)S(1)}, bf16[128,512]{1,0:T(8,128)(2,1)S(1)}, u32[]{:S(2)}, u32[]{:S(2)}) collective-permute-start(bf16[128,512]{1,0:T(8,128)(2,1)S(1)} %slice.25), channel_id=1, source_target_pairs={{0,3},{1,0},{2,1},{3,2},{4,7},{5,4},{6,5},{7,6},{8,11},{9,8},{10,9... | collective-permute-start | bytes 393224 | tf_op jit(solution)/shard_map/ppermute | solution.py:662
  69.8 9.6 %collective-permute-start.11 = (bf16[256,768]{1,0:T(8,128)(2,1)}, bf16[256,768]{1,0:T(8,128)(2,1)S(1)}, u32[]{:S(2)}, u32[]{:S(2)}) collective-permute-start(bf16[256,768]{1,0:T(8,128)(2,1)} %mix_add.3.refs_0_), channel_id=1, source_target_pairs={{0,1},{1,2},{2,3},{3,0},{4,5},{5,6},{6,7},{7,4},{8,9},{9,10},{10,1... | collective-permute-start | bytes 1179656 | tf_op jit(solution)/shard_map/ppermute | solution.py:662
  69.9 11.5 %collective-permute-start.13 = (bf16[256,768]{1,0:T(8,128)(2,1)}, bf16[256,768]{1,0:T(8,128)(2,1)S(1)}, u32[]{:S(2)}, u32[]{:S(2)}) collective-permute-start(bf16[256,768]{1,0:T(8,128)(2,1)} %mix_add.3.refs_0_), channel_id=1, source_target_pairs={{0,3},{1,0},{2,1},{3,2},{4,7},{5,4},{6,5},{7,6},{8,11},{9,8},{10,9... | collective-permute-start | bytes 1179656 | tf_op jit(solution)/shard_map/ppermute | solution.py:662
  79.4 5.7 %collective-permute-start.12 = (bf16[128,768]{1,0:T(8,128)(2,1)S(1)}, bf16[128,768]{1,0:T(8,128)(2,1)S(1)}, u32[]{:S(2)}, u32[]{:S(2)}) collective-permute-start(bf16[128,768]{1,0:T(8,128)(2,1)S(1)} %slice.26), channel_id=1, source_target_pairs={{0,1},{1,2},{2,3},{3,0},{4,5},{5,6},{6,7},{7,4},{8,9},{9,10},{10,1... | collective-permute-start | bytes 589832 | tf_op jit(solution)/shard_map/ppermute | solution.py:662
  81.4 6.9 %collective-permute-start.14 = (bf16[128,768]{1,0:T(8,128)(2,1)S(1)}, bf16[128,768]{1,0:T(8,128)(2,1)S(1)}, u32[]{:S(2)}, u32[]{:S(2)}) collective-permute-start(bf16[128,768]{1,0:T(8,128)(2,1)S(1)} %slice.27), channel_id=1, source_target_pairs={{0,3},{1,0},{2,1},{3,2},{4,7},{5,4},{6,5},{7,6},{8,11},{9,8},{10,9... | collective-permute-start | bytes 589832 | tf_op jit(solution)/shard_map/ppermute | solution.py:662
  90.3 9.1 %collective-permute-start.15 = (bf16[6,128,128]{2,1,0:T(8,128)(2,1)S(1)}, bf16[6,128,128]{2,1,0:T(8,128)(2,1)S(1)}, u32[]{:S(2)}, u32[]{:S(2)}) collective-permute-start(bf16[6,128,128]{2,1,0:T(8,128)(2,1)S(1)} %get-tuple-element.55), channel_id=1, source_target_pairs={{0,32},{4,36},{8,40},{12,44},{16,48},{20,52},{24,56},{28,60},{32,6... | collective-permute-start | bytes 589832 | tf_op jit(solution)/shard_map/ppermute | solution.py:666
  90.9 8.5 %collective-permute-start.16 = (bf16[6,128,128]{2,1,0:T(8,128)(2,1)S(1)}, bf16[6,128,128]{2,1,0:T(8,128)(2,1)S(1)}, u32[]{:S(2)}, u32[]{:S(2)}) collective-permute-start(bf16[6,128,128]{2,1,0:T(8,128)(2,1)S(1)} %get-tuple-element.56), channel_id=1, source_target_pairs={{0,64},{4,68},{8,72},{12,76},{16,80},{20,84},{24,88},{28,92},{32,9... | collective-permute-start | bytes 589832 | tf_op jit(solution)/shard_map/ppermute | solution.py:666
  92.8 7.4 %collective-permute-start.17 = (bf16[6,128,128]{2,1,0:T(8,128)(2,1)S(1)}, bf16[6,128,128]{2,1,0:T(8,128)(2,1)S(1)}, u32[]{:S(2)}, u32[]{:S(2)}) collective-permute-start(bf16[6,128,128]{2,1,0:T(8,128)(2,1)S(1)} %get-tuple-element.57), channel_id=1, source_target_pairs={{0,96},{4,100},{8,104},{12,108},{16,112},{20,116},{24,120},{28,124... | collective-permute-start | bytes 589832 | tf_op jit(solution)/shard_map/ppermute | solution.py:666
  100.3 9.3 %collective-permute-start.19 = (bf16[2,8,128,128]{3,2,1,0:T(8,128)(2,1)S(1)}, bf16[2,8,128,128]{3,2,1,0:T(8,128)(2,1)S(1)}, u32[]{:S(2)}, u32[]{:S(2)}) collective-permute-start(bf16[2,8,128,128]{3,2,1,0:T(8,128)(2,1)S(1)} %get-tuple-element.59.pair.refs_0_), channel_id=1, source_target_pairs={{0,8},{4,12},{8,16},{12,20},{16,24},{20,28},{24,0},{28,4},{32,40},... | collective-permute-start | bytes 1572872 | tf_op jit(solution)/shard_map/ppermute | solution.py:670
  101.4 10.5 %collective-permute-start.21 = (bf16[2,8,128,128]{3,2,1,0:T(8,128)(2,1)S(1)}, bf16[2,8,128,128]{3,2,1,0:T(8,128)(2,1)S(1)}, u32[]{:S(2)}, u32[]{:S(2)}) collective-permute-start(bf16[2,8,128,128]{3,2,1,0:T(8,128)(2,1)S(1)} %get-tuple-element.59.pair.refs_0_), channel_id=1, source_target_pairs={{0,24},{4,28},{8,0},{12,4},{16,8},{20,12},{24,16},{28,20},{32,56},... | collective-permute-start | bytes 1572872 | tf_op jit(solution)/shard_map/ppermute | solution.py:670
  109.7 8.4 %collective-permute-start.20 = (bf16[8,128,128]{2,1,0:T(8,128)(2,1)S(1)}, bf16[8,128,128]{2,1,0:T(8,128)(2,1)S(1)}, u32[]{:S(2)}, u32[]{:S(2)}) collective-permute-start(bf16[8,128,128]{2,1,0:T(8,128)(2,1)S(1)} %slice_bitcast_fusion.1), channel_id=1, source_target_pairs={{0,8},{4,12},{8,16},{12,20},{16,24},{20,28},{24,0},{28,4},{32,40},... | collective-permute-start | bytes 786440 | tf_op jit(solution)/shard_map/ppermute | solution.py:670
  111.9 7.7 %collective-permute-start.22 = (bf16[8,128,128]{2,1,0:T(8,128)(2,1)S(1)}, bf16[8,128,128]{2,1,0:T(8,128)(2,1)S(1)}, u32[]{:S(2)}, u32[]{:S(2)}) collective-permute-start(bf16[8,128,128]{2,1,0:T(8,128)(2,1)S(1)} %slice_bitcast_fusion), channel_id=1, source_target_pairs={{0,24},{4,28},{8,0},{12,4},{16,8},{20,12},{24,16},{28,20},{32,56},... | collective-permute-start | bytes 786440 | tf_op jit(solution)/shard_map/ppermute | solution.py:670
  126.2 6.1 %collective-permute-start.25 = (bf16[256,128]{1,0:T(8,128)(2,1)S(1)}, bf16[256,128]{1,0:T(8,128)(2,1)S(1)}, u32[]{:S(2)}, u32[]{:S(2)}) collective-permute-start(bf16[256,128]{1,0:T(8,128)(2,1)S(1)} %get-tuple-element.78), channel_id=1, source_target_pairs={{0,64},{4,68},{8,72},{12,76},{16,80},{20,84},{24,88},{28,92},{32,9... | collective-permute-start | bytes 196616 | tf_op jit(solution)/shard_map/ppermute | solution.py:666
  (23 other events, 157.8 us)

commit v4 on v3

--- a/solution.py
+++ b/solution.py
@@ -87,30 +87,39 @@
     )(ids, table, gain)
 
 
-def product_kernel(scaled_rows, squares, weight, out):
+def product_kernel(scaled_rows, squares, weight, skip, filters, out, lags_out):
+    r = spot()[1]
+    direct = jnp.broadcast_to(skip[...], (128, WIDTH)).T
+    lag = lax.broadcasted_iota(jnp.int32, (WIDTH, 128), 1)
+    first = filters[:, :128] + jnp.where((lag == 0) & (r == 0), direct, 0.0)
+    lags = jnp.concatenate([first, filters[:, 128:]], axis=1)
+    lags_out[...] = lags.astype(bf16).reshape(CTX, PER, ROWS)
     scale = lax.rsqrt(squares[...] * (1.0 / D) + epsilon)
     for i in range(3):
         out[i] = (dot(scaled_rows[...], weight[i]) * scale).astype(bf16)
 
 
-def own_features(scaled_rows, squares, weight):
+def own_features(scaled_rows, squares, weight, skip, filters):
     return pl.pallas_call(
         product_kernel,
-        out_shape=jax.ShapeDtypeStruct((3, ROWS, WIDTH), bf16),
-        in_specs=[VMEM] * 3,
-        out_specs=VMEM,
+        out_shape=(
+            jax.ShapeDtypeStruct((3, ROWS, WIDTH), bf16),
+            jax.ShapeDtypeStruct((CTX, PER, ROWS), bf16),
+        ),
+        in_specs=[VMEM] * 5,
+        out_specs=(VMEM, VMEM),
         compiler_params=params(34),
         cost_estimate=cost(8_000_000_000, 12_000_000),
         name="own_features",
-    )(scaled_rows, squares, weight)
+    )(scaled_rows, squares, weight, skip, filters)
 
 
 def feature_kernel(
-    edge_before, own, taps, skip, filters, weight, mix_hbm,
+    edge_before, own, taps, lags, weight, mix_hbm,
     send, mixed0, cut1, cut2, cut3,
     cut, cut_sem, out_sem,
 ):
-    x, r, _, _, core = spot()
+    x, _, _, _, core = spot()
 
     def cut_copy(k):
         rows = pl.ds(pl.multiple_of(core * (WIDTH // 2), WIDTH // 2), WIDTH // 2)
@@ -119,11 +128,7 @@
 
     for k in (1, 2, 3):
         cut_copy(k).start()
-    direct = jnp.broadcast_to(skip[...], (128, WIDTH)).T
-    lag = lax.broadcasted_iota(jnp.int32, (WIDTH, 128), 1)
-    first = filters[:, :128] + jnp.where((lag == 0) & (r == 0), direct, 0.0)
-    lags = jnp.concatenate([first, filters[:, 128:]], axis=1)
-    send[:, PER:, :] = lags.astype(bf16).reshape(CTX, PER, ROWS)
+    send[:, PER:, :] = lags[...]
     edge = [dot(edge_before[...], weight[i]).astype(bf16) for i in range(3)]
     outs = [
         pltpu.make_async_copy(cut.at[n], out, out_sem.at[n])
@@ -145,7 +150,7 @@
         copy.wait()
 
 
-def features(edge_before, own, taps, skip, filters, weight, mix_weight):
+def features(edge_before, own, taps, lags, weight, mix_weight):
     cut = jax.ShapeDtypeStruct((WIDTH // 2, SHARE), bf16)
     return pl.pallas_call(
         feature_kernel,
@@ -156,7 +161,7 @@
             cut,
             cut,
         ),
-        in_specs=[VMEM] * 6 + [HBM],
+        in_specs=[VMEM] * 5 + [HBM],
         out_specs=(VMEM,) * 2 + (HBM,) * 3,
         scratch_shapes=[
             pltpu.VMEM((3, WIDTH // 2, SHARE), bf16),
@@ -166,7 +171,7 @@
         compiler_params=params(34),
         cost_estimate=cost(8_000_000_000, 14_000_000),
         name="features",
-    )(edge_before, own, taps, skip, filters, weight, mix_weight)
+    )(edge_before, own, taps, lags, weight, mix_weight)
 
 
 def unit(turn):
@@ -681,13 +686,14 @@
     scaled_rows, squares, share, edge = embed(token_ids[None, :], embed_table, gain_first[None, :])
     edge_before = lax.ppermute(edge, "ctx", [(i, i + 1) for i in range(CTX - 1)])
     feat_parts = feat_weight.transpose(1, 0, 2)
-    own_parts = own_features(scaled_rows, squares, feat_parts)
+    own_parts, lags = own_features(
+        scaled_rows, squares, feat_parts, skip_gain[None, :], long_filter
+    )
     send, mixed0, *cuts = features(
         edge_before,
         own_parts,
         short_taps,
-        skip_gain[None, :],
-        long_filter,
+        lags,
         feat_parts,
         mix_weight,
     )

time: 134 us -> 134 us (level)
  no operation moved by 1% of the time
where the time goes in v4:
time: 134 us
  waiting for transfers between devices  45.6 us (34%)
  starting transfers between devices  42 us (31%)
  Pallas kernels  36.5 us (27%)
  local copies, waits for them, and re-layouts  8.02 us (6%)
    ppermute x11, waiting for transfers between devices, along_x(): return lax.ppermute(value, 'tp', [(i, (i + by) % 4) for i in range(4)])  16.8 us
    ppermute x11, starting transfers between devices, along_x(): return lax.ppermute(value, 'tp', [(i, (i + by) % 4) for i in range(4)])  11.9 us
    ppermute x6, waiting for transfers between devices, along_z(): lax.ppermute(value, 'ctx', [(i, (i + 8 * by) % CTX) for i in range(CTX)])  10 us
    pallas_call x2, Pallas kernels, attend_more(): pl.pallas_call(functools.partial(more_kernel, steps, False), out_shape=ST...  8.78 us
    ppermute x6, starting transfers between devices, along_z(): lax.ppermute(value, 'ctx', [(i, (i + 8 * by) % CTX) for i in range(CTX)])  8.42 us
    all_to_all x1, starting transfers between devices, body(): received = lax.all_to_all(send, 'ctx', 0, 0, tiled=True)  8.34 us
    unnamed x36, local copies, waits for them, and re-layouts  7.94 us
    all_to_all x1, starting transfers between devices, body(): returned = lax.all_to_all(convolve(received), 'ctx', 0, 0, tiled=True)  6.33 us
  transfers between devices with their start and end apart: 29, of which 19 were waited for; matrix products, arithmetic and copies ran while one was open for 1% of the time, Pallas kernels for 18%

profile of v4, /device:TPU:30, one launch (start us, length us, event | category | flops | bytes accessed | tf_op | source)
XLA Modules:
  0.0 133.9 jit_solution(11654332500701037482)
XLA Ops:
  6.0 2.2 %collective-permute-start = (bf16[16,3072]{1,0:T(8,128)(2,1)S(1)}, bf16[16,3072]{1,0:T(8,128)(2,1)S(1)}, u32[]{:S(2)}, u32[]{:S(2)}) collective-permute-start(bf16[16,3072]{1,0:T(8,128)(2,1)S(1)} %get-tuple-element.43), channel_id=1, source_target_pairs={{0,4},{4,8},{8,12},{12,16},{16,20},{20,24},{24,28},{28,32},{32,36}... | collective-permute-start | bytes 294920 | tf_op jit(solution)/shard_map/ppermute | solution.py:687
  8.2 2.6 %own_features.1 = (bf16[3,256,512]{2,1,0:T(8,128)(2,1)S(1)}, bf16[32,16,256]{2,1,0:T(8,128)(2,1)S(1)}) custom-call(bf16[256,3072]{1,0:T(8,128)(2,1)S(1)} %get-tuple-element.44.scaled_rows, f32[256,1]{1,0:T(8,128)S(1)} %get-tuple-element.45.squares, bf16[3,3072,512]{2,1,0:T(8,128)(2,1)S(1)} %bitcast.18, f32[1,512]{1,0:T(1,128)S(1)} %bitcast.21, ...), custom_call_target="tpu_custom_call" | custom-call | flops 8000000000 | bytes 12000000 | tf_op jit(solution)/shard_map/own_features/pallas_call | solution.py:103
  12.2 4.0 %features.1 = (bf16[32,32,256]{2,1,0:T(8,128)(2,1)}, f32[256,512]{1,0:T(8,128)S(1)}, bf16[256,768]{1,0:T(8,128)(2,1)}, bf16[256,768]{1,0:T(8,128)(2,1)S(1)}, bf16[256,768]{1,0:T(8,128)(2,1)}) custom-call(bf16[16,3072]{1,0:T(8,128)(2,1)S(1)} %collective-permute-done.edge_before, bf16[3,256,512]{2,1,0:T(8,128)(2,1)S(1)} %get-tuple-element.46.own, ...), custom_call_target="tpu_custom_call" | custom-call | flops 8000000000 | bytes 14000000 | tf_op jit(solution)/shard_map/features/pallas_call | solution.py:155
  16.2 8.3 %all-to-all-start = ((bf16[32,32,256]{2,1,0:T(8,128)(2,1)}), bf16[32,32,256]{2,1,0:T(8,128)(2,1)S(1)}, u32[]{:S(2)}, u32[]{:S(2)}) async-start(bf16[32,32,256]{2,1,0:T(8,128)(2,1)} %get-tuple-element.48), calls=%async_computation | async-start | bytes 1048576 | tf_op jit(solution)/shard_map/all_to_all | solution.py:702
  28.1 5.9 %all-to-all-done.received = bf16[32,32,256]{2,1,0:T(8,128)(2,1)S(1)} async-done(((bf16[32,32,256]{2,1,0:T(8,128)(2,1)}), bf16[32,32,256]{2,1,0:T(8,128)(2,1)S(1)}, u32[]{:S(2)}, u32[]{:S(2)}) %all-to-all-start) | async-done | bytes 524320 | tf_op jit(solution)/shard_map/all_to_all | solution.py:702
  33.9 4.3 %convolve.1 = bf16[32,16,256]{2,1,0:T(8,128)(2,1)} custom-call(bf16[32,32,256]{2,1,0:T(8,128)(2,1)S(1)} %all-to-all-done.received, f32[2,32,256]{2,1,0:T(8,128)S(1)} %copy-done.3, bf16[256,512]{1,0:T(8,128)(2,1)S(1)} %copy-done.1), custom_call_target="tpu_custom_call" | custom-call | flops 1000 | bytes 1000 | tf_op jit(solution)/shard_map/convolve/pallas_call | solution.py:303
  38.3 6.3 %all-to-all-start.1 = ((bf16[32,16,256]{2,1,0:T(8,128)(2,1)}), bf16[32,16,256]{2,1,0:T(8,128)(2,1)S(1)}, u32[]{:S(2)}, u32[]{:S(2)}) async-start(bf16[32,16,256]{2,1,0:T(8,128)(2,1)} %convolve.1), calls=%async_computation.1 | async-start | bytes 524288 | tf_op jit(solution)/shard_map/all_to_all | solution.py:703
  45.9 5.9 %all-to-all-done.1.returned = bf16[32,16,256]{2,1,0:T(8,128)(2,1)S(1)} async-done(((bf16[32,16,256]{2,1,0:T(8,128)(2,1)}), bf16[32,16,256]{2,1,0:T(8,128)(2,1)S(1)}, u32[]{:S(2)}, u32[]{:S(2)}) %all-to-all-start.1) | async-done | bytes 262176 | tf_op jit(solution)/shard_map/all_to_all | solution.py:703
  57.4 3.3 %collective-permute-done.1.refs_0_ = bf16[256,512]{1,0:T(8,128)(2,1)S(1)} collective-permute-done((bf16[256,512]{1,0:T(8,128)(2,1)S(1)}, bf16[256,512]{1,0:T(8,128)(2,1)S(1)}, u32[]{:S(2)}, u32[]{:S(2)}) %collective-permute-start.1) | collective-permute-done | bytes 262176 | tf_op jit(solution)/shard_map/ppermute | solution.py:667
  63.0 1.9 %mix_add.2.partial = f32[256,768]{1,0:T(8,128)S(1)} custom-call(f32[256,768]{1,0:T(8,128)S(1)} %mix_own.1.partial, bf16[256,512]{1,0:T(8,128)(2,1)S(1)} %collective-permute-done.1.refs_0_, bf16[256,512]{1,0:T(8,128)(2,1)S(1)} %collective-permute-done.2.refs_1_, bf16[256,768]{1,0:T(8,128)(2,1)S(1)} %collective-permute-done.3.refs_2_, ...), custom_call_target="tpu_custom_call" | custom-call | flops 2000000000 | bytes 2000000 | tf_op jit(solution)/shard_map/mix_add/pallas_call | solution.py:379
  66.0 2.8 %collective-permute-done.8.refs_1_ = bf16[128,512]{1,0:T(8,128)(2,1)S(1)} collective-permute-done((bf16[128,512]{1,0:T(8,128)(2,1)S(1)}, bf16[128,512]{1,0:T(8,128)(2,1)S(1)}, u32[]{:S(2)}, u32[]{:S(2)}) %collective-permute-start.8) | collective-permute-done | bytes 131104 | tf_op jit(solution)/shard_map/ppermute | solution.py:667
  75.2 4.4 %collective-permute-done.11.refs_0_ = bf16[256,768]{1,0:T(8,128)(2,1)S(1)} collective-permute-done((bf16[256,768]{1,0:T(8,128)(2,1)}, bf16[256,768]{1,0:T(8,128)(2,1)S(1)}, u32[]{:S(2)}, u32[]{:S(2)}) %collective-permute-start.11) | collective-permute-done | bytes 393248 | tf_op jit(solution)/shard_map/ppermute | solution.py:667
  79.5 2.0 %collective-permute-start.12 = (bf16[128,768]{1,0:T(8,128)(2,1)S(1)}, bf16[128,768]{1,0:T(8,128)(2,1)S(1)}, u32[]{:S(2)}, u32[]{:S(2)}) collective-permute-start(bf16[128,768]{1,0:T(8,128)(2,1)S(1)} %slice.26), channel_id=1, source_target_pairs={{0,1},{1,2},{2,3},{3,0},{4,5},{5,6},{6,7},{7,4},{8,9},{9,10},{10,1... | collective-permute-start | bytes 589832 | tf_op jit(solution)/shard_map/ppermute | solution.py:667
  81.7 2.6 %project.4 = (f32[3,256,512]{2,1,0:T(8,128)S(1)}, f32[256,1]{1,0:T(8,128)S(1)}) custom-call(bf16[256,768]{1,0:T(8,128)(2,1)S(1)} %collective-permute-done.11.refs_0_, bf16[256,768]{1,0:T(8,128)(2,1)S(1)} %collective-permute-done.13.refs_1_, f32[1,3072]{1,0:T(1,128)S(1)} %bitcast.16, bf16[3,3072,512]{2,1,0:T(8,128)(2,1)S(1)} %bitcast.13, ...), custom_call_target="tpu_custom_call" | custom-call | flops 3000000000 | bytes 8000000 | tf_op jit(solution)/shard_map/project/pallas_call | solution.py:458
  85.3 3.2 %collective-permute-done.14.refs_1_ = bf16[128,768]{1,0:T(8,128)(2,1)S(1)} collective-permute-done((bf16[128,768]{1,0:T(8,128)(2,1)S(1)}, bf16[128,768]{1,0:T(8,128)(2,1)S(1)}, u32[]{:S(2)}, u32[]{:S(2)}) %collective-permute-start.14) | collective-permute-done | bytes 196640 | tf_op jit(solution)/shard_map/ppermute | solution.py:667
  88.5 1.9 %project.5 = (bf16[6,128,128]{2,1,0:T(8,128)(2,1)S(1)}, bf16[6,128,128]{2,1,0:T(8,128)(2,1)S(1)}, bf16[6,128,128]{2,1,0:T(8,128)(2,1)S(1)}, bf16[6,128,128]{2,1,0:T(8,128)(2,1)S(1)}) custom-call(bf16[128,768]{1,0:T(8,128)(2,1)S(1)} %collective-permute-done.12.refs_0_, bf16[128,768]{1,0:T(8,128)(2,1)S(1)} %collective-permute-done.14.refs_1_, ...), custom_call_target="tpu_custom_call" | custom-call | flops 1500000000 | bytes 4000000 | tf_op jit(solution)/shard_map/project/pallas_call | solution.py:458
  91.0 1.9 %collective-permute-start.16 = (bf16[6,128,128]{2,1,0:T(8,128)(2,1)S(1)}, bf16[6,128,128]{2,1,0:T(8,128)(2,1)S(1)}, u32[]{:S(2)}, u32[]{:S(2)}) collective-permute-start(bf16[6,128,128]{2,1,0:T(8,128)(2,1)S(1)} %get-tuple-element.60), channel_id=1, source_target_pairs={{0,64},{4,68},{8,72},{12,76},{16,80},{20,84},{24,88},{28,92},{32,9... | collective-permute-start | bytes 589832 | tf_op jit(solution)/shard_map/ppermute | solution.py:671
  93.8 5.7 %collective-permute-done.15.a1 = bf16[6,128,128]{2,1,0:T(8,128)(2,1)S(1)} collective-permute-done((bf16[6,128,128]{2,1,0:T(8,128)(2,1)S(1)}, bf16[6,128,128]{2,1,0:T(8,128)(2,1)S(1)}, u32[]{:S(2)}, u32[]{:S(2)}) %collective-permute-start.15) | collective-permute-done | bytes 196640 | tf_op jit(solution)/shard_map/ppermute | solution.py:671
  105.9 2.7 %attend_more.2 = (f32[4,1,512]{2,1,0:T(1,128)S(1)}, f32[4,1,512]{2,1,0:T(1,128)S(1)}, f32[4,128,512]{2,1,0:T(8,128)S(1)}) custom-call(bf16[4,128,256]{2,1,0:T(8,128)(2,1)S(1)} %get-tuple-element.67.own, bf16[4,128,256]{2,1,0:T(8,128)(2,1)S(1)} %collective-permute-done.18.other, bf16[2,8,128,128]{3,2,1,0:T(8,128)(2,1)S(1)} %get-tuple-element.63.pair.refs_0_, ...), custom_call_target="tpu_custom_call" | custom-call | flops 1000 | bytes 1000 | tf_op jit(solution)/shard_map/attend_more/pallas_call | solution.py:596
  109.8 2.2 %collective-permute-start.20 = (bf16[8,128,128]{2,1,0:T(8,128)(2,1)S(1)}, bf16[8,128,128]{2,1,0:T(8,128)(2,1)S(1)}, u32[]{:S(2)}, u32[]{:S(2)}) collective-permute-start(bf16[8,128,128]{2,1,0:T(8,128)(2,1)S(1)} %slice_bitcast_fusion.1), channel_id=1, source_target_pairs={{0,8},{4,12},{8,16},{12,20},{16,24},{20,28},{24,0},{28,4},{32,40},... | collective-permute-start | bytes 786440 | tf_op jit(solution)/shard_map/ppermute | solution.py:675
  112.1 6.1 %attend_more.3 = (f32[4,1,512]{2,1,0:T(1,128)S(1)}, f32[4,1,512]{2,1,0:T(1,128)S(1)}, f32[4,128,512]{2,1,0:T(8,128)S(1)}) custom-call(bf16[4,128,256]{2,1,0:T(8,128)(2,1)S(1)} %get-tuple-element.67.own, bf16[4,128,256]{2,1,0:T(8,128)(2,1)S(1)} %collective-permute-done.18.other, bf16[2,8,128,128]{3,2,1,0:T(8,128)(2,1)S(1)} %collective-permute-done.19.refs_0_, ...), custom_call_target="tpu_custom_call" | custom-call | flops 8000000000 | bytes 1000 | tf_op jit(solution)/shard_map/attend_more/pallas_call | solution.py:596
  119.7 3.1 %attend_last.1 = (f32[4,128,256]{2,1,0:T(8,128)S(1)}, f32[4,1,256]{2,1,0:T(1,128)S(1)}, bf16[4,144,256]{2,1,0:T(8,128)(2,1)S(1)}) custom-call(bf16[4,128,256]{2,1,0:T(8,128)(2,1)S(1)} %get-tuple-element.67.own, bf16[4,128,256]{2,1,0:T(8,128)(2,1)S(1)} %collective-permute-done.18.other, bf16[8,128,128]{2,1,0:T(8,128)(2,1)S(1)} %collective-permute-done.20.refs_0_, ...), custom_call_target="tpu_custom_call" | custom-call | flops 4000000000 | bytes 3000000 | tf_op jit(solution)/shard_map/attend_last/pallas_call | solution.py:608
  126.3 2.5 %collective-permute-start.25 = (bf16[256,128]{1,0:T(8,128)(2,1)S(1)}, bf16[256,128]{1,0:T(8,128)(2,1)S(1)}, u32[]{:S(2)}, u32[]{:S(2)}) collective-permute-start(bf16[256,128]{1,0:T(8,128)(2,1)S(1)} %get-tuple-element.82), channel_id=1, source_target_pairs={{0,64},{4,68},{8,72},{12,76},{16,80},{20,84},{24,88},{28,92},{32,9... | collective-permute-start | bytes 196616 | tf_op jit(solution)/shard_map/ppermute | solution.py:671
  130.2 2.2 %collective-permute-done.25.a2 = bf16[256,128]{1,0:T(8,128)(2,1)S(1)} collective-permute-done((bf16[256,128]{1,0:T(8,128)(2,1)S(1)}, bf16[256,128]{1,0:T(8,128)(2,1)S(1)}, u32[]{:S(2)}, u32[]{:S(2)}) %collective-permute-start.25) | collective-permute-done | bytes 65568 | tf_op jit(solution)/shard_map/ppermute | solution.py:671
  (99 shorter events, 44.9 us)
Async XLA Ops:
  6.0 6.2 %collective-permute-start = (bf16[16,3072]{1,0:T(8,128)(2,1)S(1)}, bf16[16,3072]{1,0:T(8,128)(2,1)S(1)}, u32[]{:S(2)}, u32[]{:S(2)}) collective-permute-start(bf16[16,3072]{1,0:T(8,128)(2,1)S(1)} %get-tuple-element.43), channel_id=1, source_target_pairs={{0,4},{4,8},{8,12},{12,16},{16,20},{20,24},{24,28},{28,32},{32,36}... | collective-permute-start | bytes 294920 | tf_op jit(solution)/shard_map/ppermute | solution.py:687
  16.2 17.7 %all-to-all-start = ((bf16[32,32,256]{2,1,0:T(8,128)(2,1)}), bf16[32,32,256]{2,1,0:T(8,128)(2,1)S(1)}, u32[]{:S(2)}, u32[]{:S(2)}) async-start(bf16[32,32,256]{2,1,0:T(8,128)(2,1)} %get-tuple-element.48), calls=%async_computation | async-start | bytes 1048576 | tf_op jit(solution)/shard_map/all_to_all | solution.py:702
  24.6 20.1 %collective-permute-start.3 = (bf16[256,768]{1,0:T(8,128)(2,1)}, bf16[256,768]{1,0:T(8,128)(2,1)S(1)}, u32[]{:S(2)}, u32[]{:S(2)}) collective-permute-start(bf16[256,768]{1,0:T(8,128)(2,1)} %get-tuple-element.51), channel_id=1, source_target_pairs={{0,1},{1,2},{2,3},{3,0},{4,5},{5,6},{6,7},{7,4},{8,9},{9,10},{10,1... | collective-permute-start | bytes 1179656 | tf_op jit(solution)/shard_map/ppermute | solution.py:667
  25.1 20.7 %collective-permute-start.4 = (bf16[256,768]{1,0:T(8,128)(2,1)}, bf16[256,768]{1,0:T(8,128)(2,1)S(1)}, u32[]{:S(2)}, u32[]{:S(2)}) collective-permute-start(bf16[256,768]{1,0:T(8,128)(2,1)} %get-tuple-element.52), channel_id=1, source_target_pairs={{0,3},{1,0},{2,1},{3,2},{4,7},{5,4},{6,5},{7,6},{8,11},{9,8},{10,9... | collective-permute-start | bytes 1179656 | tf_op jit(solution)/shard_map/ppermute | solution.py:667
  26.7 27.3 %collective-permute-start.9 = (bf16[256,768]{1,0:T(8,128)(2,1)S(1)}, bf16[256,768]{1,0:T(8,128)(2,1)S(1)}, u32[]{:S(2)}, u32[]{:S(2)}) collective-permute-start(bf16[256,768]{1,0:T(8,128)(2,1)S(1)} %get-tuple-element.53), channel_id=1, source_target_pairs={{0,2},{1,3},{2,0},{3,1},{4,6},{5,7},{6,4},{7,5},{8,10},{9,11},{10,... | collective-permute-start | bytes 1179656 | tf_op jit(solution)/shard_map/ppermute | solution.py:667
  38.3 13.4 %all-to-all-start.1 = ((bf16[32,16,256]{2,1,0:T(8,128)(2,1)}), bf16[32,16,256]{2,1,0:T(8,128)(2,1)S(1)}, u32[]{:S(2)}, u32[]{:S(2)}) async-start(bf16[32,16,256]{2,1,0:T(8,128)(2,1)} %convolve.1), calls=%async_computation.1 | async-start | bytes 524288 | tf_op jit(solution)/shard_map/all_to_all | solution.py:703
  44.7 18.3 %collective-permute-start.5 = (bf16[256,768]{1,0:T(8,128)(2,1)S(1)}, bf16[256,768]{1,0:T(8,128)(2,1)}, u32[]{:S(2)}, u32[]{:S(2)}) collective-permute-start(bf16[256,768]{1,0:T(8,128)(2,1)S(1)} %collective-permute-done.3.refs_2_), channel_id=1, source_target_pairs={{0,4},{4,0},{8,12},{12,8},{16,20},{20,16},{24,28},{28,24},{32,36},... | collective-permute-start | bytes 1179656 | tf_op jit(solution)/shard_map/ppermute | solution.py:679
  45.8 17.1 %collective-permute-start.6 = (bf16[256,768]{1,0:T(8,128)(2,1)S(1)}, bf16[256,768]{1,0:T(8,128)(2,1)}, u32[]{:S(2)}, u32[]{:S(2)}) collective-permute-start(bf16[256,768]{1,0:T(8,128)(2,1)S(1)} %collective-permute-done.4.refs_3_), channel_id=1, source_target_pairs={{0,4},{4,0},{8,12},{12,8},{16,20},{20,16},{24,28},{28,24},{32,36},... | collective-permute-start | bytes 1179656 | tf_op jit(solution)/shard_map/ppermute | solution.py:679
  51.9 8.9 %collective-permute-start.1 = (bf16[256,512]{1,0:T(8,128)(2,1)S(1)}, bf16[256,512]{1,0:T(8,128)(2,1)S(1)}, u32[]{:S(2)}, u32[]{:S(2)}) collective-permute-start(bf16[256,512]{1,0:T(8,128)(2,1)S(1)} %gate.1.gated), channel_id=1, source_target_pairs={{0,1},{1,2},{2,3},{3,0},{4,5},{5,6},{6,7},{7,4},{8,9},{9,10},{10,1... | collective-permute-start | bytes 786440 | tf_op jit(solution)/shard_map/ppermute | solution.py:667
  52.4 10.1 %collective-permute-start.2 = (bf16[256,512]{1,0:T(8,128)(2,1)S(1)}, bf16[256,512]{1,0:T(8,128)(2,1)S(1)}, u32[]{:S(2)}, u32[]{:S(2)}) collective-permute-start(bf16[256,512]{1,0:T(8,128)(2,1)S(1)} %gate.1.gated), channel_id=1, source_target_pairs={{0,3},{1,0},{2,1},{3,2},{4,7},{5,4},{6,5},{7,6},{8,11},{9,8},{10,9... | collective-permute-start | bytes 786440 | tf_op jit(solution)/shard_map/ppermute | solution.py:667
  54.0 10.9 %collective-permute-start.10 = (bf16[256,768]{1,0:T(8,128)(2,1)S(1)}, bf16[256,768]{1,0:T(8,128)(2,1)S(1)}, u32[]{:S(2)}, u32[]{:S(2)}) collective-permute-start(bf16[256,768]{1,0:T(8,128)(2,1)S(1)} %collective-permute-done.9.refs_2_), channel_id=1, source_target_pairs={{0,4},{4,0},{8,12},{12,8},{16,20},{20,16},{24,28},{28,24},{32,36},... | collective-permute-start | bytes 1179656 | tf_op jit(solution)/shard_map/ppermute | solution.py:679
  62.5 6.2 %collective-permute-start.8 = (bf16[128,512]{1,0:T(8,128)(2,1)S(1)}, bf16[128,512]{1,0:T(8,128)(2,1)S(1)}, u32[]{:S(2)}, u32[]{:S(2)}) collective-permute-start(bf16[128,512]{1,0:T(8,128)(2,1)S(1)} %slice.25), channel_id=1, source_target_pairs={{0,3},{1,0},{2,1},{3,2},{4,7},{5,4},{6,5},{7,6},{8,11},{9,8},{10,9... | collective-permute-start | bytes 393224 | tf_op jit(solution)/shard_map/ppermute | solution.py:667
  69.9 9.6 %collective-permute-start.11 = (bf16[256,768]{1,0:T(8,128)(2,1)}, bf16[256,768]{1,0:T(8,128)(2,1)S(1)}, u32[]{:S(2)}, u32[]{:S(2)}) collective-permute-start(bf16[256,768]{1,0:T(8,128)(2,1)} %mix_add.3.refs_0_), channel_id=1, source_target_pairs={{0,1},{1,2},{2,3},{3,0},{4,5},{5,6},{6,7},{7,4},{8,9},{9,10},{10,1... | collective-permute-start | bytes 1179656 | tf_op jit(solution)/shard_map/ppermute | solution.py:667
  70.1 11.5 %collective-permute-start.13 = (bf16[256,768]{1,0:T(8,128)(2,1)}, bf16[256,768]{1,0:T(8,128)(2,1)S(1)}, u32[]{:S(2)}, u32[]{:S(2)}) collective-permute-start(bf16[256,768]{1,0:T(8,128)(2,1)} %mix_add.3.refs_0_), channel_id=1, source_target_pairs={{0,3},{1,0},{2,1},{3,2},{4,7},{5,4},{6,5},{7,6},{8,11},{9,8},{10,9... | collective-permute-start | bytes 1179656 | tf_op jit(solution)/shard_map/ppermute | solution.py:667
  79.5 5.7 %collective-permute-start.12 = (bf16[128,768]{1,0:T(8,128)(2,1)S(1)}, bf16[128,768]{1,0:T(8,128)(2,1)S(1)}, u32[]{:S(2)}, u32[]{:S(2)}) collective-permute-start(bf16[128,768]{1,0:T(8,128)(2,1)S(1)} %slice.26), channel_id=1, source_target_pairs={{0,1},{1,2},{2,3},{3,0},{4,5},{5,6},{6,7},{7,4},{8,9},{9,10},{10,1... | collective-permute-start | bytes 589832 | tf_op jit(solution)/shard_map/ppermute | solution.py:667
  81.5 6.9 %collective-permute-start.14 = (bf16[128,768]{1,0:T(8,128)(2,1)S(1)}, bf16[128,768]{1,0:T(8,128)(2,1)S(1)}, u32[]{:S(2)}, u32[]{:S(2)}) collective-permute-start(bf16[128,768]{1,0:T(8,128)(2,1)S(1)} %slice.27), channel_id=1, source_target_pairs={{0,3},{1,0},{2,1},{3,2},{4,7},{5,4},{6,5},{7,6},{8,11},{9,8},{10,9... | collective-permute-start | bytes 589832 | tf_op jit(solution)/shard_map/ppermute | solution.py:667
  90.4 9.1 %collective-permute-start.15 = (bf16[6,128,128]{2,1,0:T(8,128)(2,1)S(1)}, bf16[6,128,128]{2,1,0:T(8,128)(2,1)S(1)}, u32[]{:S(2)}, u32[]{:S(2)}) collective-permute-start(bf16[6,128,128]{2,1,0:T(8,128)(2,1)S(1)} %get-tuple-element.59), channel_id=1, source_target_pairs={{0,32},{4,36},{8,40},{12,44},{16,48},{20,52},{24,56},{28,60},{32,6... | collective-permute-start | bytes 589832 | tf_op jit(solution)/shard_map/ppermute | solution.py:671
  91.0 8.5 %collective-permute-start.16 = (bf16[6,128,128]{2,1,0:T(8,128)(2,1)S(1)}, bf16[6,128,128]{2,1,0:T(8,128)(2,1)S(1)}, u32[]{:S(2)}, u32[]{:S(2)}) collective-permute-start(bf16[6,128,128]{2,1,0:T(8,128)(2,1)S(1)} %get-tuple-element.60), channel_id=1, source_target_pairs={{0,64},{4,68},{8,72},{12,76},{16,80},{20,84},{24,88},{28,92},{32,9... | collective-permute-start | bytes 589832 | tf_op jit(solution)/shard_map/ppermute | solution.py:671
  93.0 7.4 %collective-permute-start.17 = (bf16[6,128,128]{2,1,0:T(8,128)(2,1)S(1)}, bf16[6,128,128]{2,1,0:T(8,128)(2,1)S(1)}, u32[]{:S(2)}, u32[]{:S(2)}) collective-permute-start(bf16[6,128,128]{2,1,0:T(8,128)(2,1)S(1)} %get-tuple-element.61), channel_id=1, source_target_pairs={{0,96},{4,100},{8,104},{12,108},{16,112},{20,116},{24,120},{28,124... | collective-permute-start | bytes 589832 | tf_op jit(solution)/shard_map/ppermute | solution.py:671
  100.5 9.3 %collective-permute-start.19 = (bf16[2,8,128,128]{3,2,1,0:T(8,128)(2,1)S(1)}, bf16[2,8,128,128]{3,2,1,0:T(8,128)(2,1)S(1)}, u32[]{:S(2)}, u32[]{:S(2)}) collective-permute-start(bf16[2,8,128,128]{3,2,1,0:T(8,128)(2,1)S(1)} %get-tuple-element.63.pair.refs_0_), channel_id=1, source_target_pairs={{0,8},{4,12},{8,16},{12,20},{16,24},{20,28},{24,0},{28,4},{32,40},... | collective-permute-start | bytes 1572872 | tf_op jit(solution)/shard_map/ppermute | solution.py:675
  101.5 10.5 %collective-permute-start.21 = (bf16[2,8,128,128]{3,2,1,0:T(8,128)(2,1)S(1)}, bf16[2,8,128,128]{3,2,1,0:T(8,128)(2,1)S(1)}, u32[]{:S(2)}, u32[]{:S(2)}) collective-permute-start(bf16[2,8,128,128]{3,2,1,0:T(8,128)(2,1)S(1)} %get-tuple-element.63.pair.refs_0_), channel_id=1, source_target_pairs={{0,24},{4,28},{8,0},{12,4},{16,8},{20,12},{24,16},{28,20},{32,56},... | collective-permute-start | bytes 1572872 | tf_op jit(solution)/shard_map/ppermute | solution.py:675
  109.8 8.4 %collective-permute-start.20 = (bf16[8,128,128]{2,1,0:T(8,128)(2,1)S(1)}, bf16[8,128,128]{2,1,0:T(8,128)(2,1)S(1)}, u32[]{:S(2)}, u32[]{:S(2)}) collective-permute-start(bf16[8,128,128]{2,1,0:T(8,128)(2,1)S(1)} %slice_bitcast_fusion.1), channel_id=1, source_target_pairs={{0,8},{4,12},{8,16},{12,20},{16,24},{20,28},{24,0},{28,4},{32,40},... | collective-permute-start | bytes 786440 | tf_op jit(solution)/shard_map/ppermute | solution.py:675
  112.0 7.7 %collective-permute-start.22 = (bf16[8,128,128]{2,1,0:T(8,128)(2,1)S(1)}, bf16[8,128,128]{2,1,0:T(8,128)(2,1)S(1)}, u32[]{:S(2)}, u32[]{:S(2)}) collective-permute-start(bf16[8,128,128]{2,1,0:T(8,128)(2,1)S(1)} %slice_bitcast_fusion), channel_id=1, source_target_pairs={{0,24},{4,28},{8,0},{12,4},{16,8},{20,12},{24,16},{28,20},{32,56},... | collective-permute-start | bytes 786440 | tf_op jit(solution)/shard_map/ppermute | solution.py:675
  126.3 6.1 %collective-permute-start.25 = (bf16[256,128]{1,0:T(8,128)(2,1)S(1)}, bf16[256,128]{1,0:T(8,128)(2,1)S(1)}, u32[]{:S(2)}, u32[]{:S(2)}) collective-permute-start(bf16[256,128]{1,0:T(8,128)(2,1)S(1)} %get-tuple-element.82), channel_id=1, source_target_pairs={{0,64},{4,68},{8,72},{12,76},{16,80},{20,84},{24,88},{28,92},{32,9... | collective-permute-start | bytes 196616 | tf_op jit(solution)/shard_map/ppermute | solution.py:671
  (23 other events, 158.5 us)
